TPU v7x, 128 devices: a whole 4x4x4 slice. The times are simulated.
128 devices in a mesh: shard: 4 (over x), context: 8 (over z, y_lo), tensor: 4 (over y_hi, core).
Axes of the slice: x: 4, y: 4 (y_hi: 2, y_lo: 2; y = y_hi * 2 + y_lo), z: 4, core: 2. Of those that a mesh axis runs over, the one named last changes fastest.
Arguments:
- tokens: bfloat16 [8, 1024, 2048], P('shard', 'context'), may hold values from -6 to 6
- lengths: int32 [8], P('shard'), may hold values from 256 to 1024, as said below
- routes: int32 [8, 1024, 8], P('shard', 'context'), may hold values from 0 to 9, all different within a row
- attn_gain: bfloat16 [2048], P(('shard', 'context')), may hold values from 0.099609375 to 1.8984375
- q_gain: bfloat16 [16, 128], P('tensor', ('shard', 'context')), may hold values from 0.099609375 to 1.8984375
- k_gain: bfloat16 [16, 128], P('tensor', ('shard', 'context')), may hold values from 0.099609375 to 1.8984375
- w_query: bfloat16 [2048, 2048], P(('shard', 'context'), 'tensor'), may hold values from -0.125 to 0.125
- w_key: bfloat16 [2048, 2048], P(('shard', 'context'), 'tensor'), may hold values from -0.125 to 0.125
- w_value: bfloat16 [2048, 2048], P(('shard', 'context'), 'tensor'), may hold values from -0.125 to 0.125
- w_out: bfloat16 [2048, 2048], P('tensor', ('shard', 'context')), may hold values from -1 to 1
- mlp_gain: bfloat16 [2048], P(('shard', 'context')), may hold values from 0.099609375 to 1.8984375
- router: bfloat16 [2048, 10], P(('shard', 'context')), may hold values from -0.0625 to 0.0625
- w_gate: bfloat16 [10, 2048, 1024], P(None, ('shard', 'context'), 'tensor'), may hold values from -0.125 to 0.125
- w_up: bfloat16 [10, 2048, 1024], P(None, ('shard', 'context'), 'tensor'), may hold values from -0.125 to 0.125
- w_down: bfloat16 [10, 1024, 2048], P(None, 'tensor', ('shard', 'context')), may hold values from -0.75 to 0.75
- cotangent: bfloat16 [8, 1024, 2048], P('shard', 'context'), may hold values from -6 to 6
Outputs:
- output: bfloat16 [8, 1024, 2048], P('shard', 'context')
- grad_input: float32 [8, 1024, 2048], P('shard', 'context')
- attn_gain_grad: float32 [2048], P(('shard', 'context'))
- q_gain_grad: float32 [16, 128], P('tensor', ('shard', 'context'))
- k_gain_grad: float32 [16, 128], P('tensor', ('shard', 'context'))
- w_query_grad: float32 [2048, 2048], P(('shard', 'context'), 'tensor')
- w_key_grad: float32 [2048, 2048], P(('shard', 'context'), 'tensor')
- w_value_grad: float32 [2048, 2048], P(('shard', 'context'), 'tensor')
- w_out_grad: float32 [2048, 2048], P('tensor', ('shard', 'context'))
- mlp_gain_grad: float32 [2048], P(('shard', 'context'))
- router_grad: float32 [2048, 10], P(('shard', 'context'))
- w_gate_grad: float32 [10, 2048, 1024], P(None, ('shard', 'context'), 'tensor')
- w_up_grad: float32 [10, 2048, 1024], P(None, ('shard', 'context'), 'tensor')
- w_down_grad: float32 [10, 1024, 2048], P(None, 'tensor', ('shard', 'context'))
Inputs may be any that keep to these rules, and one draw needn't show every extreme that they name: `lengths`: among the slots held by each index of shard, one, drawn from the seed, has length 1024. `routes`: each token names 8 different experts.
All inputs are finite; a program needn't handle non-finite values.
Results may differ from a plain program's by a relative error of at most 0.035.
Values may be sent and summed in bfloat16 or wider, within the bound.
No kernel may reach another device: no remote copies, remote signals or barrier semaphores. Data moves between devices by JAX's collectives and lax.ppermute only.
A program may use at most 256 MiB of HBM per device.

v0:
```python
import math

import jax
import jax.numpy as jnp
from jax import lax
from jax.sharding import Mesh
from jax.sharding import PartitionSpec as P

EPSILON = 1e-05
ROPE_BASE = 10000.0
BF = jnp.bfloat16
F32 = jnp.float32

AXES = ("x", "z", "yl", "yh", "c")
SIZES = (4, 4, 2, 2, 2)
CONTEXT = ("z", "yl")
TENSOR = ("yh", "c")
WEIGHT = ("x", "z", "yl")
Y = ("yl", "yh")
SWAP = ("yl", "c")


def exchange(axes, size, mask):
    pairs = [(at, at ^ mask) for at in range(size)]
    return lambda v: lax.ppermute(v, axes, pairs)


CUBE = (exchange("z", 4, 1), exchange(Y, 4, 2), exchange("z", 4, 3), exchange(Y, 4, 3))
swap_cores = lambda v: lax.ppermute(v, SWAP, [(0, 0), (1, 2), (2, 1), (3, 3)])


def dot(a, b, left=1, right=0):
    return lax.dot_general(a, b, (((left,), (right,)), ((), ())), preferred_element_type=F32)


def cube_gather(own):
    rows = own.shape[0] // 4
    parts = [own[i * rows : (i + 1) * rows] for i in range(4)]
    for step in range(4):
        arrived = lax.optimization_barrier(
            tuple(CUBE[(i + step) % 4](parts[i]) for i in range(4))
        )
        parts = [jnp.concatenate([a, b], axis=0) for a, b in zip(parts, arrived)]
    return jnp.concatenate(parts, axis=0)


def cube_scatter(total):
    rows = total.shape[0] // 4
    parts = [total[i * rows : (i + 1) * rows] for i in range(4)]
    for step in (3, 2, 1, 0):
        half = parts[0].shape[0] // 2
        arrived = lax.optimization_barrier(
            tuple(CUBE[(i + step) % 4](parts[i][half:].astype(BF)) for i in range(4))
        )
        parts = [a[:half].astype(F32) + b.astype(F32) for a, b in zip(parts, arrived)]
    return jnp.concatenate(parts, axis=0)


def cube_sum(rows_of):
    count = rows_of.shape[1]
    held = rows_of.reshape(4, 2, 2, 2, 2, 16, count)
    for dim in range(4):
        arrived = CUBE[dim](held)
        turned = jnp.stack(
            [jnp.flip(arrived[i], axis=3 - (dim - i) % 4) for i in range(4)], axis=0
        )
        held = held + turned
    return held.reshape(rows_of.shape)


def row_positions():
    at = jnp.arange(1024, dtype=jnp.int32)
    part, block, row = at >> 8, (at >> 4) & 15, at & 15
    turned = [(block >> ((dim - part) & 3)) & 1 for dim in range(4)]
    z = lax.axis_index("z") ^ (turned[0] ^ (3 * turned[2]))
    y = (2 * lax.axis_index("yh") + lax.axis_index("yl")) ^ (turned[1] ^ (3 * turned[3]))
    return (2 * z + (y & 1)) * 128 + (y >> 1) * 64 + 16 * part + row


def angles(positions, head_size):
    steps_half = jnp.arange(head_size // 2).astype(F32)
    frequency = jnp.exp(steps_half * (-2.0 * math.log(ROPE_BASE) / head_size))
    turned = positions.astype(F32)[:, None] * frequency[None, :]
    return (jnp.cos(turned), jnp.sin(turned))


def rotate(values, cosine, sine_table):
    half_width = values.shape[-1] // 2
    first_half = values[..., :half_width]
    second_half = values[..., half_width:]
    return jnp.concatenate(
        [
            first_half * cosine - second_half * sine_table,
            second_half * cosine + first_half * sine_table,
        ],
        axis=-1,
    )


def spread(packed):
    held = lax.all_to_all(packed, "z", split_axis=0, concat_axis=0, tiled=True)
    held = swap_cores(held)
    held = lax.all_gather(held, "x", axis=0, tiled=False)
    held = lax.all_gather(held, "c", axis=2, tiled=False)
    return held.reshape(2048, packed.shape[-1])


def collect(grads):
    width = grads.shape[-1]
    held = grads.astype(BF).reshape(4, 4, 2, 64, width)
    held = lax.psum_scatter(held, "c", scatter_dimension=2, tiled=False)
    held = lax.psum_scatter(held, "x", scatter_dimension=0, tiled=False)
    held = swap_cores(held)
    return lax.all_to_all(held, "z", split_axis=0, concat_axis=0, tiled=True)


def per_device(
    tokens,
    lengths,
    routes,
    attn_gain,
    q_gain,
    k_gain,
    w_query,
    w_key,
    w_value,
    w_out,
    mlp_gain,
    router,
    w_gate,
    w_up,
    w_down,
    cotangent,
):
    z = lax.axis_index("z")
    yh = lax.axis_index("yh")
    core = lax.axis_index("c")

    def four(w):
        return w.reshape(64, 4, -1).transpose(1, 0, 2)

    def pack_experts(w):
        return four(w.transpose(1, 0, 2).reshape(64, 2560))

    def per_row(v):
        return jnp.broadcast_to(v[None], (4,) + v.shape)

    gains = jnp.stack([q_gain, k_gain], axis=-1)
    extra = jnp.concatenate(
        [
            per_row(attn_gain[:, None]),
            per_row(mlp_gain[:, None]),
            per_row(router),
            jnp.pad(gains, ((0, 0), (0, 60), (0, 0))),
            jnp.zeros((4, 64, 114), BF),
        ],
        axis=-1,
    )
    first_pack = jnp.concatenate(
        [four(w_query), four(w_key), four(w_value), extra, four(w_out.T)], axis=-1
    )
    second_pack = jnp.concatenate(
        [pack_experts(w_gate), pack_experts(w_up), four(w_down.reshape(2560, 64).T)], axis=-1
    )
    first_all = spread(first_pack)
    second_all = spread(second_pack)
    w_qkv = first_all[:, :384]
    extra_all = first_all[:, 384:512]
    out_t = first_all[:, 512:]
    w_in = second_all[:, :1280]
    down_t = second_all[:, 1280:]
    attn_row = extra_all[:, 0].astype(F32)[None]
    mlp_row = extra_all[:, 1].astype(F32)[None]
    router_all = jnp.pad(extra_all[:, 2:12], ((0, 0), (0, 118)))
    gain_rows = extra_all[:, 12:14].reshape(32, 64, 2)[:, :4].reshape(128, 2).T.astype(F32)
    q_row, k_row = gain_rows[:1], gain_rows[1:]

    own_start = (core, yh * 64, 0)
    own_tokens = lax.dynamic_slice(tokens, own_start, (1, 64, 2048))[0]
    own_cot = lax.dynamic_slice(cotangent, own_start, (1, 64, 2048))[0]
    own_routes = lax.dynamic_slice(routes, own_start, (1, 64, 8))[0]
    slot_length = lax.dynamic_index_in_dim(lengths, core, keepdims=False)
    expert_ids = jnp.arange(10, dtype=jnp.int32)
    own_chosen = jnp.sum((own_routes[:, :, None] == expert_ids).astype(BF), axis=1)
    all_tokens = cube_gather(own_tokens)
    with_routes = cube_gather(
        jnp.concatenate([own_cot, jnp.pad(own_chosen, ((0, 0), (0, 118)))], axis=1)
    )
    positions = row_positions()
    valid = positions < slot_length
    grad_out = jnp.where(valid[:, None], with_routes[:, :2048], jnp.zeros((), BF))
    chosen = with_routes[:, 2048:2058].astype(F32)
    own_valid = (
        (2 * z + lax.axis_index("yl")) * 128 + yh * 64 + jnp.arange(64, dtype=jnp.int32)
    ) < slot_length
    own_grad_out = jnp.where(own_valid[:, None], own_cot.astype(F32), 0.0)

    all_rows = all_tokens.astype(F32)
    all_rate = lax.rsqrt(jnp.mean(all_rows * all_rows, axis=-1, keepdims=True) + EPSILON)
    normed = (all_rows * all_rate * attn_row).astype(BF)
    qkv = dot(normed, w_qkv)
    q_proj, k_proj = qkv[:, :128], qkv[:, 128:256]
    values = qkv[:, 256:].astype(BF)
    squares = cube_sum(
        jnp.stack([jnp.sum(q_proj * q_proj, axis=1), jnp.sum(k_proj * k_proj, axis=1)], axis=1)
    )
    rates = lax.rsqrt(squares / 2048 + EPSILON)
    q_rate, k_rate = rates[:, :1], rates[:, 1:]
    cosine, sine_table = angles(positions, 128)
    queries = rotate(q_proj * q_rate * q_row, cosine, sine_table).astype(BF)
    keys = rotate(k_proj * k_rate * k_row, cosine, sine_table).astype(BF)
    allowed = (positions[None, :] <= positions[:, None]) & valid[None, :]
    scale = 128 ** (-0.5)
    scores = jnp.where(allowed, dot(queries, keys, 1, 1) * scale, -1e30)
    peak = jnp.max(scores, axis=-1, keepdims=True)
    raised = jnp.where(allowed, jnp.exp(scores - peak), 0.0)
    row_total = jnp.sum(raised, axis=-1, keepdims=True)
    probs = raised / row_total
    low_probs = probs.astype(BF)
    attended = dot(low_probs, values).astype(BF)
    own_rows = own_tokens.astype(F32)
    middle = own_rows + cube_scatter(dot(attended, out_t, 1, 1))

    second_rate = lax.rsqrt(jnp.mean(middle * middle, axis=-1, keepdims=True) + EPSILON)
    mixed_in = cube_gather((middle * second_rate * mlp_row).astype(BF))
    logits = dot(mixed_in, router_all)[:, :10]
    route_probs = jax.nn.softmax(logits, axis=-1)
    gate_values = route_probs * chosen
    tile_expert = (5 * z + jnp.arange(5, dtype=jnp.int32)) // 2
    tile_of = (tile_expert[None, :] == expert_ids[:, None]).astype(F32)
    tile_gates = jnp.sum(gate_values[:, :, None] * tile_of[None], axis=1)
    wide_gates = jnp.repeat(tile_gates, 128, axis=1)
    hidden = dot(mixed_in, w_in)
    gate_h, up_h = hidden[:, :640], hidden[:, 640:]
    sig = jax.nn.sigmoid(gate_h)
    silu = gate_h * sig
    activated = (silu * up_h).astype(BF).astype(F32)
    gated = (activated * wide_gates).astype(BF)
    mixture = cube_scatter(dot(gated, down_t, 1, 1))
    own_output = (middle + mixture).astype(BF)
    out_grad = dot(grad_out, down_t)
    tile_parts = jnp.sum((activated * out_grad).reshape(1024, 5, 128), axis=-1)
    gate_part = jnp.sum(tile_parts[:, None, :] * tile_of[None], axis=-1)
    act_grad = out_grad * wide_gates
    gate_h_grad = (act_grad * up_h * sig * (1.0 + gate_h * (1.0 - sig))).astype(BF)
    up_h_grad = (act_grad * silu).astype(BF)
    chosen_grad = gate_part * chosen
    logit_grad = (
        route_probs * (chosen_grad - jnp.sum(chosen_grad * route_probs, axis=-1, keepdims=True))
    ).astype(BF)
    hidden_grad = jnp.concatenate(
        [gate_h_grad, up_h_grad, jnp.pad(logit_grad, ((0, 0), (0, 118)))], axis=1
    )
    in_grads = dot(mixed_in, hidden_grad, 0, 0)
    down_grads = dot(grad_out, gated, 0, 0)
    mixed_grad = cube_scatter(
        dot(hidden_grad, jnp.concatenate([w_in, router_all], axis=1), 1, 1)
    )
    expert_grads = collect(jnp.concatenate([in_grads, down_grads], axis=1))
    scaled = mixed_grad * mlp_row
    middle_grad = (
        own_grad_out
        + second_rate * scaled
        - middle * second_rate**3 * jnp.mean(scaled * middle, axis=-1, keepdims=True)
    )

    branch_grad = cube_gather(middle_grad.astype(BF))
    out_grads = dot(branch_grad, attended, 0, 0)
    attended_grad = dot(branch_grad, out_t).astype(BF)
    prob_grad = dot(attended_grad, values, 1, 1)
    delta = jnp.sum(probs * prob_grad, axis=-1, keepdims=True)
    score_grad = (probs * (prob_grad - delta)).astype(BF)
    query_grad = dot(score_grad, keys) * scale
    key_grad = dot(score_grad, queries, 0, 0) * scale
    v_proj_grad = dot(low_probs, attended_grad, 0, 0).astype(BF)
    q_norm_grad = rotate(query_grad, cosine, -sine_table)
    k_norm_grad = rotate(key_grad, cosine, -sine_table)
    q_scaled = q_norm_grad * q_row
    k_scaled = k_norm_grad * k_row
    inner = cube_sum(
        jnp.stack([jnp.sum(q_scaled * q_proj, axis=1), jnp.sum(k_scaled * k_proj, axis=1)], axis=1)
    )
    q_proj_grad = (q_rate * q_scaled - q_proj * q_rate**3 * inner[:, :1] / 2048).astype(BF)
    k_proj_grad = (k_rate * k_scaled - k_proj * k_rate**3 * inner[:, 1:] / 2048).astype(BF)
    qkv_grad = jnp.concatenate([q_proj_grad, k_proj_grad, v_proj_grad], axis=1)
    qkv_grads = dot(normed, qkv_grad, 0, 0)
    normed_grad = cube_scatter(dot(qkv_grad, w_qkv, 1, 1))
    gain_grads = jnp.stack(
        [
            jnp.sum(q_norm_grad * q_proj * q_rate, axis=0),
            jnp.sum(k_norm_grad * k_proj * k_rate, axis=0),
        ],
        axis=1,
    )
    gain_block = jnp.pad(gain_grads.reshape(32, 4, 2), ((0, 0), (0, 60), (0, 126)))
    attn_grads = collect(
        jnp.concatenate([qkv_grads, out_grads, gain_block.reshape(2048, 128)], axis=1)
    )
    scaled = normed_grad * attn_row
    own_rate = lax.rsqrt(jnp.mean(own_rows * own_rows, axis=-1, keepdims=True) + EPSILON)
    own_input_grad = (
        middle_grad
        + own_rate * scaled
        - own_rows * own_rate**3 * jnp.mean(scaled * own_rows, axis=-1, keepdims=True)
    )

    def whole(own):
        held = lax.all_gather(own, "yh", axis=0, tiled=True)
        return lax.all_gather(held, "c", axis=0, tiled=False)

    def wide(grads):
        return grads.transpose(1, 0, 2).reshape(64, -1).astype(F32)

    def experts(grads):
        return wide(grads).reshape(64, 10, 256).transpose(1, 0, 2)

    q_grads = wide(attn_grads[:, :, :128])
    k_grads = wide(attn_grads[:, :, 128:256])
    v_grads = wide(attn_grads[:, :, 256:384])
    o_grads = wide(attn_grads[:, :, 384:512]).T
    q_gain_grad = attn_grads[:, :4, 512].astype(F32)
    k_gain_grad = attn_grads[:, :4, 513].astype(F32)
    gate_grads = experts(expert_grads[:, :, :640])
    up_grads = experts(expert_grads[:, :, 640:1280])
    router_part = jnp.sum(expert_grads[:, :, 1280:1290].astype(F32), axis=0)
    down_out = wide(expert_grads[:, :, 1408:]).T.reshape(10, 256, 64)

    def row_sums(*pairs):
        return sum(jnp.sum(w.astype(F32) * g, axis=tuple(range(2, w.ndim)) or None) for w, g in pairs)

    attn_part = sum(
        jnp.sum(w.astype(F32) * g, axis=1)
        for w, g in ((w_query, q_grads), (w_key, k_grads), (w_value, v_grads))
    )
    mlp_part = sum(
        jnp.sum(w.astype(F32) * g, axis=(0, 2)) for w, g in ((w_gate, gate_grads), (w_up, up_grads))
    ) + jnp.sum(router.astype(F32) * router_part, axis=1)
    summed = lax.psum(
        jnp.concatenate([router_part, attn_part[:, None], mlp_part[:, None]], axis=1), TENSOR
    )
    return (
        whole(own_output),
        whole(own_input_grad.astype(BF)).astype(F32),
        summed[:, 10] / attn_gain.astype(F32),
        q_gain_grad,
        k_gain_grad,
        q_grads,
        k_grads,
        v_grads,
        o_grads,
        summed[:, 11] / mlp_gain.astype(F32),
        summed[:, :10],
        gate_grads,
        up_grads,
        down_out,
    )


def solution(mesh):
    fine = Mesh(mesh.devices.reshape(SIZES), AXES)
    rows = P("x", CONTEXT, None)
    vector = P(WEIGHT)
    gains = P(TENSOR, WEIGHT)
    tall = P(WEIGHT, TENSOR)
    routed = P(WEIGHT, None)
    hidden = P(None, WEIGHT, TENSOR)
    back = P(None, TENSOR, WEIGHT)
    weights = (vector, gains, gains, tall, tall, tall, gains, vector, routed, hidden, hidden, back)
    return jax.shard_map(
        per_device,
        mesh=fine,
        in_specs=(rows, P("x"), rows) + weights + (rows,),
        out_specs=(rows, rows) + weights,
        check_vma=False,
    )
```

profile of v0, /device:TPU:0, one launch (start us, length us, event | category | flops | bytes accessed | tf_op | source)
XLA Modules:
  0.0 869.0 jit_solution(9816179446865641674)
XLA Ops:
  16.3 5.4 all-to-all-start
  118.3 5.7 all-gather.13.cloned.1.call-done
  134.5 5.7 all-gather.15.cloned.1.call-done
  142.1 4.6 fusion.31
  188.1 7.4 collective-permute-done.24
  223.8 9.0 %collective-permute-start.53 = (bf16[4,64,1920]{2,1,0:T(8,128)(2,1)}, bf16[4,64,1920]{2,1,0:T(8,128)(2,1)}, u32[]{:S(2)}, u32[]{:S(2)}) collective-permute-start(bf16[4,64,1920]{2,1,0:T(8,128)(2,1)} %all-to-all-done.1), channel_id=1, source_target_pairs={{0,0},{1,4},{4,1},{5,5},{2,2},{3,6},{6,3},{7,7},{8,8},{9,12},{12,9... | collective-permute-start | bytes 2949128 | tf_op jit(solution)/shard_map/ppermute | solution.py:29
  271.1 7.7 collective-permute-done.36
  330.2 12.3 %concatenate.309 = bf16[1024,2176]{0,1:T(8,128)(2,1)} concatenate(bf16[16,2176]{0,1:T(8,128)(2,1)} %get-tuple-element.469, bf16[16,2176]{0,1:T(8,128)(2,1)} %copy.667, bf16[32,2176]{0,1:T(8,128)(2,1)} %copy.668, bf16[64,2176]{0,1:T(8,128)(2,1)} %copy.669, bf16[128,2176]{0,1:T(8,128)(2,1)} %collective-permute-done.66, bf16[16,2176]{0,1:T(8,128)(2,1)S(1)} %copy-done.21, ...), dimensions={0} | concatenate | bytes 8912896 | tf_op jit(solution)/shard_map/concatenate | solution.py:44
  369.1 5.6 slice.1086
  374.7 8.3 fusion.148
  383.0 9.2 %convert_multiply_fusion.2 = (f32[1024,640]{1,0:T(8,128)}, bf16[1024,640]{1,0:T(8,128)(2,1)}, f32[1024,640]{1,0:T(8,128)}) fusion(f32[1024,1280]{1,0:T(8,128)S(1)} %fusion.148, bf16[2048,1920]{1,0:T(8,128)(2,1)} %bitcast.344, bf16[1024,2176]{0,1:T(8,128)(2,1)S(1)} %bitcast.350, pred[1024]{0:T(1024)(128)(4,1)S(1)} %broadcast_compare_fusion), kind=kOutput, calls=%fused_computation.22 | convolution fusion | flops 2691694592 | bytes 18613248 | tf_op jit(solution)/shard_map/dot_general | solution.py:33
  404.6 5.5 multiply_convert_fusion.2
  410.1 6.7 fusion.166
  422.7 5.1 collective-permute-done.89
  441.1 6.3 collective-permute-done.93
  462.2 8.7 %convolution_convert_fusion = bf16[2048,1408]{1,0:T(8,128)(2,1)} fusion(bf16[1024,2048]{1,0:T(8,128)(2,1)S(1)} %copy-done.13, bf16[1024,10]{1,0:T(8,128)(2,1)S(1)} %copy.790, bf16[1024,640]{1,0:T(8,128)(2,1)S(1)} %copy-done.73, bf16[1024,640]{1,0:T(8,128)(2,1)S(1)} %copy-done.71), kind=kOutput, calls=%fused_computation.8 | convolution fusion | flops 5919997952 | bytes 12603392 | tf_op jit(solution)/shard_map/dot_general | solution.py:33
  481.3 4.9 fusion.14
  486.2 6.0 collective-permute-done.101
  501.9 8.1 pad_maximum_fusion
  510.0 8.3 copy.777
  542.5 10.6 %fusion.168 = (bf16[1024,2048]{0,1:T(8,128)(2,1)}, f32[1024,2048]{0,1:T(8,128)}) fusion(bf16[2048,1920]{1,0:T(8,128)(2,1)} %bitcast.345, f32[1024,640]{1,0:T(8,128)} %copy.679, bf16[1024,640]{1,0:T(8,128)(2,1)S(1)} %copy-done.68), kind=kOutput, calls=%fused_computation.577 | convolution fusion | flops 2688417792 | bytes 19136512 | tf_op jit(solution)/shard_map/dot_general | solution.py:33
  557.9 5.7 collective-permute-done.117
  639.7 5.2 convolution_convert_fusion.1
  653.7 10.6 %collective-permute-done.77 = bf16[64,2048]{0,1:T(8,128)(2,1)S(1)} collective-permute-done((bf16[64,2048]{0,1:T(8,128)(2,1)S(1)}, bf16[64,2048]{0,1:T(8,128)(2,1)S(1)}, u32[]{:S(2)}, u32[]{:S(2)}) %collective-permute-start.77) | collective-permute-done | bytes 262176 | tf_op jit(solution)/shard_map/ppermute | solution.py:25
  672.2 8.5 collective-permute-done.81
  699.0 4.6 collective-permute-done.85
  773.9 8.8 %all_gather.50 = bf16[128,2048]{1,0:T(8,128)(2,1)} all-gather(bf16[64,2048]{1,0:T(8,128)(2,1)S(1)} %copy.685), channel_id=1, replica_groups=mesh['x'=4,'z'=4,'yl'=2,'yh'=2,'c'=2] {'yh'}, dimensions={0}, use_global_device_ids=true | all-gather | bytes 786432 | tf_op jit(solution)/shard_map/all_gather | solution.py:308
  784.0 8.8 %all_gather.53 = bf16[128,2048]{1,0:T(8,128)(2,1)} all-gather(bf16[64,2048]{1,0:T(8,128)(2,1)S(1)} %copy.749), channel_id=1, replica_groups=mesh['x'=4,'z'=4,'yl'=2,'yh'=2,'c'=2] {'yh'}, dimensions={0}, use_global_device_ids=true | all-gather | bytes 786432 | tf_op jit(solution)/shard_map/all_gather | solution.py:308
  792.9 9.5 %collective-permute-start.138 = (bf16[4,64,2048]{2,1,0:T(8,128)(2,1)}, bf16[4,64,2048]{2,1,0:T(8,128)(2,1)}, u32[]{:S(2)}, u32[]{:S(2)}) collective-permute-start(bf16[4,64,2048]{2,1,0:T(8,128)(2,1)} %bitcast.405), channel_id=1, source_target_pairs={{0,0},{1,4},{4,1},{5,5},{2,2},{3,6},{6,3},{7,7},{8,8},{9,12},{12,9... | collective-permute-start | bytes 3145736 | tf_op jit(solution)/shard_map/ppermute | solution.py:29
  809.8 6.5 all-gather.23.cloned.1.call-done
  827.4 14.0 %all-to-all-done.2 = bf16[4,64,2048]{2,1,0:T(8,128)(2,1)S(1)} async-done(((bf16[4,64,2048]{2,1,0:T(8,128)(2,1)}), bf16[4,64,2048]{2,1,0:T(8,128)(2,1)S(1)}, u32[]{:S(2)}, u32[]{:S(2)}) %all-to-all-start.2) | async-done | bytes 1048608 | tf_op jit(solution)/shard_map/all_to_all | solution.py:114
  848.9 10.1 %psum.7 = f32[64,12]{0,1:T(8,128)S(1)} all-reduce(f32[64,12]{0,1:T(8,128)S(1)} %pad_maximum_fusion.70), channel_id=1, replica_groups=mesh['x'=4,'z'=4,'yl'=2,'yh'=2,'c'=2] {'yh','c'}, use_global_device_ids=true, to_apply=%region_32.33 | all-reduce | flops 768 | bytes 6144 | tf_op jit(solution)/shard_map/psum | solution.py:338
  (1062 shorter events, 607.6 us)
Async XLA Ops:
  16.3 62.8 %all-to-all-start = ((bf16[4,64,640]{2,1,0:T(8,128)(2,1)}), bf16[4,64,640]{2,1,0:T(8,128)(2,1)}, u32[]{:S(2)}, u32[]{:S(2)}) async-start(bf16[4,64,640]{2,1,0:T(8,128)(2,1)} %copy.583), calls=%async_computation | async-start | bytes 655360 | tf_op jit(solution)/shard_map/all_to_all | solution.py:101
  26.6 35.7 %collective-permute-start.54 = (bf16[16,2176]{1,0:T(8,128)(2,1)}, bf16[16,2176]{1,0:T(8,128)(2,1)S(1)}, u32[]{:S(2)}, u32[]{:S(2)}) collective-permute-start(bf16[16,2176]{1,0:T(8,128)(2,1)} %copy.643), channel_id=1, source_target_pairs={{0,8},{8,0},{16,24},{24,16},{1,9},{9,1},{17,25},{25,17},{2,10},{10... | collective-permute-start | bytes 208904 | tf_op jit(solution)/shard_map/ppermute | solution.py:25
  79.1 144.6 %all-to-all-start.1 = ((bf16[4,64,1920]{2,1,0:T(8,128)(2,1)}), bf16[4,64,1920]{2,1,0:T(8,128)(2,1)}, u32[]{:S(2)}, u32[]{:S(2)}) async-start(bf16[4,64,1920]{2,1,0:T(8,128)(2,1)} %copy.641), calls=%async_computation.1 | async-start | bytes 1966080 | tf_op jit(solution)/shard_map/all_to_all | solution.py:101
  83.4 40.6 %all-gather.13.cloned.1.call-start = ((), (), s32[]{:S(2)}) async-start(), calls=%async_computation.12 | async-start | bytes 1638400 | tf_op jit(solution)/shard_map/all_gather | solution.py:103
  98.3 50.5 %collective-permute-start.61 = (bf16[32,2176]{1,0:T(8,128)(2,1)}, bf16[32,2176]{1,0:T(8,128)(2,1)}, u32[]{:S(2)}, u32[]{:S(2)}) collective-permute-start(bf16[32,2176]{1,0:T(8,128)(2,1)} %pad_maximum_fusion.49), channel_id=1, source_target_pairs={{0,8},{8,0},{16,24},{24,16},{1,9},{9,1},{17,25},{25,17},{2,10},{10... | collective-permute-start | bytes 417800 | tf_op jit(solution)/shard_map/ppermute | solution.py:25
  100.1 40.1 %all-gather.15.cloned.1.call-start = ((), (), s32[]{:S(2)}) async-start(), calls=%async_computation.13 | async-start | bytes 3932160 | tf_op jit(solution)/shard_map/all_gather | solution.py:104
  105.8 43.1 %collective-permute-start.60 = (bf16[32,2176]{1,0:T(8,128)(2,1)}, bf16[32,2176]{1,0:T(8,128)(2,1)S(1)}, u32[]{:S(2)}, u32[]{:S(2)}) collective-permute-start(bf16[32,2176]{1,0:T(8,128)(2,1)} %pad_maximum_fusion.48), channel_id=1, source_target_pairs={{0,6},{2,4},{4,2},{6,0},{1,7},{3,5},{5,3},{7,1},{8,14},{10,12},{12... | collective-permute-start | bytes 417800 | tf_op jit(solution)/shard_map/ppermute | solution.py:25
  108.4 40.5 %collective-permute-start.59 = (bf16[32,2176]{1,0:T(8,128)(2,1)}, bf16[32,2176]{1,0:T(8,128)(2,1)}, u32[]{:S(2)}, u32[]{:S(2)}) collective-permute-start(bf16[32,2176]{1,0:T(8,128)(2,1)} %pad_maximum_fusion.47), channel_id=1, source_target_pairs={{0,24},{8,16},{16,8},{24,0},{1,25},{9,17},{17,9},{25,1},{2,26},{10... | collective-permute-start | bytes 417800 | tf_op jit(solution)/shard_map/ppermute | solution.py:25
  108.7 40.1 %collective-permute-start.58 = (bf16[32,2176]{1,0:T(8,128)(2,1)}, bf16[32,2176]{1,0:T(8,128)(2,1)}, u32[]{:S(2)}, u32[]{:S(2)}) collective-permute-start(bf16[32,2176]{1,0:T(8,128)(2,1)} %pad_maximum_fusion.46), channel_id=1, source_target_pairs={{0,4},{2,6},{4,0},{6,2},{1,5},{3,7},{5,1},{7,3},{8,12},{10,14},{12... | collective-permute-start | bytes 417800 | tf_op jit(solution)/shard_map/ppermute | solution.py:25
  124.0 183.2 %all-gather.17.cloned.1.call-start = ((), (), s32[]{:S(2)}) async-start(), calls=%async_computation.14 | async-start | bytes 4915200 | tf_op jit(solution)/shard_map/all_gather | solution.py:103
  161.0 45.7 %collective-permute-start.65 = (bf16[64,2176]{1,0:T(8,128)(2,1)}, bf16[64,2176]{1,0:T(8,128)(2,1)}, u32[]{:S(2)}, u32[]{:S(2)}) collective-permute-start(bf16[64,2176]{1,0:T(8,128)(2,1)} %pad_maximum_fusion.27), channel_id=1, source_target_pairs={{0,4},{2,6},{4,0},{6,2},{1,5},{3,7},{5,1},{7,3},{8,12},{10,14},{12... | collective-permute-start | bytes 835592 | tf_op jit(solution)/shard_map/ppermute | solution.py:25
  197.6 24.2 %collective-permute-start.62 = (bf16[64,2176]{1,0:T(8,128)(2,1)}, bf16[64,2176]{1,0:T(8,128)(2,1)}, u32[]{:S(2)}, u32[]{:S(2)}) collective-permute-start(bf16[64,2176]{1,0:T(8,128)(2,1)} %pad_maximum_fusion.24), channel_id=1, source_target_pairs={{0,24},{8,16},{16,8},{24,0},{1,25},{9,17},{17,9},{25,1},{2,26},{10... | collective-permute-start | bytes 835592 | tf_op jit(solution)/shard_map/ppermute | solution.py:25
  204.9 28.0 %collective-permute-start.28 = (bf16[64,2048]{0,1:T(8,128)(2,1)}, bf16[64,2048]{0,1:T(8,128)(2,1)}, u32[]{:S(2)}, u32[]{:S(2)}) collective-permute-start(bf16[64,2048]{0,1:T(8,128)(2,1)} %slice.1506), channel_id=1, source_target_pairs={{0,4},{2,6},{4,0},{6,2},{1,5},{3,7},{5,1},{7,3},{8,12},{10,14},{12... | collective-permute-start | bytes 786440 | tf_op jit(solution)/shard_map/ppermute | solution.py:25
  206.6 26.2 %collective-permute-start.25 = (bf16[64,2048]{0,1:T(8,128)(2,1)}, bf16[64,2048]{0,1:T(8,128)(2,1)}, u32[]{:S(2)}, u32[]{:S(2)}) collective-permute-start(bf16[64,2048]{0,1:T(8,128)(2,1)} %slice.1509), channel_id=1, source_target_pairs={{0,24},{8,16},{16,8},{24,0},{1,25},{9,17},{17,9},{25,1},{2,26},{10... | collective-permute-start | bytes 786440 | tf_op jit(solution)/shard_map/ppermute | solution.py:25
  206.6 26.2 %collective-permute-start.26 = (bf16[64,2048]{0,1:T(8,128)(2,1)}, bf16[64,2048]{0,1:T(8,128)(2,1)}, u32[]{:S(2)}, u32[]{:S(2)}) collective-permute-start(bf16[64,2048]{0,1:T(8,128)(2,1)} %slice.1508), channel_id=1, source_target_pairs={{0,6},{2,4},{4,2},{6,0},{1,7},{3,5},{5,3},{7,1},{8,14},{10,12},{12... | collective-permute-start | bytes 786440 | tf_op jit(solution)/shard_map/ppermute | solution.py:25
  208.8 24.0 %collective-permute-start.27 = (bf16[64,2048]{0,1:T(8,128)(2,1)}, bf16[64,2048]{0,1:T(8,128)(2,1)}, u32[]{:S(2)}, u32[]{:S(2)}) collective-permute-start(bf16[64,2048]{0,1:T(8,128)(2,1)} %slice.1507), channel_id=1, source_target_pairs={{0,8},{8,0},{16,24},{24,16},{1,9},{9,1},{17,25},{25,17},{2,10},{10... | collective-permute-start | bytes 786440 | tf_op jit(solution)/shard_map/ppermute | solution.py:25
  223.8 32.2 %collective-permute-start.53 = (bf16[4,64,1920]{2,1,0:T(8,128)(2,1)}, bf16[4,64,1920]{2,1,0:T(8,128)(2,1)}, u32[]{:S(2)}, u32[]{:S(2)}) collective-permute-start(bf16[4,64,1920]{2,1,0:T(8,128)(2,1)} %all-to-all-done.1), channel_id=1, source_target_pairs={{0,0},{1,4},{4,1},{5,5},{2,2},{3,6},{6,3},{7,7},{8,8},{9,12},{12,9... | collective-permute-start | bytes 2949128 | tf_op jit(solution)/shard_map/ppermute | solution.py:29
  256.0 65.4 %collective-permute-start.66 = (bf16[128,2176]{0,1:T(8,128)(2,1)}, bf16[128,2176]{0,1:T(8,128)(2,1)}, u32[]{:S(2)}, u32[]{:S(2)}) collective-permute-start(bf16[128,2176]{0,1:T(8,128)(2,1)} %pad_maximum_fusion.4), channel_id=1, source_target_pairs={{0,6},{2,4},{4,2},{6,0},{1,7},{3,5},{5,3},{7,1},{8,14},{10,12},{12... | collective-permute-start | bytes 1671176 | tf_op jit(solution)/shard_map/ppermute | solution.py:25
  259.0 110.0 %all-gather.19.cloned.1.call-start = ((), (), s32[]{:S(2)}) async-start(), calls=%async_computation.15 | async-start | bytes 11796480 | tf_op jit(solution)/shard_map/all_gather | solution.py:104
  307.2 385.7 %reduce-scatter.5.cloned.1.call-start = ((), (), s32[]{:S(2)}) async-start(), calls=%async_computation.8 | async-start | bytes 12582912 | tf_op jit(solution)/shard_map/reduce_scatter | solution.py:111
  318.7 25.1 %collective-permute-start.48 = (bf16[64,2048]{1,0:T(8,128)(2,1)}, bf16[64,2048]{1,0:T(8,128)(2,1)}, u32[]{:S(2)}, u32[]{:S(2)}) collective-permute-start(bf16[64,2048]{1,0:T(8,128)(2,1)} %pad_maximum_fusion.37), channel_id=1, source_target_pairs={{0,4},{2,6},{4,0},{6,2},{1,5},{3,7},{5,1},{7,3},{8,12},{10,14},{12... | collective-permute-start | bytes 786440 | tf_op jit(solution)/shard_map/ppermute | solution.py:25
  321.4 22.4 %collective-permute-start.47 = (bf16[64,2048]{1,0:T(8,128)(2,1)}, bf16[64,2048]{1,0:T(8,128)(2,1)}, u32[]{:S(2)}, u32[]{:S(2)}) collective-permute-start(bf16[64,2048]{1,0:T(8,128)(2,1)} %pad_maximum_fusion.36), channel_id=1, source_target_pairs={{0,8},{8,0},{16,24},{24,16},{1,9},{9,1},{17,25},{25,17},{2,10},{10... | collective-permute-start | bytes 786440 | tf_op jit(solution)/shard_map/ppermute | solution.py:25
  518.3 246.7 %reduce-scatter.9.cloned.1.call-start = ((), (), s32[]{:S(2)}) async-start(), calls=%async_computation.10 | async-start | bytes 3932160 | tf_op jit(solution)/shard_map/reduce_scatter | solution.py:111
  589.5 57.4 %collective-permute-start.73 = (bf16[128,2048]{0,1:T(8,128)(2,1)}, bf16[128,2048]{0,1:T(8,128)(2,1)}, u32[]{:S(2)}, u32[]{:S(2)}) collective-permute-start(bf16[128,2048]{0,1:T(8,128)(2,1)} %get-tuple-element.449), channel_id=1, source_target_pairs={{0,24},{8,16},{16,8},{24,0},{1,25},{9,17},{17,9},{25,1},{2,26},{10... | collective-permute-start | bytes 1572872 | tf_op jit(solution)/shard_map/ppermute | solution.py:25
  590.6 56.3 %collective-permute-start.72 = (bf16[128,2048]{0,1:T(8,128)(2,1)}, bf16[128,2048]{0,1:T(8,128)(2,1)}, u32[]{:S(2)}, u32[]{:S(2)}) collective-permute-start(bf16[128,2048]{0,1:T(8,128)(2,1)} %get-tuple-element.450), channel_id=1, source_target_pairs={{0,4},{2,6},{4,0},{6,2},{1,5},{3,7},{5,1},{7,3},{8,12},{10,14},{12... | collective-permute-start | bytes 1572872 | tf_op jit(solution)/shard_map/ppermute | solution.py:25
  590.7 56.3 %collective-permute-start.71 = (bf16[128,2048]{0,1:T(8,128)(2,1)}, bf16[128,2048]{0,1:T(8,128)(2,1)}, u32[]{:S(2)}, u32[]{:S(2)}) collective-permute-start(bf16[128,2048]{0,1:T(8,128)(2,1)} %get-tuple-element.451), channel_id=1, source_target_pairs={{0,8},{8,0},{16,24},{24,16},{1,9},{9,1},{17,25},{25,17},{2,10},{10... | collective-permute-start | bytes 1572872 | tf_op jit(solution)/shard_map/ppermute | solution.py:25
  590.7 56.3 %collective-permute-start.70 = (bf16[128,2048]{0,1:T(8,128)(2,1)}, bf16[128,2048]{0,1:T(8,128)(2,1)}, u32[]{:S(2)}, u32[]{:S(2)}) collective-permute-start(bf16[128,2048]{0,1:T(8,128)(2,1)} %get-tuple-element.452), channel_id=1, source_target_pairs={{0,6},{2,4},{4,2},{6,0},{1,7},{3,5},{5,3},{7,1},{8,14},{10,12},{12... | collective-permute-start | bytes 1572872 | tf_op jit(solution)/shard_map/ppermute | solution.py:25
  646.9 146.0 %reduce-scatter.7.cloned.1.call-start = ((), (), s32[]{:S(2)}) async-start(), calls=%async_computation.9 | async-start | bytes 5242880 | tf_op jit(solution)/shard_map/reduce_scatter | solution.py:112
  692.9 109.5 %reduce-scatter.11.cloned.1.call-start = ((), (), s32[]{:S(2)}) async-start(), calls=%async_computation.11 | async-start | bytes 1638400 | tf_op jit(solution)/shard_map/reduce_scatter | solution.py:112
  765.0 44.7 %all-gather.21.cloned.1.call-start = ((), (), s32[]{:S(2)}) async-start(), calls=%async_computation.16 | async-start | bytes 1572864 | tf_op jit(solution)/shard_map/all_gather | solution.py:309
  782.7 33.5 %all-gather.23.cloned.1.call-start = ((), (), s32[]{:S(2)}) async-start(), calls=%async_computation.17 | async-start | bytes 1572864 | tf_op jit(solution)/shard_map/all_gather | solution.py:309
  792.9 27.6 %collective-permute-start.138 = (bf16[4,64,2048]{2,1,0:T(8,128)(2,1)}, bf16[4,64,2048]{2,1,0:T(8,128)(2,1)}, u32[]{:S(2)}, u32[]{:S(2)}) collective-permute-start(bf16[4,64,2048]{2,1,0:T(8,128)(2,1)} %bitcast.405), channel_id=1, source_target_pairs={{0,0},{1,4},{4,1},{5,5},{2,2},{3,6},{6,3},{7,7},{8,8},{9,12},{12,9... | collective-permute-start | bytes 3145736 | tf_op jit(solution)/shard_map/ppermute | solution.py:29
  (275 other events, 3950.3 us)
Sparse Core Ops, SparseCore 0:
  100.3 23.6 all-gather.12
  125.6 14.6 all-gather.14
  259.1 43.1 all-gather.16
  307.3 20.5 all-gather.18
  518.4 19.2 reduce-scatter.4
  647.0 11.5 reduce-scatter.8
  693.0 46.5 reduce-scatter.6
  765.1 23.1 reduce-scatter.10
  790.1 11.4 all-gather.20
  803.1 13.0 all-gather.22
where the time goes:
time: 886 us; the launch traced here: 869 us
  local copies, waits for them, and re-layouts  216 us (24%)
  starting transfers between devices  213 us (24%)
  waiting for transfers between devices  182 us (21%)
  other arithmetic  130 us (15%)
  matrix products  82 us (9%)
  blocking collectives  27.7 us (3%)
  between operations  17.9 us (2%)
    ppermute x136, starting transfers between devices, exchange(): return lambda v: lax.ppermute(v, axes, pairs)  169 us
    ppermute x136, waiting for transfers between devices, exchange(): return lambda v: lax.ppermute(v, axes, pairs)  150 us
    dot_general x19, matrix products, dot(): lax.dot_general(a, b, (((left,), (right,)), ((), ())), preferred_element_...  82 us
    unnamed x373, local copies, waits for them, and re-layouts  47.3 us
    add x52, other arithmetic, cube_scatter(): a[:half].astype(F32) + b.astype(F32)  36.7 us
    optimization_barrier x24, local copies, waits for them, and re-layouts, cube_gather(): lax.optimization_barrier(tuple((CUBE[(i + step) % 4](parts[i]) for i in r...  34.2 us
    concatenate x48, other arithmetic, cube_gather(): parts = [jnp.concatenate([a, b], axis=0) for a, b in zip(parts, arrived)]  32.2 us
    slice x52, local copies, waits for them, and re-layouts, cube_scatter(): parts[i][half:].astype(BF)  27 us
  transfers between devices with their start and end apart: 154, of which 62 were waited for; matrix products, arithmetic and copies ran while one was open for 38% of the time, Pallas kernels for 0%

commit v1 on v0

v1 whole, which is shorter than its diff:
```python
import math

import jax
import jax.numpy as jnp
from jax import lax
from jax.sharding import Mesh
from jax.sharding import PartitionSpec as P
from jax.experimental import pallas as pl
from jax.experimental.pallas import tpu as pltpu

EPSILON = 1e-05
ROPE_BASE = 10000.0
BF = jnp.bfloat16
F32 = jnp.float32

AXES = ("x", "z", "yl", "yh", "c")
SIZES = (4, 4, 2, 2, 2)
CONTEXT = ("z", "yl")
TENSOR = ("yh", "c")
WEIGHT = ("x", "z", "yl")
Y = ("yl", "yh")
SWAP = ("yl", "c")


def exchange(axes, size, mask):
    pairs = [(at, at ^ mask) for at in range(size)]
    return lambda v: lax.ppermute(v, axes, pairs)


CUBE = (exchange("z", 4, 1), exchange(Y, 4, 2), exchange("z", 4, 3), exchange(Y, 4, 3))
swap_cores = lambda v: lax.ppermute(v, SWAP, [(0, 0), (1, 2), (2, 1), (3, 3)])
other_core = exchange("c", 2, 1)
other_half = exchange("yh", 2, 1)
GROUP = ("z", "yl", "yh")
VMEM = pl.BlockSpec(memory_space=pltpu.VMEM)
SMEM = pl.BlockSpec(memory_space=pltpu.SMEM)
LIMIT = 56 * 1024 * 1024


def dot(a, b, left=1, right=0):
    return lax.dot_general(a, b, (((left,), (right,)), ((), ())), preferred_element_type=F32)


def kernel_call(body, outs, in_specs, cost=None):
    return pl.pallas_call(
        body,
        out_shape=[jax.ShapeDtypeStruct(shape, kind) for shape, kind in outs],
        in_specs=in_specs,
        out_specs=[VMEM] * len(outs),
        compiler_params=pltpu.CompilerParams(vmem_limit_bytes=LIMIT),
        cost_estimate=cost,
    )


def cube_gather(own):
    rows = own.shape[0] // 4
    parts = [own[i * rows : (i + 1) * rows] for i in range(4)]
    for step in range(4):
        arrived = [CUBE[(i + step) % 4](parts[i]) for i in range(4)]
        if step < 3:
            parts = [jnp.concatenate([a, b], axis=0) for a, b in zip(parts, arrived)]
    return jnp.concatenate(parts + arrived, axis=0)


def project_kernel(rows_ref, weight_ref, *outs):
    for at, out in enumerate(outs):
        out[...] = dot(rows_ref[at * 128 : (at + 1) * 128, :], weight_ref[...], 1, 1).astype(BF)


def project(rows, weight):
    depth = rows.shape[1]
    return pl.pallas_call(
        project_kernel,
        grid=(4,),
        out_shape=[jax.ShapeDtypeStruct((128, 2048), BF)] * 8,
        in_specs=[
            pl.BlockSpec((1024, depth), lambda n: (0, 0)),
            pl.BlockSpec((512, depth), lambda n: (n, 0)),
        ],
        out_specs=[pl.BlockSpec((128, 512), lambda n: (0, n))] * 8,
        compiler_params=pltpu.CompilerParams(vmem_limit_bytes=LIMIT),
        cost_estimate=pl.CostEstimate(
            flops=2 * 1024 * 2048 * depth,
            bytes_accessed=2 * (3072 * depth + 1024 * 2048),
            transcendentals=0,
        ),
    )(rows, weight)


def fold_kernel(*refs):
    half = refs[0].shape[0] // 2
    for i in range(4):
        kept, arrived, keep, send = refs[i], refs[4 + i], refs[8 + i], refs[12 + i]
        keep[...] = (kept[:half].astype(F32) + arrived[:half].astype(F32)).astype(BF)
        send[...] = (kept[half:].astype(F32) + arrived[half:].astype(F32)).astype(BF)


def cube_scatter(pieces):
    kept, sent = pieces[:4], pieces[4:]
    for step in (3, 2, 1, 0):
        arrived = [CUBE[(i + step) % 4](sent[i]) for i in range(4)]
        if step:
            half = ((kept[0].shape[0] // 2, 2048), BF)
            folded = kernel_call(fold_kernel, [half] * 8, [VMEM] * 8)(*kept, *arrived)
            kept, sent = folded[:4], folded[4:]
    return jnp.concatenate([a.astype(F32) + b.astype(F32) for a, b in zip(kept, arrived)], axis=0)


def block_places():
    at = jnp.arange(64, dtype=jnp.int32)
    part, block = (at >> 3) & 3, (at & 7) | ((at >> 5) << 3)
    turned = [(block >> ((dim - part) & 3)) & 1 for dim in range(4)]
    z = lax.axis_index("z") ^ (turned[0] ^ (3 * turned[2]))
    y = (2 * lax.axis_index("yh") + lax.axis_index("yl")) ^ (turned[1] ^ (3 * turned[3]))
    return ((2 * z + (y & 1)) * 2 + (y >> 1)) * 4 + part


def cotangent_kernel(places, length, source, grad, chosen):
    row = lax.broadcasted_iota(jnp.int32, (16, 2048), 0)
    for at in range(64):
        start = pl.multiple_of(places[at] * 16, 16)
        held = source[pl.ds(start, 16), :]
        inside = row < length[0] - start
        grad[at * 16 : (at + 1) * 16, :] = jnp.where(inside, held[:, :2048], jnp.zeros((), BF))
        chosen[at * 16 : (at + 1) * 16, :] = held[:, 2048:]


def place_kernel(places, source, out):
    for at in range(64):
        out[pl.ds(pl.multiple_of(places[at] * 16, 16), 16), :] = source[at * 16 : (at + 1) * 16, :]


def token_sums(columns, place_of):
    count = len(columns)
    held = jnp.stack([v.reshape(64, 16) for v in columns], axis=1).reshape(64, 16 * count)
    placed = lax.dot_general(
        place_of, held, (((0,), (0,)), ((), ())), precision=lax.Precision.HIGHEST
    )
    sent = jnp.broadcast_to(placed[None], (16,) + placed.shape)
    total = jnp.sum(lax.all_to_all(sent, GROUP, split_axis=0, concat_axis=0, tiled=True), axis=0)
    back = lax.dot_general(
        place_of, total, (((1,), (0,)), ((), ())), precision=lax.Precision.HIGHEST
    )
    return back.reshape(64, count, 16).transpose(0, 2, 1).reshape(1024, count)


def angles(positions, head_size):
    steps_half = jnp.arange(head_size // 2).astype(F32)
    frequency = jnp.exp(steps_half * (-2.0 * math.log(ROPE_BASE) / head_size))
    turned = positions.astype(F32)[:, None] * frequency[None, :]
    cosine, sine = jnp.cos(turned), jnp.sin(turned)
    return (
        jnp.concatenate([cosine, cosine], axis=-1),
        jnp.concatenate([-sine, sine], axis=-1),
    )


SCALE = 128 ** (-0.5)


def forward_kernel(
    qkv, rates, gains, cosine, sine, q_pos, k_pos, queries, keys, values, attended, log_total
):
    def turn(held):
        return held * cosine[...] + pltpu.roll(held, 64, 1) * sine[...]

    queries[...] = turn(qkv[:, :128] * rates[:, 0:1] * gains[0:1, :]).astype(BF)
    keys[...] = turn(qkv[:, 128:256] * rates[:, 1:2] * gains[1:2, :]).astype(BF)
    values[...] = qkv[:, 256:].astype(BF)
    for at in range(4):
        rows = slice(at * 256, (at + 1) * 256)
        scores = dot(queries[rows, :], keys[...], 1, 1) * SCALE
        scores = jnp.where(k_pos[...] <= q_pos[rows, :], scores, -1e30)
        peak = jnp.max(scores, axis=1, keepdims=True)
        raised = jnp.exp(scores - peak)
        total = jnp.sum(raised, axis=1, keepdims=True)
        probs = (raised * (1.0 / total)).astype(BF)
        attended[rows, :] = dot(probs, values[...]).astype(BF)
        log_total[rows, :] = peak + jnp.log(total)


def backward_kernel(
    qkv, rates, gains, cosine, sine, q_pos, k_pos, queries, keys, values, log_total, grad,
    q_scaled, k_scaled, v_grad, inner, gain_grads, key_grad, value_grad,
):
    def turn_back(held):
        return held * cosine[...] - pltpu.roll(held, 64, 1) * sine[...]

    for at in range(4):
        rows = slice(at * 256, (at + 1) * 256)
        scores = dot(queries[rows, :], keys[...], 1, 1) * SCALE
        allowed = k_pos[...] <= q_pos[rows, :]
        probs = jnp.where(allowed, jnp.exp(scores - log_total[rows, :]), 0.0)
        prob_grad = dot(grad[rows, :], values[...], 1, 1)
        delta = jnp.sum(probs * prob_grad, axis=1, keepdims=True)
        score_grad = (probs * (prob_grad - delta)).astype(BF)
        q_scaled[rows, :] = dot(score_grad, keys[...]) * SCALE
        key_part = dot(score_grad, queries[rows, :], 0, 0) * SCALE
        value_part = dot(probs.astype(BF), grad[rows, :], 0, 0)
        if at == 0:
            key_grad[...] = key_part
            value_grad[...] = value_part
        else:
            key_grad[...] += key_part
            value_grad[...] += value_part
    v_grad[...] = value_grad[...].astype(BF)
    q_norm_grad = turn_back(q_scaled[...])
    k_norm_grad = turn_back(key_grad[...])
    q_turned = q_norm_grad * qkv[:, :128]
    k_turned = k_norm_grad * qkv[:, 128:256]
    gain_grads[0:1, :] = jnp.sum(q_turned * rates[:, 0:1], axis=0, keepdims=True)
    gain_grads[1:2, :] = jnp.sum(k_turned * rates[:, 1:2], axis=0, keepdims=True)
    inner[:, 0:1] = jnp.sum(q_turned * gains[0:1, :], axis=1, keepdims=True)
    inner[:, 1:2] = jnp.sum(k_turned * gains[1:2, :], axis=1, keepdims=True)
    q_scaled[...] = q_norm_grad * gains[0:1, :]
    k_scaled[...] = k_norm_grad * gains[1:2, :]


def attention_cost(products):
    return pl.CostEstimate(
        flops=products * 2 * 1024 * 1024 * 128, bytes_accessed=6 << 20, transcendentals=1 << 20
    )


def core_fold(grads):
    held = grads.astype(BF)
    return (held[:1024].astype(F32) + other_core(held[1024:]).astype(F32)).astype(BF)


def per_device(
    tokens,
    lengths,
    routes,
    attn_gain,
    q_gain,
    k_gain,
    w_query,
    w_key,
    w_value,
    w_out,
    mlp_gain,
    router,
    w_gate,
    w_up,
    w_down,
    cotangent,
):
    z = lax.axis_index("z")
    yh = lax.axis_index("yh")
    core = lax.axis_index("c")

    def four(w):
        return w.reshape(64, 4, -1).transpose(1, 0, 2)

    def pack_experts(w):
        return four(w.transpose(1, 0, 2).reshape(64, 2560))

    def per_row(v):
        return jnp.broadcast_to(v[None], (4,) + v.shape)

    gains = jnp.stack([q_gain, k_gain], axis=-1)
    extra = jnp.concatenate(
        [
            per_row(attn_gain[:, None]),
            per_row(mlp_gain[:, None]),
            per_row(router),
            jnp.pad(gains, ((0, 0), (0, 60), (0, 0))),
            jnp.zeros((4, 64, 114), BF),
        ],
        axis=-1,
    )
    first_pack = jnp.concatenate(
        [four(w_query), four(w_key), four(w_value), extra, four(w_out.T)], axis=-1
    )
    second_pack = jnp.concatenate(
        [pack_experts(w_gate), pack_experts(w_up), four(w_down.reshape(2560, 64).T)], axis=-1
    )
    first_held = swap_cores(first_pack)
    first_held = lax.all_to_all(
        jnp.broadcast_to(first_held[None], (4, 4, 64, 640)).reshape(16, 64, 640),
        ("x", "z"),
        split_axis=0,
        concat_axis=0,
        tiled=True,
    ).reshape(1024, 640)
    first_all = jnp.concatenate([first_held, other_core(first_held)], axis=0)
    second_held = lax.all_to_all(
        swap_cores(second_pack), "z", split_axis=0, concat_axis=0, tiled=True
    )
    second_held = lax.all_gather(second_held, "x", axis=0, tiled=False).reshape(1024, 1920)
    second_all = jnp.concatenate([second_held, other_core(second_held)], axis=0)
    w_qkv = first_all[:, :384]
    extra_all = first_all[:, 384:512]
    out_t = first_all[:, 512:]
    w_in = second_all[:, :1280]
    down_t = second_all[:, 1280:]
    attn_row = extra_all[:, 0].astype(F32)[None]
    mlp_row = extra_all[:, 1].astype(F32)[None]
    router_all = jnp.pad(extra_all[:, 2:12], ((0, 0), (0, 118)))
    gain_blocks = extra_all[:, 12:14].reshape(2, 16, 64, 2)[:, :, :4]
    gain_blocks = jnp.where(core == 0, gain_blocks, gain_blocks[::-1])
    gain_rows = gain_blocks.transpose(3, 1, 0, 2).reshape(2, 128).astype(F32)

    own_start = (core, yh * 64, 0)
    own_tokens = lax.dynamic_slice(tokens, own_start, (1, 64, 2048))[0]
    own_cot = lax.dynamic_slice(cotangent, own_start, (1, 64, 2048))[0]
    own_routes = lax.dynamic_slice(routes, own_start, (1, 64, 8))[0]
    slot_length = lax.dynamic_index_in_dim(lengths, core, keepdims=False)
    expert_ids = jnp.arange(10, dtype=jnp.int32)
    own_chosen = jnp.sum((own_routes[:, :, None] == expert_ids).astype(BF), axis=1)

    def own_first(v):
        halves = v.reshape(64, 16, 2, 64)
        halves = jnp.where(core == 0, halves, halves[:, :, ::-1])
        return halves.transpose(0, 2, 1, 3).reshape(64, 2048)

    def natural(v):
        halves = v.reshape(64, 2, 16, 64).transpose(0, 2, 1, 3)
        return jnp.where(core == 0, halves, halves[:, :, ::-1]).reshape(64, 2048)

    own_tokens = own_first(own_tokens)
    own_cot = own_first(own_cot)
    all_tokens = cube_gather(own_tokens)
    with_routes = lax.all_gather(
        jnp.concatenate([own_cot, jnp.pad(own_chosen, ((0, 0), (0, 118)))], axis=1),
        GROUP,
        axis=0,
        tiled=True,
    )
    places = block_places()
    place_of = (places[:, None] == jnp.arange(64, dtype=jnp.int32)[None]).astype(F32)
    positions = (places[:, None] * 16 + jnp.arange(16, dtype=jnp.int32)[None]).reshape(1024)
    grad_out, chosen = kernel_call(
        cotangent_kernel, [((1024, 2048), BF), ((1024, 128), BF)], [SMEM, SMEM, VMEM]
    )(places, slot_length[None], with_routes)
    chosen = chosen[:, :10].astype(F32)
    own_positions = (
        (2 * z + lax.axis_index("yl")) * 128 + yh * 64 + jnp.arange(64, dtype=jnp.int32)
    )
    own_grad_out = jnp.where((own_positions < slot_length)[:, None], own_cot.astype(F32), 0.0)

    all_rows = all_tokens.astype(F32)
    all_rate = lax.rsqrt(jnp.mean(all_rows * all_rows, axis=-1, keepdims=True) + EPSILON)
    normed = (all_rows * all_rate * attn_row).astype(BF)
    qkv = dot(normed, w_qkv)
    squares = token_sums(
        [
            jnp.sum(qkv[:, :128] * qkv[:, :128], axis=1),
            jnp.sum(qkv[:, 128:256] * qkv[:, 128:256], axis=1),
        ],
        place_of,
    )
    rates = lax.rsqrt(squares / 2048 + EPSILON)
    cosine, sine = angles(positions, 128)
    q_pos = positions[:, None]
    k_pos = jnp.where(positions < slot_length, positions, 1 << 20)[None]
    head = ((1024, 128), BF)
    queries, keys, values, attended, log_total = kernel_call(
        forward_kernel, [head, head, head, head, ((1024, 1), F32)], [VMEM] * 7, attention_cost(2)
    )(qkv, rates, gain_rows, cosine, sine, q_pos, k_pos)
    own_rows = own_tokens.astype(F32)
    middle = own_rows + cube_scatter(project(attended, out_t))

    second_rate = lax.rsqrt(jnp.mean(middle * middle, axis=-1, keepdims=True) + EPSILON)
    mixed_in = cube_gather((middle * second_rate * mlp_row).astype(BF))
    logits = dot(mixed_in, router_all)[:, :10]
    route_probs = jax.nn.softmax(logits, axis=-1)
    gate_values = route_probs * chosen
    tile_expert = (5 * z + jnp.arange(5, dtype=jnp.int32)) // 2
    tile_of = (tile_expert[None, :] == expert_ids[:, None]).astype(F32)
    tile_gates = jnp.sum(gate_values[:, :, None] * tile_of[None], axis=1)
    wide_gates = jnp.repeat(tile_gates, 128, axis=1)
    hidden = dot(mixed_in, w_in)
    gate_h, up_h = hidden[:, :640], hidden[:, 640:]
    sig = jax.nn.sigmoid(gate_h)
    silu = gate_h * sig
    activated = (silu * up_h).astype(BF).astype(F32)
    gated = (activated * wide_gates).astype(BF)
    (placed,) = kernel_call(place_kernel, [((1024, 640), BF)], [SMEM, VMEM])(places, gated)
    mixture = lax.all_to_all(
        dot(placed, down_t, 1, 1).astype(BF).reshape(16, 64, 2048),
        GROUP,
        split_axis=0,
        concat_axis=0,
        tiled=True,
    )
    own_output = (middle + jnp.sum(mixture.astype(F32), axis=0)).astype(BF)
    out_grad = dot(grad_out, down_t)
    tile_parts = jnp.sum((activated * out_grad).reshape(1024, 5, 128), axis=-1)
    gate_part = jnp.sum(tile_parts[:, None, :] * tile_of[None], axis=-1)
    act_grad = out_grad * wide_gates
    gate_h_grad = (act_grad * up_h * sig * (1.0 + gate_h * (1.0 - sig))).astype(BF)
    up_h_grad = (act_grad * silu).astype(BF)
    chosen_grad = gate_part * chosen
    logit_grad = (
        route_probs * (chosen_grad - jnp.sum(chosen_grad * route_probs, axis=-1, keepdims=True))
    ).astype(BF)
    hidden_grad = jnp.concatenate(
        [gate_h_grad, up_h_grad, jnp.pad(logit_grad, ((0, 0), (0, 118)))], axis=1
    )
    in_grads = dot(mixed_in, hidden_grad, 0, 0)
    down_grads = dot(grad_out, gated, 0, 0)
    mixed_grad = cube_scatter(
        project(hidden_grad, jnp.concatenate([w_in, router_all], axis=1))
    )
    expert_grads = core_fold(jnp.concatenate([in_grads, down_grads], axis=1))
    expert_grads = lax.psum_scatter(
        expert_grads.reshape(4, 256, 2048), "x", scatter_dimension=0, tiled=False
    ).reshape(4, 64, 2048)
    expert_grads = lax.all_to_all(
        swap_cores(expert_grads), "z", split_axis=0, concat_axis=0, tiled=True
    )
    scaled = mixed_grad * mlp_row
    middle_grad = (
        own_grad_out
        + second_rate * scaled
        - middle * second_rate**3 * jnp.mean(scaled * middle, axis=-1, keepdims=True)
    )

    branch_grad = cube_gather(middle_grad.astype(BF))
    out_grads = dot(branch_grad, attended, 0, 0)
    attended_grad = dot(branch_grad, out_t).astype(BF)
    wide_head = ((1024, 128), F32)
    q_scaled, k_scaled, v_proj_grad, inner, gain_grads, _, _ = kernel_call(
        backward_kernel,
        [wide_head, wide_head, head, ((1024, 2), F32), ((2, 128), F32), wide_head, wide_head],
        [VMEM] * 12,
        attention_cost(5),
    )(
        qkv, rates, gain_rows, cosine, sine, q_pos, k_pos,
        queries, keys, values, log_total, attended_grad,
    )
    inner = token_sums([inner[:, 0], inner[:, 1]], place_of) * rates**3 / 2048
    q_proj_grad = (rates[:, :1] * q_scaled - qkv[:, :128] * inner[:, :1]).astype(BF)
    k_proj_grad = (rates[:, 1:] * k_scaled - qkv[:, 128:256] * inner[:, 1:]).astype(BF)
    qkv_grad = jnp.concatenate([q_proj_grad, k_proj_grad, v_proj_grad], axis=1)
    qkv_grads = dot(normed, qkv_grad, 0, 0)
    normed_grad = cube_scatter(project(qkv_grad, w_qkv))
    gain_block = gain_grads.reshape(2, 16, 2, 4)
    gain_block = jnp.where(core == 0, gain_block, gain_block[:, :, ::-1])
    gain_block = gain_block.transpose(2, 1, 3, 0)
    gain_block = jnp.pad(gain_block, ((0, 0), (0, 0), (0, 60), (0, 126))).reshape(2048, 128)
    attn_grads = core_fold(jnp.concatenate([qkv_grads, out_grads, gain_block], axis=1))
    attn_grads = lax.all_to_all(
        attn_grads.reshape(16, 64, 640), ("x", "z"), split_axis=0, concat_axis=0, tiled=True
    )
    attn_grads = jnp.sum(attn_grads.reshape(4, 4, 64, 640).astype(F32), axis=0).astype(BF)
    attn_grads = swap_cores(attn_grads)
    scaled = normed_grad * attn_row
    own_rate = lax.rsqrt(jnp.mean(own_rows * own_rows, axis=-1, keepdims=True) + EPSILON)
    own_input_grad = (
        middle_grad
        + own_rate * scaled
        - own_rows * own_rate**3 * jnp.mean(scaled * own_rows, axis=-1, keepdims=True)
    )

    def whole(own):
        far = other_half(own)
        both = jnp.where(yh == 0, jnp.concatenate([own, far]), jnp.concatenate([far, own]))
        there = other_core(both)
        return jnp.where(core == 0, jnp.stack([both, there]), jnp.stack([there, both]))

    def wide(grads):
        return grads.transpose(1, 0, 2).reshape(64, -1).astype(F32)

    def experts(grads):
        return wide(grads).reshape(64, 10, 256).transpose(1, 0, 2)

    q_grads = wide(attn_grads[:, :, :128])
    k_grads = wide(attn_grads[:, :, 128:256])
    v_grads = wide(attn_grads[:, :, 256:384])
    o_grads = wide(attn_grads[:, :, 384:512]).T
    q_gain_grad = attn_grads[:, :4, 512].astype(F32)
    k_gain_grad = attn_grads[:, :4, 513].astype(F32)
    gate_grads = experts(expert_grads[:, :, :640])
    up_grads = experts(expert_grads[:, :, 640:1280])
    router_part = jnp.sum(expert_grads[:, :, 1280:1290].astype(F32), axis=0)
    down_out = wide(expert_grads[:, :, 1408:]).T.reshape(10, 256, 64)

    attn_part = sum(
        jnp.sum(w.astype(F32) * g, axis=1)
        for w, g in ((w_query, q_grads), (w_key, k_grads), (w_value, v_grads))
    )
    mlp_part = sum(
        jnp.sum(w.astype(F32) * g, axis=(0, 2)) for w, g in ((w_gate, gate_grads), (w_up, up_grads))
    ) + jnp.sum(router.astype(F32) * router_part, axis=1)
    summed = jnp.concatenate([router_part, attn_part[:, None], mlp_part[:, None]], axis=1)
    summed = summed + other_core(summed)
    summed = summed + other_half(summed)
    return (
        whole(natural(own_output)),
        whole(natural(own_input_grad.astype(BF))).astype(F32),
        summed[:, 10] / attn_gain.astype(F32),
        q_gain_grad,
        k_gain_grad,
        q_grads,
        k_grads,
        v_grads,
        o_grads,
        summed[:, 11] / mlp_gain.astype(F32),
        summed[:, :10],
        gate_grads,
        up_grads,
        down_out,
    )


def solution(mesh):
    fine = Mesh(mesh.devices.reshape(SIZES), AXES)
    rows = P("x", CONTEXT, None)
    vector = P(WEIGHT)
    gains = P(TENSOR, WEIGHT)
    tall = P(WEIGHT, TENSOR)
    routed = P(WEIGHT, None)
    hidden = P(None, WEIGHT, TENSOR)
    back = P(None, TENSOR, WEIGHT)
    weights = (vector, gains, gains, tall, tall, tall, gains, vector, routed, hidden, hidden, back)
    return jax.shard_map(
        per_device,
        mesh=fine,
        in_specs=(rows, P("x"), rows) + weights + (rows,),
        out_specs=(rows, rows) + weights,
        check_vma=False,
    )
```

time: 886 us -> 795 us (0.90)
  Pallas kernels: 0 us -> 78.7 us
  local copies, waits for them, and re-layouts: 216 us -> 151 us
  starting transfers between devices: 213 us -> 173 us
  blocking collectives: 27.7 us -> 0 us
  matrix products: 82 us -> 59.4 us
    pallas_call x0 -> x16, Pallas kernels: none -> 78.7 us  [the longest x3 29.6 us: project(): pl.pallas_call(project_kernel, grid=(4,), out_shape=[jax.ShapeDtypeStruct...]
    ppermute x136 -> x106, starting transfers between devices: 169 us -> 124 us  [exchange(): return lambda v: lax.ppermute(v, axes, pairs)]
    optimization_barrier x24 -> x0, local copies, waits for them, and re-layouts: 34.2 us -> none  [cube_gather(): lax.optimization_barrier(tuple((CUBE[(i + step) % 4](parts[i]) for i in r...]
    add x60 -> x15, other arithmetic: 41.9 us -> 7.83 us  [the longest x12 7.74 us: cube_scatter(): a.astype(F32) + b.astype(F32)]
    all_to_all x4 -> x7, waiting for transfers between devices: 14 us -> 47.1 us  [the longest x1 13.9 us: per_device(): lax.all_to_all(swap_cores(second_pack), 'z', split_axis=0, concat_axis=0,...]
    slice x57 -> x4, local copies, waits for them, and re-layouts: 35.1 us -> 3.47 us  [the longest x1 1.76 us: per_device(): inner = token_sums([inner[:, 0], inner[:, 1]], place_of) * rates ** 3 / 2048]
    unnamed x373 -> x303, local copies, waits for them, and re-layouts: 47.3 us -> 72.2 us
    dot_general x19 -> x10, matrix products: 82 us -> 57.3 us  [dot(): lax.dot_general(a, b, (((left,), (right,)), ((), ())), preferred_element_...]
  transfers between devices with their start and end apart: 154 -> 120, of which waited for: 62 -> 41; matrix products, arithmetic and copies ran while one was open for 38% -> 36% of each run, Pallas kernels for 0% -> 7%
where the time goes in v1:
time: 795 us; the launch traced here: 780 us
  waiting for transfers between devices  174 us (22%)
  starting transfers between devices  173 us (22%)
  local copies, waits for them, and re-layouts  151 us (19%)
  other arithmetic  128 us (16%)
  Pallas kernels  78.7 us (10%)
  matrix products  59.4 us (7%)
  between operations  16.1 us (2%)
    ppermute x106, waiting for transfers between devices, exchange(): return lambda v: lax.ppermute(v, axes, pairs)  127 us
    ppermute x106, starting transfers between devices, exchange(): return lambda v: lax.ppermute(v, axes, pairs)  124 us
    unnamed x303, local copies, waits for them, and re-layouts  72.2 us
    dot_general x10, matrix products, dot(): lax.dot_general(a, b, (((left,), (right,)), ((), ())), preferred_element_...  57.3 us
    pallas_call x3, Pallas kernels, project(): pl.pallas_call(project_kernel, grid=(4,), out_shape=[jax.ShapeDtypeStruct...  29.6 us
    pallas_call x9, Pallas kernels, cube_scatter(): folded = kernel_call(fold_kernel, [half] * 8, [VMEM] * 8)(*kept, *arrived)  24.6 us
    concatenate x36, other arithmetic, cube_gather(): parts = [jnp.concatenate([a, b], axis=0) for a, b in zip(parts, arrived)]  22.4 us
    ppermute x4, starting transfers between devices, lax.ppermute(v, SWAP, [(0, 0), (1, 2), (2, 1), (3, 3)])  15.9 us
  transfers between devices with their start and end apart: 120, of which 41 were waited for; matrix products, arithmetic and copies ran while one was open for 36% of the time, Pallas kernels for 7%

profile of v1, /device:TPU:0, one launch (start us, length us, event | category | flops | bytes accessed | tf_op | source)
XLA Modules:
  0.0 780.4 jit_solution(17984942661290819531)
XLA Ops:
  45.8 12.5 %collective-permute-done.1 = bf16[32,2048]{1,0:T(8,128)(2,1)S(1)} collective-permute-done((bf16[32,2048]{1,0:T(8,128)(2,1)S(1)}, bf16[32,2048]{1,0:T(8,128)(2,1)S(1)}, u32[]{:S(2)}, u32[]{:S(2)}) %collective-permute-start.1) | collective-permute-done | bytes 131104 | tf_op jit(solution)/shard_map/ppermute | solution.py:27
  85.5 13.9 %all-to-all-done.2 = bf16[4,64,1920]{2,1,0:T(8,128)(2,1)S(1)} async-done(((bf16[4,64,1920]{2,1,0:T(8,128)(2,1)}), bf16[4,64,1920]{2,1,0:T(8,128)(2,1)S(1)}, u32[]{:S(2)}, u32[]{:S(2)}) %all-to-all-start.2) | async-done | bytes 983072 | tf_op jit(solution)/shard_map/all_to_all | solution.py:287
  111.5 12.3 %all-to-all-done = bf16[16,64,640]{2,1,0:T(8,128)(2,1)S(1)} async-done(((bf16[16,64,640]{2,1,0:T(8,128)(2,1)}), bf16[16,64,640]{2,1,0:T(8,128)(2,1)S(1)}, u32[]{:S(2)}, u32[]{:S(2)}) %all-to-all-start) | async-done | bytes 1310752 | tf_op jit(solution)/shard_map/all_to_all | solution.py:279
  136.6 5.2 fusion.13.qkv
  146.4 4.9 all-to-all-start.1
  152.1 7.1 all-to-all-done.1
  166.0 6.5 shard_map.263
  186.4 5.2 collective-permute-done.18.refs_4_
  217.4 7.2 collective-permute-done.28.refs_6_
  233.2 5.2 collective-permute-done.32
  275.3 5.1 collective-permute-done.41
  294.0 7.5 collective-permute-done.39
  316.9 10.0 %collective-permute-done.46 = bf16[128,2048]{1,0:T(8,128)(2,1)} collective-permute-done((bf16[128,2048]{1,0:T(8,128)(2,1)}, bf16[128,2048]{1,0:T(8,128)(2,1)}, u32[]{:S(2)}, u32[]{:S(2)}) %collective-permute-start.46) | collective-permute-done | bytes 524320 | tf_op jit(solution)/shard_map/ppermute | solution.py:27
  338.3 5.4 shard_map.268
  349.6 5.6 fusion.63
  360.1 8.8 %convert_multiply_fusion.2 = (f32[1024,640]{1,0:T(8,128)}, bf16[1024,640]{1,0:T(8,128)(2,1)}, f32[1024,640]{1,0:T(8,128)}) fusion(f32[1024,1280]{1,0:T(8,128)S(1)} %fusion.63, bf16[1024,2048]{1,0:T(8,128)(2,1)} %get-tuple-element.156, bf16[1024,1920]{1,0:T(8,128)(2,1)} %collective-permute-done.51, bf16[1024,1920]{1,0:T(8,128)(2,1)S(1)} %bitcast.193), kind=kOutput, calls=%fused_computation.31 | convolution fusion | flops 2694840320 | bytes 23855104 | tf_op jit(solution)/shard_map/dot_general | solution.py:41
  381.0 6.1 multiply_convert_fusion.1
  392.3 18.4 %shard_map.270 = (bf16[128,2048]{1,0:T(8,128)(2,1)}, bf16[128,2048]{1,0:T(8,128)(2,1)}, bf16[128,2048]{1,0:T(8,128)(2,1)}, bf16[128,2048]{1,0:T(8,128)(2,1)}, bf...) custom-call(bf16[1024,1408]{1,0:T(8,128)(2,1)} %fusion.8.rows_ref, ...), custom_call_target="tpu_custom_call" | custom-call | flops 5905580032 | bytes 12845056 | tf_op jit(solution)/shard_map/pallas_call | solution.py:72
  415.4 7.2 convolution_convert_fusion.1
  422.6 5.4 all-to-all-start.3
  439.0 8.9 %convolution_convert_fusion = bf16[2048,1408]{0,1:T(8,128)(2,1)S(1)} fusion(bf16[1024,2048]{1,0:T(8,128)(2,1)} %constant_dynamic-update-slice_fusion.20, bf16[1024,10]{1,0:T(8,128)(2,1)S(1)} %copy-done.36, bf16[1024,640]{1,0:T(8,128)(2,1)} %copy-done.12, bf16[1024,640]{1,0:T(8,128)(2,1)} %copy-done.11), kind=kOutput, calls=%fused_computation.13 | convolution fusion | flops 5919997952 | bytes 12603392 | tf_op jit(solution)/shard_map/dot_general | solution.py:41
  447.9 27.8 %collective-permute-done.58.refs_4_ = bf16[64,2048]{1,0:T(8,128)(2,1)} collective-permute-done((bf16[64,2048]{1,0:T(8,128)(2,1)}, bf16[64,2048]{1,0:T(8,128)(2,1)}, u32[]{:S(2)}, u32[]{:S(2)}) %collective-permute-start.58) | collective-permute-done | bytes 262176 | tf_op jit(solution)/shard_map/ppermute | solution.py:27
  475.7 6.0 collective-permute-done.59.refs_5_
  491.9 6.6 convolution_convert_fusion.2
  551.7 4.9 add_convert_fusion
  556.5 6.5 copy.557
  580.6 6.6 collective-permute-done.82
  595.0 9.1 %shard_map.274 = (f32[1024,128]{1,0:T(8,128)}, f32[1024,128]{1,0:T(8,128)}, bf16[1024,128]{1,0:T(8,128)(2,1)}, f32[1024,2]{1,0:T(8,128)}, f32[2,128]{1,0:T(2,128...) custom-call(f32[1024,384]{1,0:T(8,128)} %copy-done.5, f32[1024,2]{1,0:T(8,128)} %bitcast.182, f32[2,128]{1,0:T(2,128)} %reshape.661.gains, ...), custom_call_target="tpu_custom_call" | custom-call | flops 1342177280 | bytes 6291456 | tf_op jit(solution)/shard_map/pallas_call | solution.py:424
  608.9 5.6 all-to-all-start.4
  632.8 6.5 shard_map.275
  717.6 9.5 %collective-permute-start.105 = (bf16[4,64,2048]{2,1,0:T(8,128)(2,1)}, bf16[4,64,2048]{2,1,0:T(8,128)(2,1)}, u32[]{:S(2)}, u32[]{:S(2)}) collective-permute-start(bf16[4,64,2048]{2,1,0:T(8,128)(2,1)} %bitcast.220), channel_id=1, source_target_pairs={{0,0},{1,4},{4,1},{5,5},{2,2},{3,6},{6,3},{7,7},{8,8},{9,12},{12,9... | collective-permute-start | bytes 3145736 | tf_op jit(solution)/shard_map/ppermute | solution.py:31
  741.3 10.9 %all-to-all-done.5 = bf16[4,64,2048]{2,1,0:T(8,128)(2,1)S(1)} async-done(((bf16[4,64,2048]{2,1,0:T(8,128)(2,1)}), bf16[4,64,2048]{2,1,0:T(8,128)(2,1)S(1)}, u32[]{:S(2)}, u32[]{:S(2)}) %all-to-all-start.5) | async-done | bytes 1048608 | tf_op jit(solution)/shard_map/all_to_all | solution.py:410
  (777 shorter events, 495.8 us)
Async XLA Ops:
  15.3 49.7 %collective-permute-start.16 = (bf16[4,64,640]{2,0,1:T(4,128)(2,1)}, bf16[4,64,640]{2,0,1:T(4,128)(2,1)}, u32[]{:S(2)}, u32[]{:S(2)}) collective-permute-start(bf16[4,64,640]{2,0,1:T(4,128)(2,1)} %concatenate.299), channel_id=1, source_target_pairs={{0,0},{1,4},{4,1},{5,5},{2,2},{3,6},{6,3},{7,7},{8,8},{9,12},{12,9... | collective-permute-start | bytes 983048 | tf_op jit(solution)/shard_map/ppermute | solution.py:31
  22.1 19.3 %collective-permute-start = (bf16[16,2048]{1,0:T(8,128)(2,1)S(1)}, bf16[16,2048]{1,0:T(8,128)(2,1)S(1)}, u32[]{:S(2)}, u32[]{:S(2)}) collective-permute-start(bf16[16,2048]{1,0:T(8,128)(2,1)S(1)} %slice.172), channel_id=1, source_target_pairs={{0,8},{8,0},{16,24},{24,16},{1,9},{9,1},{17,25},{25,17},{2,10},{10... | collective-permute-start | bytes 196616 | tf_op jit(solution)/shard_map/ppermute | solution.py:27
  41.4 35.7 %collective-permute-start.50 = (bf16[4,64,1920]{2,0,1:T(4,128)(2,1)}, bf16[4,64,1920]{2,0,1:T(4,128)(2,1)S(1)}, u32[]{:S(2)}, u32[]{:S(2)}) collective-permute-start(bf16[4,64,1920]{2,0,1:T(4,128)(2,1)} %pad_maximum_fusion.3), channel_id=1, source_target_pairs={{0,0},{1,4},{4,1},{5,5},{2,2},{3,6},{6,3},{7,7},{8,8},{9,12},{12,9... | collective-permute-start | bytes 2949128 | tf_op jit(solution)/shard_map/ppermute | solution.py:31
  68.0 55.8 %collective-permute-start.12 = (bf16[128,2048]{1,0:T(8,128)(2,1)}, bf16[128,2048]{1,0:T(8,128)(2,1)}, u32[]{:S(2)}, u32[]{:S(2)}) collective-permute-start(bf16[128,2048]{1,0:T(8,128)(2,1)} %pad_maximum_fusion.6), channel_id=1, source_target_pairs={{0,6},{2,4},{4,2},{6,0},{1,7},{3,5},{5,3},{7,1},{8,14},{10,12},{12... | collective-permute-start | bytes 1572872 | tf_op jit(solution)/shard_map/ppermute | solution.py:27
  70.8 54.9 %collective-permute-start.13 = (bf16[128,2048]{1,0:T(8,128)(2,1)}, bf16[128,2048]{1,0:T(8,128)(2,1)}, u32[]{:S(2)}, u32[]{:S(2)}) collective-permute-start(bf16[128,2048]{1,0:T(8,128)(2,1)} %pad_maximum_fusion.7), channel_id=1, source_target_pairs={{0,8},{8,0},{16,24},{24,16},{1,9},{9,1},{17,25},{25,17},{2,10},{10... | collective-permute-start | bytes 1572872 | tf_op jit(solution)/shard_map/ppermute | solution.py:27
  71.7 55.8 %collective-permute-start.14 = (bf16[128,2048]{1,0:T(8,128)(2,1)}, bf16[128,2048]{1,0:T(8,128)(2,1)}, u32[]{:S(2)}, u32[]{:S(2)}) collective-permute-start(bf16[128,2048]{1,0:T(8,128)(2,1)} %pad_maximum_fusion.8), channel_id=1, source_target_pairs={{0,4},{2,6},{4,0},{6,2},{1,5},{3,7},{5,1},{7,3},{8,12},{10,14},{12... | collective-permute-start | bytes 1572872 | tf_op jit(solution)/shard_map/ppermute | solution.py:27
  74.4 55.1 %collective-permute-start.15 = (bf16[128,2048]{1,0:T(8,128)(2,1)}, bf16[128,2048]{1,0:T(8,128)(2,1)}, u32[]{:S(2)}, u32[]{:S(2)}) collective-permute-start(bf16[128,2048]{1,0:T(8,128)(2,1)} %pad_maximum_fusion.9), channel_id=1, source_target_pairs={{0,24},{8,16},{16,8},{24,0},{1,25},{9,17},{17,9},{25,1},{2,26},{10... | collective-permute-start | bytes 1572872 | tf_op jit(solution)/shard_map/ppermute | solution.py:27
  78.1 21.3 %all-to-all-start.2 = ((bf16[4,64,1920]{2,1,0:T(8,128)(2,1)}), bf16[4,64,1920]{2,1,0:T(8,128)(2,1)S(1)}, u32[]{:S(2)}, u32[]{:S(2)}) async-start(bf16[4,64,1920]{2,1,0:T(8,128)(2,1)} %copy.514), calls=%async_computation.2 | async-start | bytes 1966080 | tf_op jit(solution)/shard_map/all_to_all | solution.py:287
  100.7 23.0 %all-to-all-start = ((bf16[16,64,640]{2,1,0:T(8,128)(2,1)}), bf16[16,64,640]{2,1,0:T(8,128)(2,1)S(1)}, u32[]{:S(2)}, u32[]{:S(2)}) async-start(bf16[16,64,640]{2,1,0:T(8,128)(2,1)} %bitcast.8), calls=%async_computation | async-start | bytes 2621440 | tf_op jit(solution)/shard_map/all_to_all | solution.py:279
  105.5 205.2 %all-gather.6.cloned.1.call-start = ((), (), s32[]{:S(2)}) async-start(), calls=%async_computation.10 | async-start | bytes 4915200 | tf_op jit(solution)/shard_map/all_gather | solution.py:290
  151.2 187.1 %all-gather.4.cloned.1.call-start = ((), (), s32[]{:S(2)}) async-start(), calls=%async_computation.8 | async-start | bytes 4734976 | tf_op jit(solution)/shard_map/all_gather | solution.py:324
  282.2 19.3 %collective-permute-start.39 = (bf16[64,2048]{1,0:T(8,128)(2,1)S(1)}, bf16[64,2048]{1,0:T(8,128)(2,1)S(1)}, u32[]{:S(2)}, u32[]{:S(2)}) collective-permute-start(bf16[64,2048]{1,0:T(8,128)(2,1)S(1)} %pad_maximum_fusion.25), channel_id=1, source_target_pairs={{0,6},{2,4},{4,2},{6,0},{1,7},{3,5},{5,3},{7,1},{8,14},{10,12},{12... | collective-permute-start | bytes 786440 | tf_op jit(solution)/shard_map/ppermute | solution.py:27
  284.7 20.8 %collective-permute-start.36 = (bf16[64,2048]{1,0:T(8,128)(2,1)S(1)}, bf16[64,2048]{1,0:T(8,128)(2,1)S(1)}, u32[]{:S(2)}, u32[]{:S(2)}) collective-permute-start(bf16[64,2048]{1,0:T(8,128)(2,1)S(1)} %pad_maximum_fusion.24), channel_id=1, source_target_pairs={{0,24},{8,16},{16,8},{24,0},{1,25},{9,17},{17,9},{25,1},{2,26},{10... | collective-permute-start | bytes 786440 | tf_op jit(solution)/shard_map/ppermute | solution.py:27
  289.4 41.3 %collective-permute-start.48 = (bf16[128,2048]{1,0:T(8,128)(2,1)}, bf16[128,2048]{1,0:T(8,128)(2,1)}, u32[]{:S(2)}, u32[]{:S(2)}) collective-permute-start(bf16[128,2048]{1,0:T(8,128)(2,1)} %pad_maximum_fusion.14), channel_id=1, source_target_pairs={{0,4},{2,6},{4,0},{6,2},{1,5},{3,7},{5,1},{7,3},{8,12},{10,14},{12... | collective-permute-start | bytes 1572872 | tf_op jit(solution)/shard_map/ppermute | solution.py:27
  291.1 41.5 %collective-permute-start.49 = (bf16[128,2048]{1,0:T(8,128)(2,1)}, bf16[128,2048]{1,0:T(8,128)(2,1)}, u32[]{:S(2)}, u32[]{:S(2)}) collective-permute-start(bf16[128,2048]{1,0:T(8,128)(2,1)} %pad_maximum_fusion.15), channel_id=1, source_target_pairs={{0,24},{8,16},{16,8},{24,0},{1,25},{9,17},{17,9},{25,1},{2,26},{10... | collective-permute-start | bytes 1572872 | tf_op jit(solution)/shard_map/ppermute | solution.py:27
  303.2 25.5 %collective-permute-start.47 = (bf16[128,2048]{1,0:T(8,128)(2,1)}, bf16[128,2048]{1,0:T(8,128)(2,1)}, u32[]{:S(2)}, u32[]{:S(2)}) collective-permute-start(bf16[128,2048]{1,0:T(8,128)(2,1)} %pad_maximum_fusion.13), channel_id=1, source_target_pairs={{0,8},{8,0},{16,24},{24,16},{1,9},{9,1},{17,25},{25,17},{2,10},{10... | collective-permute-start | bytes 1572872 | tf_op jit(solution)/shard_map/ppermute | solution.py:27
  307.3 19.6 %collective-permute-start.46 = (bf16[128,2048]{1,0:T(8,128)(2,1)}, bf16[128,2048]{1,0:T(8,128)(2,1)}, u32[]{:S(2)}, u32[]{:S(2)}) collective-permute-start(bf16[128,2048]{1,0:T(8,128)(2,1)} %pad_maximum_fusion.12), channel_id=1, source_target_pairs={{0,6},{2,4},{4,2},{6,0},{1,7},{3,5},{5,3},{7,1},{8,14},{10,12},{12... | collective-permute-start | bytes 1572872 | tf_op jit(solution)/shard_map/ppermute | solution.py:27
  310.7 35.2 %collective-permute-start.51 = (bf16[1024,1920]{1,0:T(8,128)(2,1)}, bf16[1024,1920]{1,0:T(8,128)(2,1)}, u32[]{:S(2)}, u32[]{:S(2)}) collective-permute-start(bf16[1024,1920]{1,0:T(8,128)(2,1)} %bitcast.191), channel_id=1, source_target_pairs={{0,1},{1,0},{2,3},{3,2},{4,5},{5,4},{6,7},{7,6},{8,9},{9,8},{10,11... | collective-permute-start | bytes 11796488 | tf_op jit(solution)/shard_map/ppermute | solution.py:27
  422.6 96.1 %all-to-all-start.3 = ((bf16[16,64,2048]{2,1,0:T(8,128)(2,1)}), bf16[16,64,2048]{2,1,0:T(8,128)(2,1)}, u32[]{:S(2)}, u32[]{:S(2)}) async-start(bf16[16,64,2048]{2,1,0:T(8,128)(2,1)} %bitcast.190), calls=%async_computation.3 | async-start | bytes 8388608 | tf_op jit(solution)/shard_map/all_to_all | solution.py:380
  428.0 289.6 %reduce-scatter.2.cloned.1.call-start = ((), (), s32[]{:S(2)}) async-start(), calls=%async_computation.9 | async-start | bytes 5242880 | tf_op jit(solution)/shard_map/reduce_scatter | solution.py:407
  432.7 43.0 %collective-permute-start.58 = (bf16[64,2048]{1,0:T(8,128)(2,1)}, bf16[64,2048]{1,0:T(8,128)(2,1)}, u32[]{:S(2)}, u32[]{:S(2)}) collective-permute-start(bf16[64,2048]{1,0:T(8,128)(2,1)} %get-tuple-element.169), channel_id=1, source_target_pairs={{0,24},{8,16},{16,8},{24,0},{1,25},{9,17},{17,9},{25,1},{2,26},{10... | collective-permute-start | bytes 786440 | tf_op jit(solution)/shard_map/ppermute | solution.py:27
  435.8 46.0 %collective-permute-start.59 = (bf16[64,2048]{1,0:T(8,128)(2,1)}, bf16[64,2048]{1,0:T(8,128)(2,1)}, u32[]{:S(2)}, u32[]{:S(2)}) collective-permute-start(bf16[64,2048]{1,0:T(8,128)(2,1)} %get-tuple-element.170), channel_id=1, source_target_pairs={{0,6},{2,4},{4,2},{6,0},{1,7},{3,5},{5,3},{7,1},{8,14},{10,12},{12... | collective-permute-start | bytes 786440 | tf_op jit(solution)/shard_map/ppermute | solution.py:27
  438.5 43.3 %collective-permute-start.60 = (bf16[64,2048]{1,0:T(8,128)(2,1)}, bf16[64,2048]{1,0:T(8,128)(2,1)}, u32[]{:S(2)}, u32[]{:S(2)}) collective-permute-start(bf16[64,2048]{1,0:T(8,128)(2,1)} %get-tuple-element.171), channel_id=1, source_target_pairs={{0,8},{8,0},{16,24},{24,16},{1,9},{9,1},{17,25},{25,17},{2,10},{10... | collective-permute-start | bytes 786440 | tf_op jit(solution)/shard_map/ppermute | solution.py:27
  438.7 43.1 %collective-permute-start.61 = (bf16[64,2048]{1,0:T(8,128)(2,1)}, bf16[64,2048]{1,0:T(8,128)(2,1)}, u32[]{:S(2)}, u32[]{:S(2)}) collective-permute-start(bf16[64,2048]{1,0:T(8,128)(2,1)} %get-tuple-element.172), channel_id=1, source_target_pairs={{0,4},{2,6},{4,0},{6,2},{1,5},{3,7},{5,1},{7,3},{8,12},{10,14},{12... | collective-permute-start | bytes 786440 | tf_op jit(solution)/shard_map/ppermute | solution.py:27
  506.9 44.8 %collective-permute-start.104 = (bf16[1024,2048]{0,1:T(8,128)(2,1)}, bf16[1024,2048]{0,1:T(8,128)(2,1)}, u32[]{:S(2)}, u32[]{:S(2)}) collective-permute-start(bf16[1024,2048]{0,1:T(8,128)(2,1)} %pad_maximum_fusion), channel_id=1, source_target_pairs={{0,1},{1,0},{2,3},{3,2},{4,5},{5,4},{6,7},{7,6},{8,9},{9,8},{10,11... | collective-permute-start | bytes 12582920 | tf_op jit(solution)/shard_map/ppermute | solution.py:27
  543.9 29.5 %collective-permute-start.81 = (bf16[64,2048]{1,0:T(8,128)(2,1)}, bf16[64,2048]{1,0:T(8,128)(2,1)S(1)}, u32[]{:S(2)}, u32[]{:S(2)}) collective-permute-start(bf16[64,2048]{1,0:T(8,128)(2,1)} %pad_maximum_fusion.31), channel_id=1, source_target_pairs={{0,4},{2,6},{4,0},{6,2},{1,5},{3,7},{5,1},{7,3},{8,12},{10,14},{12... | collective-permute-start | bytes 786440 | tf_op jit(solution)/shard_map/ppermute | solution.py:27
  546.1 22.1 %collective-permute-start.78 = (bf16[64,2048]{1,0:T(8,128)(2,1)}, bf16[64,2048]{1,0:T(8,128)(2,1)}, u32[]{:S(2)}, u32[]{:S(2)}) collective-permute-start(bf16[64,2048]{1,0:T(8,128)(2,1)} %pad_maximum_fusion.30), channel_id=1, source_target_pairs={{0,8},{8,0},{16,24},{24,16},{1,9},{9,1},{17,25},{25,17},{2,10},{10... | collective-permute-start | bytes 786440 | tf_op jit(solution)/shard_map/ppermute | solution.py:27
  569.2 19.8 %collective-permute-start.84 = (bf16[128,2048]{1,0:T(8,128)(2,1)S(1)}, bf16[128,2048]{1,0:T(8,128)(2,1)S(1)}, u32[]{:S(2)}, u32[]{:S(2)}) collective-permute-start(bf16[128,2048]{1,0:T(8,128)(2,1)S(1)} %pad_maximum_fusion.18), channel_id=1, source_target_pairs={{0,4},{2,6},{4,0},{6,2},{1,5},{3,7},{5,1},{7,3},{8,12},{10,14},{12... | collective-permute-start | bytes 1572872 | tf_op jit(solution)/shard_map/ppermute | solution.py:27
  616.3 27.5 %collective-permute-start.52 = (bf16[64,2048]{1,0:T(8,128)(2,1)}, bf16[64,2048]{1,0:T(8,128)(2,1)}, u32[]{:S(2)}, u32[]{:S(2)}) collective-permute-start(bf16[64,2048]{1,0:T(8,128)(2,1)} %reshape.648), channel_id=1, source_target_pairs={{0,2},{2,0},{1,3},{3,1},{4,6},{6,4},{5,7},{7,5},{8,10},{10,8},{9,1... | collective-permute-start | bytes 786440 | tf_op jit(solution)/shard_map/ppermute | solution.py:27
  645.8 82.5 %collective-permute-start.53 = (bf16[128,2048]{1,0:T(8,128)(2,1)}, bf16[128,2048]{1,0:T(8,128)(2,1)}, u32[]{:S(2)}, u32[]{:S(2)}) collective-permute-start(bf16[128,2048]{1,0:T(8,128)(2,1)} %maximum_select_fusion.3), channel_id=1, source_target_pairs={{0,1},{1,0},{2,3},{3,2},{4,5},{5,4},{6,7},{7,6},{8,9},{9,8},{10,11... | collective-permute-start | bytes 1572872 | tf_op jit(solution)/shard_map/ppermute | solution.py:27
  706.1 25.0 %all-to-all-start.6 = ((bf16[16,64,640]{2,1,0:T(8,128)(2,1)}), bf16[16,64,640]{2,1,0:T(8,128)(2,1)S(1)}, u32[]{:S(2)}, u32[]{:S(2)}) async-start(bf16[16,64,640]{2,1,0:T(8,128)(2,1)} %bitcast.46), calls=%async_computation.7 | async-start | bytes 2621440 | tf_op jit(solution)/shard_map/all_to_all | solution.py:444
  733.0 28.4 %collective-permute-start.103 = (bf16[128,2048]{1,0:T(8,128)(2,1)}, bf16[128,2048]{1,0:T(8,128)(2,1)}, u32[]{:S(2)}, u32[]{:S(2)}) collective-permute-start(bf16[128,2048]{1,0:T(8,128)(2,1)} %maximum_select_fusion.5), channel_id=1, source_target_pairs={{0,1},{1,0},{2,3},{3,2},{4,5},{5,4},{6,7},{7,6},{8,9},{9,8},{10,11... | collective-permute-start | bytes 1572872 | tf_op jit(solution)/shard_map/ppermute | solution.py:27
  (206 other events, 2349.3 us)
Sparse Core Ops, SparseCore 0:
  108.5 47.1 all-gather.5
  202.1 122.2 all-gather.3
  563.2 45.1 reduce-scatter.1

commit v2 on v0

v2 whole, which is shorter than its diff:
```python
import math

import jax
import jax.numpy as jnp
from jax import lax
from jax.experimental import pallas as pl
from jax.experimental.pallas import tpu as pltpu
from jax.sharding import Mesh
from jax.sharding import PartitionSpec as P

EPSILON = 1e-05
ROPE_BASE = 10000.0
SCALE = 128 ** (-0.5)
BF = jnp.bfloat16
F32 = jnp.float32
HIGHEST = lax.Precision.HIGHEST

AXES = ("x", "z", "yl", "yh", "c")
SIZES = (4, 4, 2, 2, 2)
CONTEXT = ("z", "yl")
TENSOR = ("yh", "c")
WEIGHT = ("x", "z", "yl")
GROUP = ("z", "yl", "yh")
Y = ("yl", "yh")
SWAP = ("yl", "c")
VMEM = pl.BlockSpec(memory_space=pltpu.VMEM)
SMEM = pl.BlockSpec(memory_space=pltpu.SMEM)
MIB = 1024 * 1024


def exchange(axes, size, mask):
    pairs = [(at, at ^ mask) for at in range(size)]
    return lambda v: lax.ppermute(v, axes, pairs)


CUBE = (exchange("z", 4, 1), exchange(Y, 4, 2), exchange("z", 4, 3), exchange(Y, 4, 3))
swap_cores = lambda v: lax.ppermute(v, SWAP, [(0, 0), (1, 2), (2, 1), (3, 3)])
other_core = exchange("c", 2, 1)
other_half = exchange("yh", 2, 1)


def dot(a, b, left=1, right=0, precision=None):
    return lax.dot_general(
        a, b, (((left,), (right,)), ((), ())), preferred_element_type=F32, precision=precision
    )


def all_to_all(v, axes):
    return lax.all_to_all(v, axes, split_axis=0, concat_axis=0, tiled=True)


def kernel_call(body, outs, in_specs, limit, flops=0, scratch=()):
    return pl.pallas_call(
        body,
        out_shape=[jax.ShapeDtypeStruct(shape, kind) for shape, kind in outs],
        in_specs=in_specs,
        out_specs=[VMEM] * len(outs),
        scratch_shapes=list(scratch),
        compiler_params=pltpu.CompilerParams(vmem_limit_bytes=limit * MIB),
        cost_estimate=pl.CostEstimate(flops=flops, bytes_accessed=4 * MIB, transcendentals=0),
    )


PIECE = ((128, 2048), BF)
HEAD = ((1024, 128), BF)
WIDE_HEAD = ((1024, 128), F32)


def rows_at(places, at):
    return pl.ds(pl.multiple_of(places[at] * 16, 16), 16)


def join_kernel(*refs):
    half = refs[0].shape[0]
    for i in range(4):
        refs[8 + i][:half, :] = refs[i][...]
        refs[8 + i][half:, :] = refs[4 + i][...]


def cube_gather(parts):
    parts = list(parts)
    for step in range(4):
        arrived = [CUBE[(i + step) % 4](parts[i]) for i in range(4)]
        if step < 3:
            rows = 2 * parts[0].shape[0]
            parts = kernel_call(join_kernel, [((rows, 2048), BF)] * 4, [VMEM] * 8, 8)(
                *parts, *arrived
            )
    return list(parts) + arrived


def fold_kernel(*refs):
    half = refs[0].shape[0] // 2
    for i in range(4):
        kept, arrived, keep, send = refs[i], refs[4 + i], refs[8 + i], refs[12 + i]
        keep[...] = (kept[:half, :].astype(F32) + arrived[:half, :].astype(F32)).astype(BF)
        send[...] = (kept[half:, :].astype(F32) + arrived[half:, :].astype(F32)).astype(BF)


def cube_scatter(pieces):
    kept, sent = pieces[:4], pieces[4:]
    for step in (3, 2, 1, 0):
        arrived = [CUBE[(i + step) % 4](sent[i]) for i in range(4)]
        if step:
            half = ((kept[0].shape[0] // 2, 2048), BF)
            folded = kernel_call(fold_kernel, [half] * 8, [VMEM] * 8, 10)(*kept, *arrived)
            kept, sent = folded[:4], folded[4:]
    return list(kept) + arrived


def block_places():
    at = jnp.arange(64, dtype=jnp.int32)
    part, block = (at >> 3) & 3, (at & 7) | ((at >> 5) << 3)
    turned = [(block >> ((dim - part) & 3)) & 1 for dim in range(4)]
    z = lax.axis_index("z") ^ (turned[0] ^ (3 * turned[2]))
    y = (2 * lax.axis_index("yh") + lax.axis_index("yl")) ^ (turned[1] ^ (3 * turned[3]))
    return ((2 * z + (y & 1)) * 2 + (y >> 1)) * 4 + part


def put_pieces(places, pieces, out):
    for k, piece in enumerate(pieces):
        for j in range(8):
            out[rows_at(places, 8 * k + j), :] = piece[16 * j : 16 * j + 16, :]


def take_rows(places, source, out):
    for n in range(64):
        out[16 * n : 16 * n + 16, :] = source[rows_at(places, n), :]


def project(rows, near, far, columns, pieces):
    for b in range(4):
        held = rows[256 * b : 256 * b + 256, :]
        for at, weight in enumerate((near, far)):
            wide = dot(held, weight[:, columns], 1, 1).astype(BF)
            for k in range(2):
                pieces[2 * b + k][:, 1024 * at : 1024 * at + 1024] = wide[128 * k : 128 * k + 128]


def row_sums(v):
    return dot(jnp.ones((8, 128), F32), v, 1, 1, HIGHEST)[0:1]


def enter_kernel(places, *refs):
    pieces, (gain, near, far, normed, qkv, stats) = refs[:8], refs[8:]
    for k in range(8):

        def norm_rows(j, _):
            held = pieces[k][pl.ds(pl.multiple_of(j * 16, 16), 16), :].astype(F32)
            rate = lax.rsqrt(jnp.mean(held * held, axis=1, keepdims=True) + EPSILON)
            normed[rows_at(places, 8 * k + j), :] = (held * rate * gain[...]).astype(BF)
            return 0

        lax.fori_loop(0, 8, norm_rows, 0)
    for b in range(4):
        rows = slice(256 * b, 256 * b + 256)
        held = dot(normed[rows, :1024], near[:, :384]) + dot(normed[rows, 1024:], far[:, :384])
        qkv[rows, :] = held
        stats[0:1, rows] = row_sums(held[:, :128] * held[:, :128])
        stats[1:2, rows] = row_sums(held[:, 128:256] * held[:, 128:256])


def allowed_block(length, at):
    q_pos = 256 * at + lax.broadcasted_iota(jnp.int32, (256, 256 * at + 256), 0)
    k_pos = lax.broadcasted_iota(jnp.int32, (256, 256 * at + 256), 1)
    return jnp.logical_and(k_pos <= q_pos, k_pos < length[0])


def forward_kernel(
    places, length, qkv, rates, gains, cosine, sine, near, far,
    queries, keys, values, attended, log_total, *rest,
):
    pieces, ordered = rest[:8], rest[8]

    def turn(held):
        return held * cosine[...] + pltpu.roll(held, 64, 1) * sine[...]

    queries[...] = turn(qkv[:, :128] * rates[:, 0:1] * gains[0:1, :]).astype(BF)
    keys[...] = turn(qkv[:, 128:256] * rates[:, 1:2] * gains[1:2, :]).astype(BF)
    values[...] = qkv[:, 256:].astype(BF)
    for at in range(4):
        rows, upto = slice(256 * at, 256 * at + 256), slice(0, 256 * at + 256)
        scores = dot(queries[rows, :], keys[upto, :], 1, 1) * SCALE
        scores = jnp.where(allowed_block(length, at), scores, -1e30)
        peak = jnp.max(scores, axis=1, keepdims=True)
        raised = jnp.exp(scores - peak)
        total = jnp.sum(raised, axis=1, keepdims=True)
        probs = (raised * (1.0 / total)).astype(BF)
        attended[rows, :] = dot(probs, values[upto, :]).astype(BF)
        log_total[rows, :] = peak + jnp.log(total)
    take_rows(places, attended, ordered)
    project(ordered, near, far, slice(512, 640), pieces)


def middle_kernel(*refs):
    terms, (own, gain, middle), outs = refs[:8], refs[8:11], refs[11:]
    for i in range(4):
        rows = slice(16 * i, 16 * i + 16)
        held = own[rows, :].astype(F32) + (terms[i][...].astype(F32) + terms[4 + i][...].astype(F32))
        middle[rows, :] = held
        rate = lax.rsqrt(jnp.mean(held * held, axis=1, keepdims=True) + EPSILON)
        outs[i][...] = (held * rate * gain[...]).astype(BF)


def mixture_kernel(places, length, *refs):
    pieces, (routed, near, far, spread), refs = refs[:8], refs[8:12], refs[12:]
    (mixed, grad_out, gated, hidden_grad), outs, ordered = refs[:4], refs[4:12], refs[12]
    put_pieces(places, pieces, mixed)
    lane = lax.broadcasted_iota(jnp.int32, (256, 128), 1)

    def block(b, _):
        rows = pl.ds(pl.multiple_of(b * 256, 256), 256)
        inside = b * 256 + lax.broadcasted_iota(jnp.int32, (256, 1), 0) < length[0]
        grad_out[rows, :] = jnp.where(inside, routed[rows, :2048], jnp.zeros((), BF))
        chosen = routed[rows, 2048:].astype(F32)
        hidden = dot(mixed[rows, :1024], near[:, :1408]) + dot(mixed[rows, 1024:], far[:, :1408])
        out_grad = dot(grad_out[rows, :1024], near[:, 1408:]) + dot(
            grad_out[rows, 1024:], far[:, 1408:]
        )
        gate_h, up_h = hidden[:, :640], hidden[:, 640:1280]
        logits = jnp.where(lane < 10, hidden[:, 1280:], -1e30)
        raised = jnp.exp(logits - jnp.max(logits, axis=1, keepdims=True))
        route_probs = raised / jnp.sum(raised, axis=1, keepdims=True)
        gates = dot(route_probs * chosen, spread[...], 1, 0, HIGHEST)
        sig = 1.0 / (1.0 + jnp.exp(-gate_h))
        silu = gate_h * sig
        activated = (silu * up_h).astype(BF).astype(F32)
        gated[rows, :] = (activated * gates).astype(BF)
        act_grad = out_grad * gates
        hidden_grad[rows, :640] = (act_grad * up_h * sig * (1.0 + gate_h * (1.0 - sig))).astype(BF)
        hidden_grad[rows, 640:1280] = (act_grad * silu).astype(BF)
        chosen_grad = dot(activated * out_grad, spread[...], 1, 1, HIGHEST) * chosen
        inner = jnp.sum(chosen_grad * route_probs, axis=1, keepdims=True)
        hidden_grad[rows, 1280:] = (route_probs * (chosen_grad - inner)).astype(BF)
        return 0

    lax.fori_loop(0, 4, block, 0)
    take_rows(places, hidden_grad, ordered)
    project(ordered, near, far, slice(0, 1408), outs)


def output_kernel(gated, near, far, out):
    for b in range(4):
        rows = slice(256 * b, 256 * b + 256)
        out[rows, :1024] = dot(gated[rows, :], near[:, 1408:], 1, 1).astype(BF)
        out[rows, 1024:] = dot(gated[rows, :], far[:, 1408:], 1, 1).astype(BF)


def middle_grad_kernel(start, length, *refs):
    terms, (middle, cot, gain, middle_grad), outs = refs[:8], refs[8:12], refs[12:]
    for i in range(4):
        rows = slice(16 * i, 16 * i + 16)
        inside = (
            start[0] + 16 * i + lax.broadcasted_iota(jnp.int32, (16, 1), 0) < length[0]
        )
        grad = jnp.where(inside, cot[rows, :].astype(F32), 0.0)
        scaled = (terms[i][...].astype(F32) + terms[4 + i][...].astype(F32)) * gain[...]
        held = middle[rows, :]
        rate = lax.rsqrt(jnp.mean(held * held, axis=1, keepdims=True) + EPSILON)
        inner = jnp.mean(scaled * held, axis=1, keepdims=True)
        total = grad + rate * scaled - held * (rate * rate * rate * inner)
        middle_grad[rows, :] = total
        outs[i][...] = total.astype(BF)


def backward_kernel(places, length, *refs):
    pieces, refs = refs[:8], refs[8:]
    (near, far, qkv, rates, gains, cosine, sine, queries, keys, values, log_total) = refs[:11]
    (branch, q_scaled, k_scaled, v_grad, inner, gain_grads) = refs[11:17]
    grad, key_grad, value_grad = refs[17:]

    def turn_back(held):
        return held * cosine[...] - pltpu.roll(held, 64, 1) * sine[...]

    put_pieces(places, pieces, branch)
    key_grad[...] = jnp.zeros_like(key_grad)
    value_grad[...] = jnp.zeros_like(value_grad)
    for at in range(4):
        rows, upto = slice(256 * at, 256 * at + 256), slice(0, 256 * at + 256)
        held = dot(branch[rows, :1024], near[:, 512:]) + dot(branch[rows, 1024:], far[:, 512:])
        grad[rows, :] = held.astype(BF)
        scores = dot(queries[rows, :], keys[upto, :], 1, 1) * SCALE
        probs = jnp.where(allowed_block(length, at), jnp.exp(scores - log_total[rows, :]), 0.0)
        prob_grad = dot(grad[rows, :], values[upto, :], 1, 1)
        delta = jnp.sum(probs * prob_grad, axis=1, keepdims=True)
        score_grad = (probs * (prob_grad - delta)).astype(BF)
        q_scaled[rows, :] = dot(score_grad, keys[upto, :]) * SCALE
        key_grad[upto, :] += dot(score_grad, queries[rows, :], 0, 0) * SCALE
        value_grad[upto, :] += dot(probs.astype(BF), grad[rows, :], 0, 0)
    v_grad[...] = value_grad[...].astype(BF)
    q_norm_grad = turn_back(q_scaled[...])
    k_norm_grad = turn_back(key_grad[...])
    q_turned = q_norm_grad * qkv[:, :128]
    k_turned = k_norm_grad * qkv[:, 128:256]
    gain_grads[0:1, :] = jnp.sum(q_turned * rates[:, 0:1], axis=0, keepdims=True)
    gain_grads[1:2, :] = jnp.sum(k_turned * rates[:, 1:2], axis=0, keepdims=True)
    inner[0:1, :] = row_sums(q_turned * gains[0:1, :])
    inner[1:2, :] = row_sums(k_turned * gains[1:2, :])
    q_scaled[...] = q_norm_grad * gains[0:1, :]
    k_scaled[...] = k_norm_grad * gains[1:2, :]


def exit_kernel(places, q_scaled, k_scaled, v_grad, qkv, rates, inner, near, far, grad, *rest):
    pieces, ordered = rest[:8], rest[8]
    for at, scaled in enumerate((q_scaled, k_scaled)):
        columns = slice(128 * at, 128 * at + 128)
        rate = rates[:, at : at + 1]
        factor = rate * rate * rate * inner[:, at : at + 1] * (1.0 / 2048)
        grad[:, columns] = (rate * scaled[...] - qkv[:, columns] * factor).astype(BF)
    grad[:, 256:] = v_grad[...]
    take_rows(places, grad, ordered)
    project(ordered, near, far, slice(0, 384), pieces)


def input_grad_kernel(*refs):
    terms, (middle_grad, own, gain, out) = refs[:8], refs[8:]
    for i in range(4):
        rows = slice(16 * i, 16 * i + 16)
        scaled = (terms[i][...].astype(F32) + terms[4 + i][...].astype(F32)) * gain[...]
        held = own[rows, :].astype(F32)
        rate = lax.rsqrt(jnp.mean(held * held, axis=1, keepdims=True) + EPSILON)
        inner = jnp.mean(scaled * held, axis=1, keepdims=True)
        total = middle_grad[rows, :] + rate * scaled - held * (rate * rate * rate * inner)
        out[rows, :] = total.astype(BF)


def token_sums(stats):
    held = stats.reshape(1, 16, 128)
    arrived = all_to_all(jnp.broadcast_to(held, (16, 16, 128)), GROUP)
    return jnp.sum(arrived, axis=0).reshape(2, 1024).T


def angles(head_size):
    steps_half = jnp.arange(head_size // 2).astype(F32)
    frequency = jnp.exp(steps_half * (-2.0 * math.log(ROPE_BASE) / head_size))
    turned = jnp.arange(1024, dtype=jnp.int32).astype(F32)[:, None] * frequency[None, :]
    cosine, sine = jnp.cos(turned), jnp.sin(turned)
    return (
        jnp.concatenate([cosine, cosine], axis=-1),
        jnp.concatenate([-sine, sine], axis=-1),
    )


def after(value, earlier):
    return lax.optimization_barrier((value, earlier))[0]


def per_device(
    tokens,
    lengths,
    routes,
    attn_gain,
    q_gain,
    k_gain,
    w_query,
    w_key,
    w_value,
    w_out,
    mlp_gain,
    router,
    w_gate,
    w_up,
    w_down,
    cotangent,
):
    z = lax.axis_index("z")
    yh = lax.axis_index("yh")
    core = lax.axis_index("c")

    def own_first(v):
        halves = v.reshape(64, 16, 2, 64)
        halves = jnp.where(core == 0, halves, halves[:, :, ::-1])
        return halves.transpose(0, 2, 1, 3).reshape(64, 2048)

    def natural(v):
        halves = v.reshape(64, 2, 16, 64).transpose(0, 2, 1, 3)
        return jnp.where(core == 0, halves, halves[:, :, ::-1]).reshape(64, 2048)

    own_start = (core, yh * 64, 0)
    own_tokens = own_first(lax.dynamic_slice(tokens, own_start, (1, 64, 2048))[0])
    token_pieces = cube_gather([own_tokens[16 * i : 16 * i + 16] for i in range(4)])
    places = block_places()
    slot_length = lax.dynamic_slice(lengths, (core,), (1,))

    def four(w):
        return w.reshape(64, 4, -1).transpose(1, 0, 2)

    def pack_experts(w):
        return four(w.transpose(1, 0, 2).reshape(64, 2560))

    def per_row(v):
        return jnp.broadcast_to(v[None], (4,) + v.shape)

    gains = jnp.stack([q_gain, k_gain], axis=-1)
    extra = jnp.concatenate(
        [
            per_row(jnp.stack([attn_gain, mlp_gain], axis=1)),
            jnp.pad(gains, ((0, 0), (0, 60), (0, 0))),
            jnp.zeros((4, 64, 124), BF),
        ],
        axis=-1,
    )
    first_pack = jnp.concatenate(
        [four(w_query), four(w_key), four(w_value), extra, four(w_out.T)], axis=-1
    )
    first = all_to_all(
        jnp.broadcast_to(swap_cores(first_pack)[None], (4, 4, 64, 640)).reshape(16, 64, 640),
        ("x", "z"),
    ).reshape(1024, 640)
    first_far = other_core(first)
    second_pack = jnp.concatenate(
        [
            pack_experts(w_gate),
            pack_experts(w_up),
            per_row(jnp.pad(router, ((0, 0), (0, 118)))),
            four(w_down.reshape(2560, 64).T),
        ],
        axis=-1,
    )
    second = all_to_all(swap_cores(after(second_pack, first)), "z")
    second = lax.all_gather(second, "x", axis=0, tiled=False).reshape(1024, 2048)
    second_far = other_core(second)
    extra_all = jnp.concatenate([first[:, 384:388], first_far[:, 384:388]], axis=0)
    gain_lines = extra_all[:, :2].astype(F32).T
    attn_row, mlp_row = gain_lines[0:1], gain_lines[1:2]
    gain_blocks = extra_all[:, 2:4].reshape(2, 16, 64, 2)[:, :, :4]
    gain_blocks = jnp.where(core == 0, gain_blocks, gain_blocks[::-1])
    gain_rows = gain_blocks.transpose(3, 1, 0, 2).reshape(2, 128).astype(F32)

    own_cot = own_first(lax.dynamic_slice(cotangent, own_start, (1, 64, 2048))[0])
    own_routes = lax.dynamic_slice(routes, own_start, (1, 64, 8))[0]
    expert_ids = jnp.arange(128, dtype=jnp.int32)
    own_chosen = jnp.sum((own_routes[:, :, None] == expert_ids).astype(BF), axis=1)
    routed = after(jnp.concatenate([own_cot, own_chosen], axis=1), first)
    routed = all_to_all(jnp.broadcast_to(routed[None], (16, 64, 2176)), GROUP).reshape(1024, 2176)

    normed, qkv, stats = kernel_call(
        enter_kernel,
        [((1024, 2048), BF), ((1024, 384), F32), ((2, 1024), F32)],
        [SMEM] + [VMEM] * 11,
        24,
        2 * 1024 * 2048 * 384,
    )(places, *token_pieces, attn_row, first, first_far)
    rates = lax.rsqrt(token_sums(stats) / 2048 + EPSILON)
    cosine, sine = angles(128)
    queries, keys, values, attended, log_total, *pieces = kernel_call(
        forward_kernel,
        [HEAD, HEAD, HEAD, HEAD, ((1024, 1), F32)] + [PIECE] * 8,
        [SMEM, SMEM] + [VMEM] * 7,
        28,
        4 * 1024 * 1024 * 128,
        [pltpu.VMEM((1024, 128), BF)],
    )(places, slot_length, qkv, rates, gain_rows, cosine, sine, first, first_far)
    own_row = ((64, 2048), F32)
    own_part = ((16, 2048), BF)
    middle, *parts = kernel_call(middle_kernel, [own_row] + [own_part] * 4, [VMEM] * 10, 8)(
        *cube_scatter(pieces), own_tokens, mlp_row
    )

    tile_expert = (5 * z + jnp.arange(640, dtype=jnp.int32) // 128) // 2
    tile_of = (tile_expert[None, :] == expert_ids[:, None]).astype(F32)
    mixed, grad_out, gated, hidden_grad, *pieces = kernel_call(
        mixture_kernel,
        [((1024, 2048), BF), ((1024, 2048), BF), ((1024, 640), BF), ((1024, 1408), BF)]
        + [PIECE] * 8,
        [SMEM, SMEM] + [VMEM] * 12,
        56,
        2 * 1024 * 2048 * 3456,
        [pltpu.VMEM((1024, 1408), BF)],
    )(places, slot_length, *cube_gather(parts), routed, second, second_far, tile_of)
    own_place = ((2 * z + lax.axis_index("yl")) * 128 + yh * 64)[None]
    middle_grad, *parts = kernel_call(
        middle_grad_kernel, [own_row] + [own_part] * 4, [SMEM, SMEM] + [VMEM] * 11, 8
    )(own_place, slot_length, *cube_scatter(pieces), middle, own_cot, mlp_row)

    def fold_cores(left, right):
        near = dot(left[:, :1024], right, 0, 0)
        far = other_core(dot(left[:, 1024:], right, 0, 0).astype(BF))
        return (near + far.astype(F32)).astype(BF)

    def fold_shards(grads):
        return lax.psum_scatter(
            grads.reshape(4, 256, -1), "x", scatter_dimension=0, tiled=False
        ).reshape(4, 64, -1)

    expert_grads = jnp.concatenate(
        [fold_shards(fold_cores(mixed, hidden_grad)), fold_shards(fold_cores(grad_out, gated))],
        axis=-1,
    )
    expert_grads = all_to_all(swap_cores(expert_grads), "z")

    branch, q_scaled, k_scaled, v_grad, inner, gain_grads = kernel_call(
        backward_kernel,
        [((1024, 2048), BF), WIDE_HEAD, WIDE_HEAD, HEAD, ((2, 1024), F32), ((2, 128), F32)],
        [SMEM, SMEM] + [VMEM] * 19,
        40,
        10 * 1024 * 1024 * 128,
        [pltpu.VMEM((1024, 128), BF), pltpu.VMEM((1024, 128), F32), pltpu.VMEM((1024, 128), F32)],
    )(
        places, slot_length, *cube_gather(parts), first, first_far,
        qkv, rates, gain_rows, cosine, sine, queries, keys, values, log_total,
    )
    (products,) = kernel_call(
        output_kernel, [((1024, 2048), BF)], [VMEM] * 3, 20, 2 * 1024 * 2048 * 640
    )(gated, second, second_far)
    products = after(products, inner)
    mixture = all_to_all(products.reshape(16, 64, 2048), GROUP)
    own_output = (middle + jnp.sum(mixture.astype(F32), axis=0)).astype(BF)
    qkv_grad, *pieces = kernel_call(
        exit_kernel,
        [((1024, 384), BF)] + [PIECE] * 8,
        [SMEM] + [VMEM] * 8,
        20,
        2 * 1024 * 2048 * 384,
        [pltpu.VMEM((1024, 384), BF)],
    )(places, q_scaled, k_scaled, v_grad, qkv, rates, token_sums(inner), first, first_far)
    (own_input_grad,) = kernel_call(input_grad_kernel, [((64, 2048), BF)], [VMEM] * 11, 8)(
        *cube_scatter(pieces), middle_grad, own_tokens, attn_row
    )
    gain_block = gain_grads.reshape(2, 16, 2, 4)
    gain_block = jnp.where(core == 0, gain_block, gain_block[:, :, ::-1])
    gain_block = gain_block.transpose(2, 1, 3, 0)
    gain_block = jnp.pad(gain_block, ((0, 0), (0, 0), (0, 60), (0, 126))).reshape(2048, 128)
    gain_block = gain_block[:1024] + other_core(gain_block[1024:])
    attn_grads = jnp.concatenate(
        [fold_cores(normed, qkv_grad), fold_cores(branch, attended), gain_block.astype(BF)], axis=1
    )
    attn_grads = all_to_all(attn_grads.reshape(16, 64, 640), ("x", "z"))
    attn_grads = jnp.sum(attn_grads.reshape(4, 4, 64, 640).astype(F32), axis=0).astype(BF)
    attn_grads = swap_cores(attn_grads)

    def whole(own):
        far = other_half(own)
        both = jnp.where(yh == 0, jnp.concatenate([own, far]), jnp.concatenate([far, own]))
        there = other_core(both)
        return jnp.where(core == 0, jnp.stack([both, there]), jnp.stack([there, both]))

    def wide(grads):
        return grads.transpose(1, 0, 2).reshape(64, -1).astype(F32)

    def experts(grads):
        return wide(grads).reshape(64, 10, 256).transpose(1, 0, 2)

    q_grads = wide(attn_grads[:, :, :128])
    k_grads = wide(attn_grads[:, :, 128:256])
    v_grads = wide(attn_grads[:, :, 256:384])
    o_grads = wide(attn_grads[:, :, 384:512]).T
    q_gain_grad = attn_grads[:, :4, 512].astype(F32)
    k_gain_grad = attn_grads[:, :4, 513].astype(F32)
    gate_grads = experts(expert_grads[:, :, :640])
    up_grads = experts(expert_grads[:, :, 640:1280])
    router_part = jnp.sum(expert_grads[:, :, 1280:1290].astype(F32), axis=0)
    down_out = wide(expert_grads[:, :, 1408:]).T.reshape(10, 256, 64)

    attn_part = sum(
        jnp.sum(w.astype(F32) * g, axis=1)
        for w, g in ((w_query, q_grads), (w_key, k_grads), (w_value, v_grads))
    )
    mlp_part = sum(
        jnp.sum(w.astype(F32) * g, axis=(0, 2)) for w, g in ((w_gate, gate_grads), (w_up, up_grads))
    ) + jnp.sum(router.astype(F32) * router_part, axis=1)
    summed = jnp.concatenate([router_part, attn_part[:, None], mlp_part[:, None]], axis=1)
    summed = summed + other_core(summed)
    summed = summed + other_half(summed)
    return (
        whole(natural(own_output)),
        whole(natural(own_input_grad)).astype(F32),
        summed[:, 10] / attn_gain.astype(F32),
        q_gain_grad,
        k_gain_grad,
        q_grads,
        k_grads,
        v_grads,
        o_grads,
        summed[:, 11] / mlp_gain.astype(F32),
        summed[:, :10],
        gate_grads,
        up_grads,
        down_out,
    )


def solution(mesh):
    fine = Mesh(mesh.devices.reshape(SIZES), AXES)
    rows = P("x", CONTEXT, None)
    vector = P(WEIGHT)
    gains = P(TENSOR, WEIGHT)
    tall = P(WEIGHT, TENSOR)
    routed = P(WEIGHT, None)
    hidden = P(None, WEIGHT, TENSOR)
    back = P(None, TENSOR, WEIGHT)
    weights = (vector, gains, gains, tall, tall, tall, gains, vector, routed, hidden, hidden, back)
    return jax.shard_map(
        per_device,
        mesh=fine,
        in_specs=(rows, P("x"), rows) + weights + (rows,),
        out_specs=(rows, rows) + weights,
        check_vma=False,
    )
```

time: 886 us -> 753 us (0.85)
  local copies, waits for them, and re-layouts: 216 us -> 105 us
  other arithmetic: 130 us -> 31.2 us
  Pallas kernels: 0 us -> 83.7 us
  waiting for transfers between devices: 182 us -> 253 us
  matrix products: 82 us -> 29.7 us
  blocking collectives: 27.7 us -> 14 us
    pallas_call x0 -> x27, Pallas kernels: none -> 83.7 us  [the longest x1 33.7 us: per_device(): kernel_call(mixture_kernel, [((1024, 2048), BF), ((1024, 2048), BF), ((10...]
    ppermute x136 -> x109, waiting for transfers between devices: 150 us -> 208 us  [exchange(): return lambda v: lax.ppermute(v, axes, pairs)]
    dot_general x19 -> x8, matrix products: 82 us -> 29.7 us  [dot(): lax.dot_general(a, b, (((left,), (right,)), ((), ())), preferred_element_...]
    slice x78 -> x17, local copies, waits for them, and re-layouts: 55.2 us -> 5.49 us  [the longest x5 2.85 us: per_device(): gain_block = gain_block[:1024] + other_core(gain_block[1024:])]
    add x60 -> x3, other arithmetic: 41.9 us -> 0.03 us  [the longest x1 0.02 us: block_places(): return ((2 * z + (y & 1)) * 2 + (y >> 1)) * 4 + part]
    concatenate x52 -> x6, other arithmetic: 44 us -> 5.36 us  [the longest x1 2.32 us: per_device(): jnp.concatenate([fold_shards(fold_cores(mixed, hidden_grad)), fold_shards...]
    optimization_barrier x24 -> x0, local copies, waits for them, and re-layouts: 34.2 us -> none  [cube_gather(): lax.optimization_barrier(tuple((CUBE[(i + step) % 4](parts[i]) for i in r...]
    all_to_all x4 -> x7, waiting for transfers between devices: 14 us -> 45 us  [all_to_all(): return lax.all_to_all(v, axes, split_axis=0, concat_axis=0, tiled=True)]
  transfers between devices with their start and end apart: 154 -> 123, of which waited for: 62 -> 71; matrix products, arithmetic and copies ran while one was open for 38% -> 14% of each run, Pallas kernels for 0% -> 7%
where the time goes in v2:
time: 753 us; the launch traced here: 741 us
  waiting for transfers between devices  253 us (34%)
  starting transfers between devices  209 us (28%)
  local copies, waits for them, and re-layouts  105 us (14%)
  Pallas kernels  83.7 us (11%)
  other arithmetic  31.2 us (4%)
  matrix products  29.7 us (4%)
  between operations  15.6 us (2%)
  blocking collectives  14 us (2%)
    ppermute x109, waiting for transfers between devices, exchange(): return lambda v: lax.ppermute(v, axes, pairs)  208 us
    ppermute x109, starting transfers between devices, exchange(): return lambda v: lax.ppermute(v, axes, pairs)  156 us
    unnamed x207, local copies, waits for them, and re-layouts  54.2 us
    all_to_all x7, waiting for transfers between devices, all_to_all(): return lax.all_to_all(v, axes, split_axis=0, concat_axis=0, tiled=True)  45 us
    all_to_all x7, starting transfers between devices, all_to_all(): return lax.all_to_all(v, axes, split_axis=0, concat_axis=0, tiled=True)  39.2 us
    pallas_call x1, Pallas kernels, per_device(): kernel_call(mixture_kernel, [((1024, 2048), BF), ((1024, 2048), BF), ((10...  33.7 us
    dot_general x8, matrix products, dot(): lax.dot_general(a, b, (((left,), (right,)), ((), ())), preferred_element_...  29.7 us
  transfers between devices with their start and end apart: 123, of which 71 were waited for; matrix products, arithmetic and copies ran while one was open for 14% of the time, Pallas kernels for 7%

profile of v2, /device:TPU:0, one launch (start us, length us, event | category | flops | bytes accessed | tf_op | source)
XLA Modules:
  0.0 740.8 jit_solution(18403117735932829329)
XLA Ops:
  14.9 8.1 %all-to-all-start = ((bf16[16,64,640]{2,1,0:T(8,128)(2,1)}), bf16[16,64,640]{2,1,0:T(8,128)(2,1)S(1)}, u32[]{:S(2)}, u32[]{:S(2)}) async-start(bf16[16,64,640]{2,1,0:T(8,128)(2,1)} %bitcast.10), calls=%async_computation | async-start | bytes 2621440 | tf_op jit(solution)/shard_map/all_to_all | solution.py:49
  26.1 11.7 %all-to-all-done = bf16[16,64,640]{2,1,0:T(8,128)(2,1)S(1)} async-done(((bf16[16,64,640]{2,1,0:T(8,128)(2,1)}), bf16[16,64,640]{2,1,0:T(8,128)(2,1)S(1)}, u32[]{:S(2)}, u32[]{:S(2)}) %all-to-all-start) | async-done | bytes 1310752 | tf_op jit(solution)/shard_map/all_to_all | solution.py:49
  40.2 14.0 %all_to_all.40 = bf16[4,64,2048]{2,1,0:T(8,128)(2,1)} all-to-all(bf16[4,64,2048]{2,1,0:T(8,128)(2,1)S(1)} %copy.348), channel_id=1, replica_groups=mesh['x'=4,'z'=4,'yl'=2,'yh'=2,'c'=2] {'z'}, dimensions={0} | all-to-all | bytes 2097152 | tf_op jit(solution)/shard_map/all_to_all | solution.py:49
  55.8 20.7 %collective-permute-start.17 = (bf16[1024,640]{0,1:T(8,128)(2,1)}, bf16[1024,640]{0,1:T(8,128)(2,1)}, u32[]{:S(2)}, u32[]{:S(2)}) collective-permute-start(bf16[1024,640]{0,1:T(8,128)(2,1)} %copy.335), channel_id=1, source_target_pairs={{0,1},{1,0},{2,3},{3,2},{4,5},{5,4},{6,7},{7,6},{8,9},{9,8},{10,11... | collective-permute-start | bytes 3932168 | tf_op jit(solution)/shard_map/ppermute | solution.py:33
  82.1 4.3 collective-permute-start.3
  131.6 12.9 %shard_map.266 = (bf16[1024,2048]{1,0:T(8,128)(2,1)S(1)}, f32[1024,384]{1,0:T(8,128)S(1)}, f32[2,1024]{1,0:T(2,128)S(1)}) custom-call(s32[64]{0:T(128)S(1)} %multiply_add_fusion.places, bf16[128,2048]{1,0:T(8,128)(2,1)S(1)} %get-tuple-element.186.refs_0_, bf16[128,2048]{1,0:T(8,128)(2,1)} %get-tuple-element.187.refs_1_, ...), custom_call_target="tpu_custom_call" | custom-call | flops 1610612736 | bytes 4194304 | tf_op jit(solution)/shard_map/pallas_call | solution.py:437
  148.3 5.9 all-to-all-start.1
  154.4 7.9 %all-to-all-done.1 = f32[16,16,128]{2,1,0:T(8,128)S(1)} async-done(((f32[16,16,128]{2,1,0:T(8,128)}), f32[16,16,128]{2,1,0:T(8,128)S(1)}, u32[]{:S(2)}, u32[]{:S(2)}) %all-to-all-start.1) | async-done | bytes 131104 | tf_op jit(solution)/shard_map/all_to_all | solution.py:49
  165.0 4.7 all-to-all-start.2
  178.1 5.4 shard_map.267
  190.9 39.8 %collective-permute-done.18.refs_4_ = bf16[128,2048]{1,0:T(8,128)(2,1)S(1)} collective-permute-done((bf16[128,2048]{1,0:T(8,128)(2,1)S(1)}, bf16[128,2048]{1,0:T(8,128)(2,1)S(1)}, u32[]{:S(2)}, u32[]{:S(2)}) %collective-permute-start.18) | collective-permute-done | bytes 524320 | tf_op jit(solution)/shard_map/ppermute | solution.py:33
  232.1 4.8 collective-permute-start.23
  292.9 6.5 collective-permute-done.42.refs_4_
  315.4 33.7 %shard_map.275 = (bf16[1024,2048]{1,0:T(8,128)(2,1)}, bf16[1024,2048]{1,0:T(8,128)(2,1)}, bf16[1024,640]{1,0:T(8,128)(2,1)}, bf16[1024,1408]{1,0:T(8,128)(2,1)},...) custom-call(s32[64]{0:T(128)} %copy-done.67, ...), custom_call_target="tpu_custom_call" | custom-call | flops 14495514624 | bytes 4194304 | tf_op jit(solution)/shard_map/pallas_call | solution.py:462
  354.9 7.7 %collective-permute-done.52.refs_4_ = bf16[128,2048]{1,0:T(8,128)(2,1)S(1)} collective-permute-done((bf16[128,2048]{1,0:T(8,128)(2,1)}, bf16[128,2048]{1,0:T(8,128)(2,1)S(1)}, u32[]{:S(2)}, u32[]{:S(2)}) %collective-permute-start.52) | collective-permute-done | bytes 524320 | tf_op jit(solution)/shard_map/ppermute | solution.py:33
  372.9 4.6 fusion.14
  383.3 4.9 convolution_convert_fusion
  435.4 4.9 add_convert_fusion.1
  449.1 5.9 collective-permute-done.80.refs_4_
  463.2 8.4 %shard_map.284 = (bf16[1024,2048]{1,0:T(8,128)(2,1)}, f32[1024,128]{1,0:T(8,128)S(1)}, f32[1024,128]{1,0:T(8,128)S(1)}, bf16[1024,128]{1,0:T(8,128)(2,1)S(1)}, f...) custom-call(s32[64]{0:T(128)S(1)} %copy-done.68, s32[1]{0:T(128)} %dynamic_slice.12.length, ...), custom_call_target="tpu_custom_call" | custom-call | flops 1342177280 | bytes 4194304 | tf_op jit(solution)/shard_map/pallas_call | solution.py:492
  474.8 5.5 all-to-all-start.5
  483.4 5.0 all-to-all-done.5
  495.9 3.8 shard_map.285
  504.7 6.2 add_convert_fusion
  521.3 3.7 all-to-all-start.7
  527.3 5.7 shard_map.276
  535.0 20.5 %all-to-all-done.7 = bf16[16,64,640]{2,1,0:T(8,128)(2,1)S(1)} async-done(((bf16[16,64,640]{2,1,0:T(8,128)(2,1)}), bf16[16,64,640]{2,1,0:T(8,128)(2,1)S(1)}, u32[]{:S(2)}, u32[]{:S(2)}) %all-to-all-start.7) | async-done | bytes 1310752 | tf_op jit(solution)/shard_map/all_to_all | solution.py:49
  556.5 7.8 %all-to-all-start.4 = ((bf16[16,64,2048]{2,1,0:T(8,128)(2,1)}), bf16[16,64,2048]{2,1,0:T(8,128)(2,1)}, u32[]{:S(2)}, u32[]{:S(2)}) async-start(bf16[16,64,2048]{2,1,0:T(8,128)(2,1)} %bitcast.146), calls=%async_computation.4 | async-start | bytes 8388608 | tf_op jit(solution)/shard_map/all_to_all | solution.py:49
  571.2 59.5 %collective-permute-done.86.refs_4_ = bf16[128,2048]{1,0:T(8,128)(2,1)S(1)} collective-permute-done((bf16[128,2048]{1,0:T(8,128)(2,1)}, bf16[128,2048]{1,0:T(8,128)(2,1)S(1)}, u32[]{:S(2)}, u32[]{:S(2)}) %collective-permute-start.86) | collective-permute-done | bytes 524320 | tf_op jit(solution)/shard_map/ppermute | solution.py:33
  667.5 6.5 collective-permute-done.102
  680.9 9.6 %collective-permute-start.106 = (bf16[4,64,2048]{2,1,0:T(8,128)(2,1)}, bf16[4,64,2048]{2,1,0:T(8,128)(2,1)}, u32[]{:S(2)}, u32[]{:S(2)}) collective-permute-start(bf16[4,64,2048]{2,1,0:T(8,128)(2,1)} %pad_maximum_fusion.2), channel_id=1, source_target_pairs={{0,0},{1,4},{4,1},{5,5},{2,2},{3,6},{6,3},{7,7},{8,8},{9,12},{12,9... | collective-permute-start | bytes 3145736 | tf_op jit(solution)/shard_map/ppermute | solution.py:37
  712.3 3.7 collective-permute-start.85
  (594 shorter events, 370.7 us)
Async XLA Ops:
  14.9 22.9 %all-to-all-start = ((bf16[16,64,640]{2,1,0:T(8,128)(2,1)}), bf16[16,64,640]{2,1,0:T(8,128)(2,1)S(1)}, u32[]{:S(2)}, u32[]{:S(2)}) async-start(bf16[16,64,640]{2,1,0:T(8,128)(2,1)} %bitcast.10), calls=%async_computation | async-start | bytes 2621440 | tf_op jit(solution)/shard_map/all_to_all | solution.py:49
  23.0 131.3 %all-gather.3.cloned.1.call-start = ((), (), s32[]{:S(2)}) async-start(), calls=%async_computation.12 | async-start | bytes 5242880 | tf_op jit(solution)/shard_map/all_gather | solution.py:421
  55.8 67.6 %collective-permute-start.17 = (bf16[1024,640]{0,1:T(8,128)(2,1)}, bf16[1024,640]{0,1:T(8,128)(2,1)}, u32[]{:S(2)}, u32[]{:S(2)}) collective-permute-start(bf16[1024,640]{0,1:T(8,128)(2,1)} %copy.335), channel_id=1, source_target_pairs={{0,1},{1,0},{2,3},{3,2},{4,5},{5,4},{6,7},{7,6},{8,9},{9,8},{10,11... | collective-permute-start | bytes 3932168 | tf_op jit(solution)/shard_map/ppermute | solution.py:33
  117.6 11.6 %collective-permute-start.12 = (bf16[128,2048]{1,0:T(8,128)(2,1)S(1)}, bf16[128,2048]{1,0:T(8,128)(2,1)}, u32[]{:S(2)}, u32[]{:S(2)}) collective-permute-start(bf16[128,2048]{1,0:T(8,128)(2,1)S(1)} %get-tuple-element.186.refs_0_), channel_id=1, source_target_pairs={{0,6},{2,4},{4,2},{6,0},{1,7},{3,5},{5,3},{7,1},{8,14},{10,12},{12... | collective-permute-start | bytes 1572872 | tf_op jit(solution)/shard_map/ppermute | solution.py:33
  120.6 11.0 %collective-permute-start.15 = (bf16[128,2048]{1,0:T(8,128)(2,1)}, bf16[128,2048]{1,0:T(8,128)(2,1)}, u32[]{:S(2)}, u32[]{:S(2)}) collective-permute-start(bf16[128,2048]{1,0:T(8,128)(2,1)} %get-tuple-element.189.refs_3_), channel_id=1, source_target_pairs={{0,24},{8,16},{16,8},{24,0},{1,25},{9,17},{17,9},{25,1},{2,26},{10... | collective-permute-start | bytes 1572872 | tf_op jit(solution)/shard_map/ppermute | solution.py:33
  148.3 13.9 %all-to-all-start.1 = ((f32[16,16,128]{2,1,0:T(8,128)}), f32[16,16,128]{2,1,0:T(8,128)S(1)}, u32[]{:S(2)}, u32[]{:S(2)}) async-start(f32[16,16,128]{2,1,0:T(8,128)} %broadcast_in_dim.24), calls=%async_computation.1 | async-start | bytes 262144 | tf_op jit(solution)/shard_map/all_to_all | solution.py:49
  154.3 161.1 %collective-permute-start.51 = (bf16[1024,2048]{1,0:T(8,128)(2,1)}, bf16[1024,2048]{1,0:T(8,128)(2,1)}, u32[]{:S(2)}, u32[]{:S(2)}) collective-permute-start(bf16[1024,2048]{1,0:T(8,128)(2,1)} %bitcast.150), channel_id=1, source_target_pairs={{0,1},{1,0},{2,3},{3,2},{4,5},{5,4},{6,7},{7,6},{8,9},{9,8},{10,11... | collective-permute-start | bytes 12582920 | tf_op jit(solution)/shard_map/ppermute | solution.py:33
  165.0 150.4 %all-to-all-start.2 = ((bf16[16,64,2176]{2,1,0:T(8,128)(2,1)}), bf16[16,64,2176]{2,1,0:T(8,128)(2,1)}, u32[]{:S(2)}, u32[]{:S(2)}) async-start(bf16[16,64,2176]{2,1,0:T(8,128)(2,1)} %broadcast_in_dim.25), calls=%async_computation.2 | async-start | bytes 8912896 | tf_op jit(solution)/shard_map/all_to_all | solution.py:49
  169.6 508.9 %reduce-scatter.5.cloned.1.call-start = ((), (), s32[]{:S(2)}) async-start(), calls=%async_computation.11 | async-start | bytes 1638400 | tf_op jit(solution)/shard_map/reduce_scatter | solution.py:482
  184.0 46.7 %collective-permute-start.18 = (bf16[128,2048]{1,0:T(8,128)(2,1)S(1)}, bf16[128,2048]{1,0:T(8,128)(2,1)S(1)}, u32[]{:S(2)}, u32[]{:S(2)}) collective-permute-start(bf16[128,2048]{1,0:T(8,128)(2,1)S(1)} %get-tuple-element.196), channel_id=1, source_target_pairs={{0,6},{2,4},{4,2},{6,0},{1,7},{3,5},{5,3},{7,1},{8,14},{10,12},{12... | collective-permute-start | bytes 1572872 | tf_op jit(solution)/shard_map/ppermute | solution.py:33
  187.1 43.6 %collective-permute-start.19 = (bf16[128,2048]{1,0:T(8,128)(2,1)S(1)}, bf16[128,2048]{1,0:T(8,128)(2,1)S(1)}, u32[]{:S(2)}, u32[]{:S(2)}) collective-permute-start(bf16[128,2048]{1,0:T(8,128)(2,1)S(1)} %get-tuple-element.197), channel_id=1, source_target_pairs={{0,8},{8,0},{16,24},{24,16},{1,9},{9,1},{17,25},{25,17},{2,10},{10... | collective-permute-start | bytes 1572872 | tf_op jit(solution)/shard_map/ppermute | solution.py:33
  188.6 42.2 %collective-permute-start.20 = (bf16[128,2048]{1,0:T(8,128)(2,1)S(1)}, bf16[128,2048]{1,0:T(8,128)(2,1)S(1)}, u32[]{:S(2)}, u32[]{:S(2)}) collective-permute-start(bf16[128,2048]{1,0:T(8,128)(2,1)S(1)} %get-tuple-element.198), channel_id=1, source_target_pairs={{0,4},{2,6},{4,0},{6,2},{1,5},{3,7},{5,1},{7,3},{8,12},{10,14},{12... | collective-permute-start | bytes 1572872 | tf_op jit(solution)/shard_map/ppermute | solution.py:33
  188.8 41.9 %collective-permute-start.21 = (bf16[128,2048]{1,0:T(8,128)(2,1)S(1)}, bf16[128,2048]{1,0:T(8,128)(2,1)S(1)}, u32[]{:S(2)}, u32[]{:S(2)}) collective-permute-start(bf16[128,2048]{1,0:T(8,128)(2,1)S(1)} %get-tuple-element.199), channel_id=1, source_target_pairs={{0,24},{8,16},{16,8},{24,0},{1,25},{9,17},{17,9},{25,1},{2,26},{10... | collective-permute-start | bytes 1572872 | tf_op jit(solution)/shard_map/ppermute | solution.py:33
  349.1 13.5 %collective-permute-start.52 = (bf16[128,2048]{1,0:T(8,128)(2,1)}, bf16[128,2048]{1,0:T(8,128)(2,1)S(1)}, u32[]{:S(2)}, u32[]{:S(2)}) collective-permute-start(bf16[128,2048]{1,0:T(8,128)(2,1)} %get-tuple-element.248), channel_id=1, source_target_pairs={{0,6},{2,4},{4,2},{6,0},{1,7},{3,5},{5,3},{7,1},{8,14},{10,12},{12... | collective-permute-start | bytes 1572872 | tf_op jit(solution)/shard_map/ppermute | solution.py:33
  350.5 12.2 %collective-permute-start.53 = (bf16[128,2048]{1,0:T(8,128)(2,1)}, bf16[128,2048]{1,0:T(8,128)(2,1)S(1)}, u32[]{:S(2)}, u32[]{:S(2)}) collective-permute-start(bf16[128,2048]{1,0:T(8,128)(2,1)} %get-tuple-element.249), channel_id=1, source_target_pairs={{0,8},{8,0},{16,24},{24,16},{1,9},{9,1},{17,25},{25,17},{2,10},{10... | collective-permute-start | bytes 1572872 | tf_op jit(solution)/shard_map/ppermute | solution.py:33
  350.6 12.2 %collective-permute-start.54 = (bf16[128,2048]{1,0:T(8,128)(2,1)}, bf16[128,2048]{1,0:T(8,128)(2,1)S(1)}, u32[]{:S(2)}, u32[]{:S(2)}) collective-permute-start(bf16[128,2048]{1,0:T(8,128)(2,1)} %get-tuple-element.250), channel_id=1, source_target_pairs={{0,4},{2,6},{4,0},{6,2},{1,5},{3,7},{5,1},{7,3},{8,12},{10,14},{12... | collective-permute-start | bytes 1572872 | tf_op jit(solution)/shard_map/ppermute | solution.py:33
  351.9 10.9 %collective-permute-start.55 = (bf16[128,2048]{1,0:T(8,128)(2,1)}, bf16[128,2048]{1,0:T(8,128)(2,1)S(1)}, u32[]{:S(2)}, u32[]{:S(2)}) collective-permute-start(bf16[128,2048]{1,0:T(8,128)(2,1)} %get-tuple-element.251), channel_id=1, source_target_pairs={{0,24},{8,16},{16,8},{24,0},{1,25},{9,17},{17,9},{25,1},{2,26},{10... | collective-permute-start | bytes 1572872 | tf_op jit(solution)/shard_map/ppermute | solution.py:33
  377.6 57.6 %collective-permute-start.105 = (bf16[1024,640]{1,0:T(8,128)(2,1)}, bf16[1024,640]{1,0:T(8,128)(2,1)}, u32[]{:S(2)}, u32[]{:S(2)}) collective-permute-start(bf16[1024,640]{1,0:T(8,128)(2,1)} %fusion.14), channel_id=1, source_target_pairs={{0,1},{1,0},{2,3},{3,2},{4,5},{5,4},{6,7},{7,6},{8,9},{9,8},{10,11... | collective-permute-start | bytes 3932168 | tf_op jit(solution)/shard_map/ppermute | solution.py:33
  388.2 114.1 %collective-permute-start.104 = (bf16[1024,1408]{1,0:T(8,128)(2,1)}, bf16[1024,1408]{1,0:T(8,128)(2,1)}, u32[]{:S(2)}, u32[]{:S(2)}) collective-permute-start(bf16[1024,1408]{1,0:T(8,128)(2,1)} %convolution_convert_fusion), channel_id=1, source_target_pairs={{0,1},{1,0},{2,3},{3,2},{4,5},{5,4},{6,7},{7,6},{8,9},{9,8},{10,11... | collective-permute-start | bytes 8650760 | tf_op jit(solution)/shard_map/ppermute | solution.py:33
  474.8 13.6 %all-to-all-start.5 = ((f32[16,16,128]{2,1,0:T(8,128)}), f32[16,16,128]{2,1,0:T(8,128)}, u32[]{:S(2)}, u32[]{:S(2)}) async-start(f32[16,16,128]{2,1,0:T(8,128)} %broadcast_in_dim.29), calls=%async_computation.5 | async-start | bytes 262144 | tf_op jit(solution)/shard_map/all_to_all | solution.py:49
  480.3 198.2 %reduce-scatter.3.cloned.1.call-start = ((), (), s32[]{:S(2)}) async-start(), calls=%async_computation.10 | async-start | bytes 3604480 | tf_op jit(solution)/shard_map/reduce_scatter | solution.py:482
  483.2 30.8 %collective-permute-start.108 = (bf16[1024,128]{0,1:T(8,128)(2,1)}, bf16[1024,128]{0,1:T(8,128)(2,1)}, u32[]{:S(2)}, u32[]{:S(2)}) collective-permute-start(bf16[1024,128]{0,1:T(8,128)(2,1)} %fusion.27), channel_id=1, source_target_pairs={{0,1},{1,0},{2,3},{3,2},{4,5},{5,4},{6,7},{7,6},{8,9},{9,8},{10,11... | collective-permute-start | bytes 786440 | tf_op jit(solution)/shard_map/ppermute | solution.py:33
  501.8 14.5 %collective-permute-start.107 = (bf16[1024,384]{0,1:T(8,128)(2,1)}, bf16[1024,384]{0,1:T(8,128)(2,1)}, u32[]{:S(2)}, u32[]{:S(2)}) collective-permute-start(bf16[1024,384]{0,1:T(8,128)(2,1)} %fusion.21), channel_id=1, source_target_pairs={{0,1},{1,0},{2,3},{3,2},{4,5},{5,4},{6,7},{7,6},{8,9},{9,8},{10,11... | collective-permute-start | bytes 2359304 | tf_op jit(solution)/shard_map/ppermute | solution.py:33
  521.3 34.1 %all-to-all-start.7 = ((bf16[16,64,640]{2,1,0:T(8,128)(2,1)}), bf16[16,64,640]{2,1,0:T(8,128)(2,1)S(1)}, u32[]{:S(2)}, u32[]{:S(2)}) async-start(bf16[16,64,640]{2,1,0:T(8,128)(2,1)} %bitcast.157), calls=%async_computation.9 | async-start | bytes 2621440 | tf_op jit(solution)/shard_map/all_to_all | solution.py:49
  556.5 135.6 %all-to-all-start.4 = ((bf16[16,64,2048]{2,1,0:T(8,128)(2,1)}), bf16[16,64,2048]{2,1,0:T(8,128)(2,1)}, u32[]{:S(2)}, u32[]{:S(2)}) async-start(bf16[16,64,2048]{2,1,0:T(8,128)(2,1)} %bitcast.146), calls=%async_computation.4 | async-start | bytes 8388608 | tf_op jit(solution)/shard_map/all_to_all | solution.py:49
  564.3 66.4 %collective-permute-start.86 = (bf16[128,2048]{1,0:T(8,128)(2,1)}, bf16[128,2048]{1,0:T(8,128)(2,1)S(1)}, u32[]{:S(2)}, u32[]{:S(2)}) collective-permute-start(bf16[128,2048]{1,0:T(8,128)(2,1)} %get-tuple-element.305), channel_id=1, source_target_pairs={{0,6},{2,4},{4,2},{6,0},{1,7},{3,5},{5,3},{7,1},{8,14},{10,12},{12... | collective-permute-start | bytes 1572872 | tf_op jit(solution)/shard_map/ppermute | solution.py:33
  567.4 63.3 %collective-permute-start.87 = (bf16[128,2048]{1,0:T(8,128)(2,1)}, bf16[128,2048]{1,0:T(8,128)(2,1)S(1)}, u32[]{:S(2)}, u32[]{:S(2)}) collective-permute-start(bf16[128,2048]{1,0:T(8,128)(2,1)} %copy-done.76), channel_id=1, source_target_pairs={{0,8},{8,0},{16,24},{24,16},{1,9},{9,1},{17,25},{25,17},{2,10},{10... | collective-permute-start | bytes 1572872 | tf_op jit(solution)/shard_map/ppermute | solution.py:33
  568.9 61.8 %collective-permute-start.88 = (bf16[128,2048]{1,0:T(8,128)(2,1)}, bf16[128,2048]{1,0:T(8,128)(2,1)S(1)}, u32[]{:S(2)}, u32[]{:S(2)}) collective-permute-start(bf16[128,2048]{1,0:T(8,128)(2,1)} %copy-done.75), channel_id=1, source_target_pairs={{0,4},{2,6},{4,0},{6,2},{1,5},{3,7},{5,1},{7,3},{8,12},{10,14},{12... | collective-permute-start | bytes 1572872 | tf_op jit(solution)/shard_map/ppermute | solution.py:33
  569.1 61.6 %collective-permute-start.89 = (bf16[128,2048]{1,0:T(8,128)(2,1)}, bf16[128,2048]{1,0:T(8,128)(2,1)S(1)}, u32[]{:S(2)}, u32[]{:S(2)}) collective-permute-start(bf16[128,2048]{1,0:T(8,128)(2,1)} %copy-done.74), channel_id=1, source_target_pairs={{0,24},{8,16},{16,8},{24,0},{1,25},{9,17},{17,9},{25,1},{2,26},{10... | collective-permute-start | bytes 1572872 | tf_op jit(solution)/shard_map/ppermute | solution.py:33
  680.9 17.9 %collective-permute-start.106 = (bf16[4,64,2048]{2,1,0:T(8,128)(2,1)}, bf16[4,64,2048]{2,1,0:T(8,128)(2,1)}, u32[]{:S(2)}, u32[]{:S(2)}) collective-permute-start(bf16[4,64,2048]{2,1,0:T(8,128)(2,1)} %pad_maximum_fusion.2), channel_id=1, source_target_pairs={{0,0},{1,4},{4,1},{5,5},{2,2},{3,6},{6,3},{7,7},{8,8},{9,12},{12,9... | collective-permute-start | bytes 3145736 | tf_op jit(solution)/shard_map/ppermute | solution.py:37
  698.8 17.2 %all-to-all-start.6 = ((bf16[4,64,2048]{2,1,0:T(8,128)(2,1)}), bf16[4,64,2048]{2,1,0:T(8,128)(2,1)S(1)}, u32[]{:S(2)}, u32[]{:S(2)}) async-start(bf16[4,64,2048]{2,1,0:T(8,128)(2,1)} %collective-permute-done.106), calls=%async_computation.8 | async-start | bytes 2097152 | tf_op jit(solution)/shard_map/all_to_all | solution.py:49
  712.3 15.3 %collective-permute-start.85 = (bf16[128,2048]{1,0:T(8,128)(2,1)}, bf16[128,2048]{1,0:T(8,128)(2,1)}, u32[]{:S(2)}, u32[]{:S(2)}) collective-permute-start(bf16[128,2048]{1,0:T(8,128)(2,1)} %maximum_select_fusion.3), channel_id=1, source_target_pairs={{0,1},{1,0},{2,3},{3,2},{4,5},{5,4},{6,7},{7,6},{8,9},{9,8},{10,11... | collective-permute-start | bytes 1572872 | tf_op jit(solution)/shard_map/ppermute | solution.py:33
  (192 other events, 1645.5 us)
Sparse Core Ops, SparseCore 0:
  54.4 67.6 all-gather.2
  440.4 23.0 reduce-scatter.4
  511.1 44.0 reduce-scatter.2

commit v3 on v2

v3 whole, which is shorter than its diff:
```python
import math

import jax
import jax.numpy as jnp
import numpy as np
from jax import lax
from jax.experimental import pallas as pl
from jax.experimental.pallas import tpu as pltpu
from jax.sharding import Mesh
from jax.sharding import PartitionSpec as P

EPSILON = 1e-05
ROPE_BASE = 10000.0
SCALE = 128 ** (-0.5)
BF = jnp.bfloat16
F32 = jnp.float32
HIGHEST = lax.Precision.HIGHEST

AXES = ("x", "z", "yl", "yh", "c")
SIZES = (4, 4, 2, 2, 2)
CONTEXT = ("z", "yl")
TENSOR = ("yh", "c")
WEIGHT = ("x", "z", "yl")
GROUP = ("z", "yl", "yh")
Y = ("yl", "yh")
SWAP = ("yl", "c")
VMEM = pl.BlockSpec(memory_space=pltpu.VMEM)
SMEM = pl.BlockSpec(memory_space=pltpu.SMEM)
ANY = pl.BlockSpec(memory_space=pl.ANY)
MIB = 1024 * 1024


def exchange(axes, size, mask):
    pairs = [(at, at ^ mask) for at in range(size)]
    return lambda v: lax.ppermute(v, axes, pairs)


CUBE = (exchange("z", 4, 1), exchange(Y, 4, 2), exchange("z", 4, 3), exchange(Y, 4, 3))
ALONG_Z = (exchange("z", 4, 1), exchange("z", 4, 3), exchange("z", 4, 2))
ALONG_Y = (exchange(Y, 4, 2), exchange(Y, 4, 3), exchange(Y, 4, 1))
X_PAIR, X_ACROSS = exchange("x", 4, 1), exchange("x", 4, 3)
swap_cores = lambda v: lax.ppermute(v, SWAP, [(0, 0), (1, 2), (2, 1), (3, 3)])
other_core = exchange("c", 2, 1)
other_half = exchange("yh", 2, 1)


def dot(a, b, left=1, right=0, precision=None):
    return lax.dot_general(
        a, b, (((left,), (right,)), ((), ())), preferred_element_type=F32, precision=precision
    )


def all_to_all(v, axes):
    return lax.all_to_all(v, axes, split_axis=0, concat_axis=0, tiled=True)


def kernel_call(body, outs, in_specs, limit, flops=0, scratch=(), earlier=()):
    def whole_body(*refs):
        body(*refs[len(earlier) :])

    call = pl.pallas_call(
        whole_body,
        out_shape=[jax.ShapeDtypeStruct(shape, kind) for shape, kind in outs],
        in_specs=[ANY] * len(earlier) + in_specs,
        out_specs=[VMEM] * len(outs),
        scratch_shapes=list(scratch),
        compiler_params=pltpu.CompilerParams(vmem_limit_bytes=limit * MIB),
        cost_estimate=pl.CostEstimate(flops=flops, bytes_accessed=4 * MIB, transcendentals=0),
    )
    return lambda *args: call(*earlier, *args)


PIECE = ((128, 2048), BF)
HEAD = ((1024, 128), BF)
WIDE_HEAD = ((1024, 128), F32)


def rows_at(places, at):
    return pl.ds(pl.multiple_of(places[at] * 16, 16), 16)


def join_kernel(*refs):
    half, cuts = refs[0].shape[0], len(refs[8:]) // 4
    for i in range(4):
        at = 0
        for out in refs[8 + cuts * i : 8 + cuts * i + cuts]:
            columns = slice(at, at + out.shape[1])
            out[:half, :] = refs[i][:, columns]
            out[half:, :] = refs[4 + i][:, columns]
            at += out.shape[1]


def join(parts, arrived, widths, earlier=()):
    rows = 2 * parts[0].shape[0]
    outs = [((rows, width), BF) for width in widths] * 4
    return kernel_call(join_kernel, outs, [VMEM] * 8, 16, earlier=earlier)(*parts, *arrived)


def cube_step(parts, step):
    return [CUBE[(i + step) % 4](parts[i]) for i in range(4)]


def cube_gather(parts, seen=None):
    parts = list(parts)
    for step in range(3):
        arrived = cube_step(parts, step)
        parts = join(parts, arrived, [parts[0].shape[1]])
        if seen is not None:
            seen.append(arrived)
    return list(parts) + cube_step(parts, 3)


def pick_kernel(ids, blocks, *outs):
    for mask, out in zip((0, 1, 3, 2), outs):
        out[...] = blocks[pl.ds(ids[3] ^ mask, 1)]


def place_kernel(ids, own, a, b, c, out):
    for mask, held in zip((0, 1, 3, 2), (own, a, b, c)):
        out[pl.ds(ids[3] ^ mask, 1)] = held[...]


def pair_kernel(bit, ids, own, far, out):
    rows = own.shape[0]
    here = pl.multiple_of(ids[bit] * rows, rows)
    out[pl.ds(here, rows), :] = own[...]
    out[pl.ds(rows - here, rows), :] = far[...]


def pair(bit, ids, own, far):
    rows, width = own.shape
    return kernel_call(
        lambda *refs: pair_kernel(bit, *refs),
        [((2 * rows, width), BF)],
        [SMEM] + [VMEM] * 2,
        max(4, rows * width * 8 // MIB + 2),
    )(ids, own, far)[0]


def split_kernel(bit, ids, a, b, keep, send):
    rows = keep.shape[0]
    here = pl.multiple_of(ids[bit] * rows, rows)
    for out, at in ((keep, here), (send, rows - here)):
        for n in range(0, rows, 64):
            held = pl.ds(pl.multiple_of(at + n, 64), 64)
            out[n : n + 64, :] = (a[held, :].astype(F32) + b[held, :].astype(F32)).astype(BF)


def split(bit, ids, a, b):
    rows, width = a.shape
    return kernel_call(
        lambda *refs: split_kernel(bit, *refs),
        [((rows // 2, width), BF)] * 2,
        [SMEM] + [VMEM] * 2,
        max(4, rows * width * 8 // MIB + 2),
    )(ids, a, b)


def line_exchange(blocks, ids):
    sent = kernel_call(pick_kernel, [((1,) + blocks.shape[1:], BF)] * 4, [SMEM, VMEM], 8)(
        ids, blocks
    )
    arrived = [move(held) for move, held in zip(ALONG_Z, sent[1:])]
    return kernel_call(
        place_kernel, [(blocks.shape, BF)], [SMEM] + [VMEM] * 4, 8
    )(ids, sent[0], *arrived)[0]


def token_terms(stats):
    held = stats + ALONG_Z[0](stats) + ALONG_Z[1](stats) + ALONG_Z[2](stats)
    return [held] + [move(held) for move in ALONG_Y]


def fold_kernel(*refs):
    half = refs[0].shape[0] // 2
    for i in range(4):
        kept, arrived, keep, send = refs[i], refs[4 + i], refs[8 + i], refs[12 + i]
        keep[...] = (kept[:half, :].astype(F32) + arrived[:half, :].astype(F32)).astype(BF)
        send[...] = (kept[half:, :].astype(F32) + arrived[half:, :].astype(F32)).astype(BF)


def cube_scatter(pieces, seen=None):
    kept, sent = pieces[:4], pieces[4:]
    for step in (3, 2, 1, 0):
        arrived = cube_step(sent, step)
        if seen is not None:
            seen.append(arrived)
        if step:
            half = ((kept[0].shape[0] // 2, kept[0].shape[1]), BF)
            folded = kernel_call(fold_kernel, [half] * 8, [VMEM] * 8, 16)(*kept, *arrived)
            kept, sent = folded[:4], folded[4:]
    return list(kept) + arrived


def block_places():
    at = jnp.arange(64, dtype=jnp.int32)
    part, block = (at >> 3) & 3, (at & 7) | ((at >> 5) << 3)
    turned = [(block >> ((dim - part) & 3)) & 1 for dim in range(4)]
    z = lax.axis_index("z") ^ (turned[0] ^ (3 * turned[2]))
    y = (2 * lax.axis_index("yh") + lax.axis_index("yl")) ^ (turned[1] ^ (3 * turned[3]))
    return ((2 * z + (y & 1)) * 2 + (y >> 1)) * 4 + part


def put_pieces(places, pieces, out):
    for k, piece in enumerate(pieces):
        for j in range(8):
            out[rows_at(places, 8 * k + j), :] = piece[16 * j : 16 * j + 16, :]


def take_rows(places, source, out, start=0):
    for n in range(out.shape[0] // 16):
        out[16 * n : 16 * n + 16, :] = source[rows_at(places, start + n), :]


def project(rows, near, far, columns, pieces, start=0):
    for b in range(len(pieces) // 2):
        held = rows[256 * b : 256 * b + 256, :]
        for at, weight in enumerate((near, far)):
            wide = dot(held, weight[:, columns], 1, 1).astype(BF)
            place = slice(start + 1024 * at, start + 1024 * at + 1024)
            for k in range(2):
                pieces[2 * b + k][:, place] = wide[128 * k : 128 * k + 128]


def natural_order(near, core, out):
    first = lax.broadcasted_iota(jnp.int32, (near.shape[0], 128), 1) < 64
    for j in range(8):
        mine = near[:, 128 * j : 128 * j + 128]
        other = near[:, 1024 + 128 * j : 1024 + 128 * j + 128]
        low = jnp.where(core == 0, mine, other)
        high = jnp.where(core == 0, other, mine)
        out[:, 256 * j : 256 * j + 128] = jnp.where(first, low, pltpu.roll(high, 64, 1)).astype(BF)
        out[:, 256 * j + 128 : 256 * j + 256] = jnp.where(
            first, pltpu.roll(low, 64, 1), high
        ).astype(BF)


def prepare_kernel(ids, places, length, tokens, cot, routes, own_tokens, own_cot, p0, p1, p2, p3, wide):
    core, parts = ids[0], (p0, p1, p2, p3)
    first = lax.broadcasted_iota(jnp.int32, (64, 128), 1) < 64
    for source, out, at in ((tokens, own_tokens, 0), (cot, own_cot, 2048)):
        for j in range(8):
            a = source[0, :, 256 * j : 256 * j + 128].astype(F32)
            b = source[0, :, 256 * j + 128 : 256 * j + 256].astype(F32)
            low = jnp.where(first, a, pltpu.roll(b, 64, 1))
            high = jnp.where(first, pltpu.roll(a, 64, 1), b)
            out[:, 128 * j : 128 * j + 128] = jnp.where(core == 0, low, high).astype(BF)
            out[:, 1024 + 128 * j : 1152 + 128 * j] = jnp.where(core == 0, high, low).astype(BF)
        for i in range(4):
            parts[i][:, at : at + 2048] = out[16 * i : 16 * i + 16, :]
    expert = lax.broadcasted_iota(jnp.int32, (128, 128), 0)
    chosen = jnp.zeros((128, 128), F32)
    for k in range(8):
        chosen += (expert == routes[0, k : k + 1, :]).astype(F32)
    wide[...] = dot(chosen.astype(BF), identity(128, BF), 0, 0)
    for i in range(4):
        rows = pl.ds(pl.multiple_of(ids[1] * 64 + 16 * i, 16), 16)
        parts[i][:, 4096:] = wide[rows, :].astype(BF)


def prepare(ids, places, length, tokens, cot, routes):
    own = lambda n, ids: (ids[0], ids[1], 0)
    whole = lambda n, ids: (0, 0)
    return pl.pallas_call(
        prepare_kernel,
        grid_spec=pltpu.PrefetchScalarGridSpec(
            num_scalar_prefetch=1,
            grid=(1,),
            in_specs=[
                SMEM,
                SMEM,
                pl.BlockSpec((1, 64, 2048), own),
                pl.BlockSpec((1, 64, 2048), own),
                pl.BlockSpec((1, 8, 128), lambda n, ids: (ids[0], 0, 0)),
            ],
            out_specs=[pl.BlockSpec((64, 2048), whole)] * 2 + [pl.BlockSpec((16, 4224), whole)] * 4,
            scratch_shapes=[pltpu.VMEM((128, 128), F32)],
        ),
        out_shape=[jax.ShapeDtypeStruct((64, 2048), BF)] * 2
        + [jax.ShapeDtypeStruct((16, 4224), BF)] * 4,
        compiler_params=pltpu.CompilerParams(vmem_limit_bytes=8 * MIB),
    )(ids, places, length, tokens, cot, routes)


def identity(size, kind):
    row = lax.broadcasted_iota(jnp.int32, (size, size), 0)
    return (row == lax.broadcasted_iota(jnp.int32, (size, size), 1)).astype(kind)


def first_pack_kernel(query, key, value, w_out, attn_gain, mlp_gain, q_gain, k_gain, out):
    row = lax.broadcasted_iota(jnp.int32, (64, 128), 0)
    lane = lax.broadcasted_iota(jnp.int32, (64, 128), 1)
    extra = jnp.zeros((64, 128), F32)
    for at, gain in enumerate((attn_gain, mlp_gain)):
        column = jnp.sum(gain[...].astype(F32) * identity(64, F32), axis=1, keepdims=True)
        extra = jnp.where(lane == at, column, extra)
    for k in range(4):
        columns = slice(128 * k, 128 * k + 128)
        for at, w in ((0, query), (128, key), (256, value), (512, w_out)):
            out[k, :, at : at + 128] = w[:, columns]
        held = extra
        for at, gain in enumerate((q_gain, k_gain)):
            for j in range(4):
                here = jnp.logical_and(row == j, lane == 2 + at)
                held = jnp.where(here, gain[k : k + 1, j : j + 1].astype(F32), held)
        out[k, :, 384:512] = held.astype(BF)


def second_pack_kernel(gate, up, down, router, out):
    lane = lax.broadcasted_iota(jnp.int32, (64, 128), 1)
    routed = jnp.zeros((64, 128), F32)
    for e in range(10):
        column = jnp.sum(
            router[e : e + 1, :].astype(F32) * identity(64, F32), axis=1, keepdims=True
        )
        routed = jnp.where(lane == e, column, routed)
    for k in range(4):
        for m in range(5):
            tile = 5 * k + m
            columns = slice(128 * (tile % 2), 128 * (tile % 2) + 128)
            for w, at in ((gate, 0), (up, 640), (down, 1408)):
                out[k, :, at + 128 * m : at + 128 * m + 128] = w[tile // 2, :, columns]
        out[k, :, 1280:1408] = routed.astype(BF)


def second_unpack_kernel(grads, gate, up, router, gate_out, up_out, down_out, small):
    part = jnp.zeros((64, 1), F32)
    routed = jnp.zeros((64, 128), F32)
    for k in range(4):
        for m in range(5):
            tile = 5 * k + m
            expert, columns = tile // 2, slice(128 * (tile % 2), 128 * (tile % 2) + 128)
            for w, out, at in ((gate, gate_out, 0), (up, up_out, 640), (None, down_out, 1408)):
                held = grads[k, :, at + 128 * m : at + 128 * m + 128].astype(F32)
                out[expert, :, columns] = held
                if w is not None:
                    held = held * w[expert, :, columns].astype(F32)
                    part += jnp.sum(held, axis=1, keepdims=True)
        routed += grads[k, :, 1280:1408].astype(F32)
    weights = dot(identity(64, BF), router[...], 1, 1)
    part += jnp.sum(routed[:, :10] * weights, axis=1, keepdims=True)
    lane = lax.broadcasted_iota(jnp.int32, (64, 128), 1)
    small[...] = jnp.where(lane < 10, routed, 0.0) + jnp.where(lane == 10, part, 0.0)


def first_unpack_kernel(grads, query, key, value, query_out, key_out, value_out, out_out, small):
    part = jnp.zeros((64, 1), F32)
    for k in range(4):
        columns = slice(128 * k, 128 * k + 128)
        for at, (w, out) in enumerate(((query, query_out), (key, key_out), (value, value_out))):
            held = grads[k, :, 128 * at : 128 * at + 128].astype(F32)
            out[:, columns] = held
            part += jnp.sum(held * w[:, columns].astype(F32), axis=1, keepdims=True)
        out_out[:, columns] = grads[k, :, 384:512].astype(F32)
    small[...] = jnp.broadcast_to(part, (64, 128))


def as_column(rows):
    eye = identity(128, F32)
    return [
        jnp.sum(rows[n : n + 1, :] * eye, axis=1, keepdims=True) for n in range(rows.shape[0])
    ]


def row_sums(v):
    return dot(jnp.ones((8, 128), F32), v, 1, 1, HIGHEST)[0:1]


def put_sums(stats, at, b, row):
    for half in range(2):
        place = 8 * at + 2 * b + half
        stats[place : place + 1, :] = row[:, 128 * half : 128 * half + 128]


def gain_places(core, at):
    row = lax.broadcasted_iota(jnp.int32, (1024, 128), 0)
    element = lax.broadcasted_iota(jnp.int32, (1024, 128), 1)
    yl = core if at == 0 else 1 - core
    here = ((row >> 6) * 2 + yl) * 4 + (row & 63) == element
    return jnp.where(jnp.logical_and(here, (row & 63) < 4), 1.0, 0.0).astype(BF)


def enter_kernel(places, *refs):
    pieces, (ids, near, far, normed, qkv, stats, lines, gains) = refs[:8], refs[8:]
    eye = identity(128, F32)
    for at, weight in enumerate((near, far)):
        for b in range(8):
            held = weight[128 * b : 128 * b + 128, 384:512].astype(F32)
            for n in range(2):
                line = jnp.sum(held[:, n : n + 1] * eye, axis=0, keepdims=True)
                lines[n : n + 1, 1024 * at + 128 * b : 1024 * at + 128 * b + 128] = line
    total = jnp.zeros((128, 128), F32)
    for at, weight in enumerate((near, far)):
        total += dot(weight[:, 384:512], gain_places(ids[0], at), 0, 0)
    gains[...] = total[2:4, :]
    gain = lines.at[0:1, :]
    for k in range(8):

        def norm_rows(j, _):
            held = pieces[k][pl.ds(pl.multiple_of(j * 16, 16), 16), :].astype(F32)
            rate = lax.rsqrt(jnp.mean(held * held, axis=1, keepdims=True) + EPSILON)
            normed[rows_at(places, 8 * k + j), :] = (held * rate * gain[...]).astype(BF)
            return 0

        lax.fori_loop(0, 8, norm_rows, 0)
    for b in range(4):
        rows = slice(256 * b, 256 * b + 256)
        held = dot(normed[rows, :1024], near[:, :384]) + dot(normed[rows, 1024:], far[:, :384])
        qkv[rows, :] = held
        for at in range(2):
            columns = slice(128 * at, 128 * at + 128)
            put_sums(stats, at, b, row_sums(held[:, columns] * held[:, columns]))


def allowed_block(length, at):
    q_pos = 256 * at + lax.broadcasted_iota(jnp.int32, (256, 256 * at + 256), 0)
    k_pos = lax.broadcasted_iota(jnp.int32, (256, 256 * at + 256), 1)
    return jnp.logical_and(k_pos <= q_pos, k_pos < length[0])


def forward_kernel(
    places, length, qkv, s0, s1, s2, s3, gains, cosine, sine, near, far,
    rates, queries, keys, values, attended, log_total, *rest,
):
    pieces, ordered = rest[:8], rest[8]
    for n, column in enumerate(as_column((s0[...] + s1[...]) + (s2[...] + s3[...]))):
        rate = lax.rsqrt(column * (1.0 / 2048) + EPSILON)
        rates[128 * (n % 8) : 128 * (n % 8) + 128, n // 8 : n // 8 + 1] = rate

    def turn(held):
        return held * cosine[...] + pltpu.roll(held, 64, 1) * sine[...]

    queries[...] = turn(qkv[:, :128] * rates[:, 0:1] * gains[0:1, :]).astype(BF)
    keys[...] = turn(qkv[:, 128:256] * rates[:, 1:2] * gains[1:2, :]).astype(BF)
    values[...] = qkv[:, 256:].astype(BF)
    for at in range(4):
        rows, upto = slice(256 * at, 256 * at + 256), slice(0, 256 * at + 256)
        scores = dot(queries[rows, :], keys[upto, :], 1, 1) * SCALE
        scores = jnp.where(allowed_block(length, at), scores, -1e30)
        peak = jnp.max(scores, axis=1, keepdims=True)
        raised = jnp.exp(scores - peak)
        total = jnp.sum(raised, axis=1, keepdims=True)
        probs = (raised * (1.0 / total)).astype(BF)
        attended[rows, :] = dot(probs, values[upto, :]).astype(BF)
        log_total[rows, :] = peak + jnp.log(total)
    take_rows(places, attended, ordered)
    project(ordered, near, far, slice(512, 640), pieces)


def middle_kernel(*refs):
    terms, (own, gain, middle), outs = refs[:8], refs[8:11], refs[11:]
    for i in range(4):
        rows = slice(16 * i, 16 * i + 16)
        held = own[rows, :].astype(F32) + (terms[i][...].astype(F32) + terms[4 + i][...].astype(F32))
        middle[rows, :] = held
        rate = lax.rsqrt(jnp.mean(held * held, axis=1, keepdims=True) + EPSILON)
        outs[i][...] = (held * rate * gain[...]).astype(BF)


def mixture_kernel(places, length, ids, *refs):
    arrays, scratch = refs[:30], refs[30:]
    sources, outs = arrays[:18], arrays[18:]
    held, (mixed, grad_out, gated, hidden_grad), made = scratch[:18], scratch[18:22], scratch[22:30]
    chosen_rows, ordered, gated_ordered, spread, in_sems, out_sems = scratch[30:]
    loads = [
        pltpu.make_async_copy(source, target, in_sems.at[n])
        for n, (source, target) in enumerate(zip(sources, held))
    ]
    stores = [
        pltpu.make_async_copy(source, target, out_sems.at[n])
        for n, (source, target) in enumerate(
            zip((mixed, grad_out, gated, hidden_grad) + tuple(made), outs)
        )
    ]
    for load in loads:
        load.start()
    pieces, routed, (near, far) = held[:8], held[8:16], held[16:]
    expert = lax.broadcasted_iota(jnp.int32, (128, 640), 0)
    tile = 5 * ids[3] + (lax.broadcasted_iota(jnp.int32, (128, 640), 1) >> 7)
    spread[...] = ((tile >> 1) == expert).astype(F32)
    for load in loads[:8]:
        load.wait()
    put_pieces(places, pieces, mixed)
    stores[0].start()
    for load in loads[8:16]:
        load.wait()
    row = lax.broadcasted_iota(jnp.int32, (16, 1), 0)
    for k, piece in enumerate(routed):
        for j in range(8):
            rows = rows_at(places, 8 * k + j)
            inside = row < length[0] - places[8 * k + j] * 16
            kept = piece[16 * j : 16 * j + 16, :2048]
            grad_out[rows, :] = jnp.where(inside, kept, jnp.zeros((), BF))
            chosen_rows[rows, :] = piece[16 * j : 16 * j + 16, 2048:]
    stores[1].start()
    for load in loads[16:]:
        load.wait()
    lane = lax.broadcasted_iota(jnp.int32, (256, 128), 1)

    def block(b, _):
        rows = pl.ds(pl.multiple_of(b * 256, 256), 256)
        chosen = chosen_rows[rows, :].astype(F32)
        hidden = dot(mixed[rows, :1024], near[:, :1408]) + dot(mixed[rows, 1024:], far[:, :1408])
        out_grad = dot(grad_out[rows, :1024], near[:, 1408:]) + dot(
            grad_out[rows, 1024:], far[:, 1408:]
        )
        gate_h, up_h = hidden[:, :640], hidden[:, 640:1280]
        logits = jnp.where(lane < 10, hidden[:, 1280:], -1e30)
        raised = jnp.exp(logits - jnp.max(logits, axis=1, keepdims=True))
        route_probs = raised / jnp.sum(raised, axis=1, keepdims=True)
        gates = dot(route_probs * chosen, spread[...], 1, 0, HIGHEST)
        sig = 1.0 / (1.0 + jnp.exp(-gate_h))
        silu = gate_h * sig
        activated = (silu * up_h).astype(BF).astype(F32)
        gated[rows, :] = (activated * gates).astype(BF)
        act_grad = out_grad * gates
        hidden_grad[rows, :640] = (act_grad * up_h * sig * (1.0 + gate_h * (1.0 - sig))).astype(BF)
        hidden_grad[rows, 640:1280] = (act_grad * silu).astype(BF)
        chosen_grad = dot(activated * out_grad, spread[...], 1, 1, HIGHEST) * chosen
        inner = jnp.sum(chosen_grad * route_probs, axis=1, keepdims=True)
        hidden_grad[rows, 1280:] = (route_probs * (chosen_grad - inner)).astype(BF)
        return 0

    lax.fori_loop(0, 4, block, 0)
    stores[2].start()
    stores[3].start()
    for first in (4, 0):
        outs = made[first : first + 4]
        take_rows(places, hidden_grad, ordered, 8 * first)
        project(ordered, near, far, slice(0, 1408), outs)
        take_rows(places, gated, gated_ordered, 8 * first)
        project(gated_ordered, near, far, slice(1408, 2048), outs, 2048)
        for store in stores[4 + first : 8 + first]:
            store.start()
    for store in stores:
        store.wait()


def middle_grad_kernel(ids, length, *refs):
    terms, (middle, cot, gain, middle_grad, output), outs = refs[:8], refs[8:13], refs[13:]
    for i in range(4):
        rows = slice(16 * i, 16 * i + 16)
        inside = ids[2] + 16 * i + lax.broadcasted_iota(jnp.int32, (16, 1), 0) < length[0]
        grad = jnp.where(inside, cot[rows, :].astype(F32), 0.0)
        summed = terms[i][...].astype(F32) + terms[4 + i][...].astype(F32)
        scaled = summed[:, :2048] * gain[...]
        held = middle[rows, :]
        rate = lax.rsqrt(jnp.mean(held * held, axis=1, keepdims=True) + EPSILON)
        inner = jnp.mean(scaled * held, axis=1, keepdims=True)
        total = grad + rate * scaled - held * (rate * rate * rate * inner)
        middle_grad[rows, :] = total
        outs[i][...] = total.astype(BF)
        natural_order(held + summed[:, 2048:], ids[0], output.at[rows, :])


def backward_kernel(places, length, *refs):
    pieces, refs = refs[:8], refs[8:]
    (near, far, qkv, rates, gains, cosine, sine, queries, keys, values, log_total) = refs[:11]
    (branch, q_scaled, k_scaled, v_grad, inner, gain_grads) = refs[11:17]
    grad, key_grad, value_grad = refs[17:]

    def turn_back(held):
        return held * cosine[...] - pltpu.roll(held, 64, 1) * sine[...]

    put_pieces(places, pieces, branch)
    key_grad[...] = jnp.zeros_like(key_grad)
    value_grad[...] = jnp.zeros_like(value_grad)
    for at in range(4):
        rows, upto = slice(256 * at, 256 * at + 256), slice(0, 256 * at + 256)
        held = dot(branch[rows, :1024], near[:, 512:]) + dot(branch[rows, 1024:], far[:, 512:])
        grad[rows, :] = held.astype(BF)
        scores = dot(queries[rows, :], keys[upto, :], 1, 1) * SCALE
        probs = jnp.where(allowed_block(length, at), jnp.exp(scores - log_total[rows, :]), 0.0)
        prob_grad = dot(grad[rows, :], values[upto, :], 1, 1)
        delta = jnp.sum(probs * prob_grad, axis=1, keepdims=True)
        score_grad = (probs * (prob_grad - delta)).astype(BF)
        q_scaled[rows, :] = dot(score_grad, keys[upto, :]) * SCALE
        key_grad[upto, :] += dot(score_grad, queries[rows, :], 0, 0) * SCALE
        value_grad[upto, :] += dot(probs.astype(BF), grad[rows, :], 0, 0)
    v_grad[...] = value_grad[...].astype(BF)
    q_norm_grad = turn_back(q_scaled[...])
    k_norm_grad = turn_back(key_grad[...])
    q_turned = q_norm_grad * qkv[:, :128]
    k_turned = k_norm_grad * qkv[:, 128:256]
    gain_grads[0:1, :] = jnp.sum(q_turned * rates[:, 0:1], axis=0, keepdims=True)
    gain_grads[1:2, :] = jnp.sum(k_turned * rates[:, 1:2], axis=0, keepdims=True)
    for at, turned in enumerate((q_turned, k_turned)):
        products = turned * gains[at : at + 1, :]
        for b in range(4):
            put_sums(inner, at, b, row_sums(products[256 * b : 256 * b + 256]))
    q_scaled[...] = q_norm_grad * gains[0:1, :]
    k_scaled[...] = k_norm_grad * gains[1:2, :]


def exit_kernel(
    places, q_scaled, k_scaled, v_grad, qkv, rates, s0, s1, s2, s3, near, far, grad, *rest
):
    pieces, ordered = rest[:8], rest[8]
    for n, column in enumerate(as_column((s0[...] + s1[...]) + (s2[...] + s3[...]))):
        at, rows = n // 8, slice(128 * (n % 8), 128 * (n % 8) + 128)
        columns, scaled = slice(128 * at, 128 * at + 128), (q_scaled, k_scaled)[at]
        rate = rates[rows, at : at + 1]
        factor = rate * rate * rate * column * (1.0 / 2048)
        grad[rows, columns] = (rate * scaled[rows, :] - qkv[rows, columns] * factor).astype(BF)
    grad[:, 256:] = v_grad[...]
    take_rows(places, grad, ordered)
    project(ordered, near, far, slice(0, 384), pieces)


def exit_rest_kernel(places, grad, near, far, *refs):
    take_rows(places, grad, refs[4])
    project(refs[4], near, far, slice(0, 384), refs[:4])


def expert_weights_kernel(mixed, hidden_grad, grad_out, gated, near, far):
    for at, out in enumerate((near, far)):
        for n in range(1024 * at, 1024 * at + 1024, 512):
            rows, columns = slice(n - 1024 * at, n - 1024 * at + 512), slice(n, n + 512)
            out[rows, :1408] = dot(mixed[:, columns], hidden_grad[...], 0, 0).astype(BF)
            out[rows, 1408:] = dot(grad_out[:, columns], gated[...], 0, 0).astype(BF)


def attention_weights_kernel(ids, normed, qkv_grad, branch, attended, gain_grads, near, far):
    gains = jnp.concatenate([gain_grads[...], jnp.zeros((6, 128), F32)], axis=0).astype(BF)
    for at, out in enumerate((near, far)):
        columns = slice(1024 * at, 1024 * at + 1024)
        out[:, :384] = dot(normed[:, columns], qkv_grad[...], 0, 0).astype(BF)
        out[:, 384:512] = dot(branch[:, columns], attended[...], 0, 0).astype(BF)
        out[:, 512:] = jnp.zeros((1024, 128), BF)
        out[:, 512:520] = dot(gain_places(ids[0], at), gains, 1, 1).astype(BF)


def input_grad_kernel(ids, *refs):
    terms, (middle_grad, own, gain, out) = refs[:8], refs[8:]
    for i in range(4):
        rows = slice(16 * i, 16 * i + 16)
        scaled = (terms[i][...].astype(F32) + terms[4 + i][...].astype(F32)) * gain[...]
        held = own[rows, :].astype(F32)
        rate = lax.rsqrt(jnp.mean(held * held, axis=1, keepdims=True) + EPSILON)
        inner = jnp.mean(scaled * held, axis=1, keepdims=True)
        total = middle_grad[rows, :] + rate * scaled - held * (rate * rate * rate * inner)
        natural_order(total, ids[0], out.at[rows, :])


def both_kernel(ids, own, far, out):
    here = pl.multiple_of(ids[1] * 64, 64)
    out[pl.ds(here, 64), :] = own[...]
    out[pl.ds(64 - here, 64), :] = far[...]


def slots_kernel(ids, own, far, out):
    out[pl.ds(ids[0], 1), :, :] = own[...].astype(out.dtype)[None]
    out[pl.ds(1 - ids[0], 1), :, :] = far[...].astype(out.dtype)[None]


def angles(head_size):
    steps_half = np.arange(head_size // 2, dtype=np.float32)
    frequency = np.exp(steps_half * np.float32(-2.0 * math.log(ROPE_BASE) / head_size))
    turned = np.arange(1024, dtype=np.float32)[:, None] * frequency.astype(np.float32)[None, :]
    cosine, sine = np.cos(turned.astype(np.float64)), np.sin(turned.astype(np.float64))
    return (
        jnp.asarray(np.concatenate([cosine, cosine], axis=-1).astype(np.float32)),
        jnp.asarray(np.concatenate([-sine, sine], axis=-1).astype(np.float32)),
    )


def after(value, earlier):
    return lax.optimization_barrier((value, earlier))[0]


def per_device(
    tokens,
    lengths,
    routes,
    attn_gain,
    q_gain,
    k_gain,
    w_query,
    w_key,
    w_value,
    w_out,
    mlp_gain,
    router,
    w_gate,
    w_up,
    w_down,
    cotangent,
):
    z = lax.axis_index("z")
    yh = lax.axis_index("yh")
    core = lax.axis_index("c")

    own_place = (2 * z + lax.axis_index("yl")) * 128 + yh * 64
    x = lax.axis_index("x")
    ids = jnp.stack([core, yh, own_place, z, x & 1, x >> 1]).astype(jnp.int32)
    places = block_places()
    slot_length = lax.dynamic_slice(lengths, (core,), (1,))
    own_tokens, own_cot, *parts = prepare(
        ids, places, slot_length, tokens, cotangent, routes.swapaxes(1, 2)
    )
    (first_pack,) = kernel_call(first_pack_kernel, [((4, 64, 640), BF)], [VMEM] * 8, 8)(
        w_query, w_key, w_value, w_out.T, attn_gain[None], mlp_gain[None], q_gain, k_gain
    )

    swapped = swap_cores(after(first_pack, own_tokens))
    arrived = cube_step(parts, 0)
    parts = join(parts, arrived, [4224])
    held = all_to_all(after(swapped, arrived), "z").reshape(256, 640)
    arrived = cube_step(parts, 1)
    parts = join(parts, arrived, [4224])
    held = after(pair(4, ids, held, X_PAIR(held)), arrived)
    (second_pack,) = kernel_call(
        second_pack_kernel, [((4, 64, 2048), BF)], [VMEM] * 4, 12, earlier=arrived
    )(w_gate, w_up, w_down.swapaxes(1, 2), router.T)
    arrived = cube_step(parts, 2)
    joined = join(parts, arrived, [2048, 2176])
    first = after(pair(5, ids, held, X_ACROSS(held)), arrived)
    first_far = other_core(first)
    token_pieces, routed_pieces = list(joined[0::2]), list(joined[1::2])
    token_pieces += cube_step(token_pieces, 3)
    routed_pieces += cube_step(after(routed_pieces, token_pieces), 3)
    swapped = swap_cores(after(second_pack, token_pieces[4:]))

    normed, qkv, stats, lines, gain_rows = kernel_call(
        enter_kernel,
        [
            ((1024, 2048), BF),
            ((1024, 384), F32),
            ((16, 128), F32),
            ((2, 2048), F32),
            ((2, 128), F32),
        ],
        [SMEM] + [VMEM] * 8 + [SMEM] + [VMEM] * 2,
        24,
        2 * 1024 * 2048 * 384,
    )(places, *token_pieces, ids, first, first_far)
    attn_row, mlp_row = lines[0:1], lines[1:2]
    terms = token_terms(after(stats, routed_pieces[4:]))
    held = line_exchange(after(swapped, terms[0]), ids).reshape(256, 2048)
    cosine, sine = angles(128)
    rates, queries, keys, values, attended, log_total, *pieces = kernel_call(
        forward_kernel,
        [((1024, 2), F32), HEAD, HEAD, HEAD, HEAD, ((1024, 1), F32)] + [PIECE] * 8,
        [SMEM, SMEM] + [VMEM] * 10,
        28,
        4 * 1024 * 1024 * 128,
        [pltpu.VMEM((1024, 128), BF)],
    )(
        places, slot_length, qkv, *terms, gain_rows, cosine, sine, first, first_far
    )
    own_row = ((64, 2048), F32)
    own_part = ((16, 2048), BF)
    held = pair(4, ids, held, X_PAIR(after(held, pieces)))
    seen = []
    terms = cube_scatter(pieces, seen)
    second = pair(5, ids, held, X_ACROSS(after(held, seen[0])))
    middle, *parts = kernel_call(
        middle_kernel, [own_row] + [own_part] * 4, [VMEM] * 10, 8
    )(*terms, own_tokens, mlp_row)

    seen = []
    mixed_pieces = cube_gather(parts, seen)
    second_far = other_core(after(second, seen[1]))
    sums = [((1024, 2048), BF), ((1024, 2048), BF), ((1024, 640), BF), ((1024, 1408), BF)]
    sums += [((128, 4096), BF)] * 8
    taken = [*mixed_pieces, *routed_pieces, second, second_far]
    mixed, grad_out, gated, hidden_grad, *pieces = pl.pallas_call(
        mixture_kernel,
        out_shape=[jax.ShapeDtypeStruct(shape, kind) for shape, kind in sums],
        in_specs=[SMEM] * 3 + [ANY] * 18,
        out_specs=[ANY] * 12,
        scratch_shapes=[pltpu.VMEM(held.shape, BF) for held in taken]
        + [pltpu.VMEM(shape, BF) for shape, _ in sums]
        + [
            pltpu.VMEM((1024, 128), BF),
            pltpu.VMEM((512, 1408), BF),
            pltpu.VMEM((512, 640), BF),
            pltpu.VMEM((128, 640), F32),
            pltpu.SemaphoreType.DMA((18,)),
            pltpu.SemaphoreType.DMA((12,)),
        ],
        compiler_params=pltpu.CompilerParams(vmem_limit_bytes=58 * MIB),
        cost_estimate=pl.CostEstimate(
            flops=2 * 1024 * 2048 * 4096, bytes_accessed=36 * MIB, transcendentals=0
        ),
    )(places, slot_length, ids, *taken)
    seen = []
    terms = cube_scatter(pieces, seen)
    near, far = kernel_call(
        expert_weights_kernel,
        [((1024, 2048), BF)] * 2,
        [VMEM] * 4,
        40,
        2 * 1024 * 2048 * 2048,
    )(mixed, hidden_grad, grad_out, gated)
    keep, send = split(5, ids, near, other_core(after(far, seen[0])))
    far_seen = seen
    middle_grad, own_output, *parts = kernel_call(
        middle_grad_kernel,
        [own_row, ((64, 2048), BF)] + [own_part] * 4,
        [SMEM, SMEM] + [VMEM] * 11,
        8,
    )(ids, slot_length, *terms, middle, own_cot, mlp_row)
    seen = []
    branch_pieces = cube_gather(parts, seen)
    keep, send = split(4, ids, keep, X_ACROSS(after(send, far_seen[2])))
    send = after(send, seen[0])

    branch, q_scaled, k_scaled, v_grad, inner, gain_grads = kernel_call(
        backward_kernel,
        [((1024, 2048), BF), WIDE_HEAD, WIDE_HEAD, HEAD, ((16, 128), F32), ((2, 128), F32)],
        [SMEM, SMEM] + [VMEM] * 19,
        40,
        10 * 1024 * 1024 * 128,
        [pltpu.VMEM((1024, 128), BF), pltpu.VMEM((1024, 128), F32), pltpu.VMEM((1024, 128), F32)],
    )(
        places, slot_length, *branch_pieces, first, first_far,
        qkv, rates, gain_rows, cosine, sine, queries, keys, values, log_total,
    )
    def whole(own, kind, earlier=None):
        (both,) = kernel_call(both_kernel, [((128, 2048), BF)], [SMEM] + [VMEM] * 2, 4)(
            ids, own, other_half(own)
        )
        if earlier is not None:
            both = after(both, earlier)
        return kernel_call(slots_kernel, [((2, 128, 2048), kind)], [SMEM] + [VMEM] * 2, 8)(
            ids, both, other_core(both)
        )[0]

    expert_grads = (keep + X_PAIR(send)).reshape(4, 64, 2048)
    output = whole(after(own_output, seen[2]), BF, inner)
    qkv_grad, *pieces = kernel_call(
        exit_kernel,
        [((1024, 384), BF)] + [PIECE] * 8,
        [SMEM] + [VMEM] * 11,
        20,
        2 * 1024 * 2048 * 384,
        [pltpu.VMEM((1024, 384), BF)],
        [output, expert_grads],
    )(places, q_scaled, k_scaled, v_grad, qkv, rates, *token_terms(inner), first, first_far)
    seen = []
    terms = cube_scatter(pieces, seen)
    near, far = kernel_call(
        attention_weights_kernel,
        [((1024, 640), BF)] * 2,
        [SMEM] + [VMEM] * 5,
        24,
        2 * 1024 * 2048 * 512,
    )(ids, normed, qkv_grad, branch, attended, gain_grads)
    attn_grads = near + other_core(after(far, seen[0]))
    attn_grads = all_to_all(attn_grads.reshape(16, 64, 640), ("x", "z"))
    attn_grads = jnp.sum(attn_grads.reshape(4, 4, 64, 640).astype(F32), axis=0).astype(BF)
    attn_grads = swap_cores(attn_grads)
    (own_input_grad,) = kernel_call(
        input_grad_kernel, [((64, 2048), BF)], [SMEM] + [VMEM] * 11, 8, earlier=[attn_grads]
    )(ids, *terms, middle_grad, own_tokens, attn_row)
    expert_grads = swap_cores(after(expert_grads, seen[0]))
    expert_grads = line_exchange(after(expert_grads, own_input_grad), ids)

    q_grads, k_grads, v_grads, o_grads, attn_part = kernel_call(
        first_unpack_kernel,
        [((64, 512), F32)] * 4 + [((64, 128), F32)],
        [VMEM] * 4,
        8,
    )(attn_grads, w_query, w_key, w_value)
    o_grads = o_grads.T
    gate_grads, up_grads, down_grads, small = kernel_call(
        second_unpack_kernel,
        [((10, 64, 256), F32)] * 3 + [((64, 128), F32)],
        [VMEM] * 4,
        20,
    )(expert_grads, w_gate, w_up, router.T)
    summed = jnp.concatenate([small[:, :11], attn_part[:, :1]], axis=1)
    summed = summed + other_core(summed)
    summed = summed + other_half(summed)
    return (
        output,
        whole(own_input_grad, F32),
        summed[:, 11] / attn_gain.astype(F32),
        attn_grads[:, :4, 512].astype(F32),
        attn_grads[:, :4, 513].astype(F32),
        q_grads,
        k_grads,
        v_grads,
        o_grads,
        summed[:, 10] / mlp_gain.astype(F32),
        summed[:, :10],
        gate_grads,
        up_grads,
        down_grads.swapaxes(1, 2),
    )


def solution(mesh):
    fine = Mesh(mesh.devices.reshape(SIZES), AXES)
    rows = P("x", CONTEXT, None)
    vector = P(WEIGHT)
    gains = P(TENSOR, WEIGHT)
    tall = P(WEIGHT, TENSOR)
    routed = P(WEIGHT, None)
    hidden = P(None, WEIGHT, TENSOR)
    back = P(None, TENSOR, WEIGHT)
    weights = (vector, gains, gains, tall, tall, tall, gains, vector, routed, hidden, hidden, back)
    return jax.shard_map(
        per_device,
        mesh=fine,
        in_specs=(rows, P("x"), rows) + weights + (rows,),
        out_specs=(rows, rows) + weights,
        check_vma=False,
    )
```

time: 753 us -> 536 us (0.71)
  local copies, waits for them, and re-layouts: 105 us -> 31.8 us
  starting transfers between devices: 209 us -> 161 us
  waiting for transfers between devices: 253 us -> 205 us
  matrix products: 29.7 us -> 0 us
  Pallas kernels: 83.7 us -> 113 us
  other arithmetic: 31.2 us -> 5.46 us
  between operations: 15.6 us -> 2.16 us
    all_to_all x7 -> x1, waiting for transfers between devices: 45 us -> 0.01 us  [all_to_all(): return lax.all_to_all(v, axes, split_axis=0, concat_axis=0, tiled=True)]
    all_to_all x7 -> x1, starting transfers between devices: 39.2 us -> 4.54 us  [all_to_all(): return lax.all_to_all(v, axes, split_axis=0, concat_axis=0, tiled=True)]
    dot_general x8 -> x0, matrix products: 29.7 us -> none  [dot(): lax.dot_general(a, b, (((left,), (right,)), ((), ())), preferred_element_...]
    pallas_call x27 -> x47, Pallas kernels: 83.7 us -> 113 us  [the longest x45 73.8 us: kernel_call(): return lambda *args: call(*earlier, *args)]
    unnamed x207 -> x214, local copies, waits for them, and re-layouts: 54.2 us -> 29.8 us
    reshape x21 -> x0, local copies, waits for them, and re-layouts: 13 us -> none  [the longest x5 3.52 us: four(): return w.reshape(64, 4, -1).transpose(1, 0, 2)]
    rev x6 -> x0, local copies, waits for them, and re-layouts: 10.4 us -> none  [the longest x2 5.11 us: natural(): return jnp.where(core == 0, halves, halves[:, :, ::-1]).reshape(64, 2048)]
    ppermute x4, starting transfers between devices: 12.9 us -> 3.88 us  [lax.ppermute(v, SWAP, [(0, 0), (1, 2), (2, 1), (3, 3)])]
  transfers between devices with their start and end apart: 123 -> 139, of which waited for: 71 -> 89; matrix products, arithmetic and copies ran while one was open for 14% -> 1% of each run, Pallas kernels for 7% -> 12%
where the time goes in v3:
time: 536 us; the launch traced here: 528 us
  waiting for transfers between devices  205 us (38%)
  starting transfers between devices  161 us (30%)
  Pallas kernels  113 us (21%)
  local copies, waits for them, and re-layouts  31.8 us (6%)
  blocking collectives  9.47 us (2%)
  other arithmetic  5.46 us (1%)
    ppermute x134, waiting for transfers between devices, exchange(): return lambda v: lax.ppermute(v, axes, pairs)  205 us
    ppermute x134, starting transfers between devices, exchange(): return lambda v: lax.ppermute(v, axes, pairs)  153 us
    pallas_call x45, Pallas kernels, kernel_call(): return lambda *args: call(*earlier, *args)  73.8 us
    pallas_call x1, Pallas kernels, per_device(): pl.pallas_call(mixture_kernel, out_shape=[jax.ShapeDtypeStruct(shape, kin...  37.4 us
    unnamed x214, local copies, waits for them, and re-layouts  29.8 us
  transfers between devices with their start and end apart: 139, of which 89 were waited for; matrix products, arithmetic and copies ran while one was open for 1% of the time, Pallas kernels for 12%

profile of v3, /device:TPU:0, one launch (start us, length us, event | category | flops | bytes accessed | tf_op | source)
XLA Modules:
  0.0 528.4 jit_solution(4901136107317433390)
XLA Ops:
  22.2 9.5 %all_to_all.10 = bf16[4,64,640]{2,1,0:T(8,128)(2,1)S(1)} all-to-all(bf16[4,64,640]{2,1,0:T(8,128)(2,1)S(1)} %collective-permute-done.16), channel_id=1, replica_groups=mesh['x'=4,'z'=4,'yl'=2,'yh'=2,'c'=2] {'z'}, dimensions={0} | all-to-all | bytes 655360 | tf_op jit(solution)/shard_map/all_to_all | solution.py:54
  50.5 9.2 %collective-permute-done.18.refs_2_ = bf16[512,640]{1,0:T(8,128)(2,1)S(1)} collective-permute-done((bf16[512,640]{1,0:T(8,128)(2,1)S(1)}, bf16[512,640]{1,0:T(8,128)(2,1)S(1)}, u32[]{:S(2)}, u32[]{:S(2)}) %collective-permute-start.18) | collective-permute-done | bytes 655392 | tf_op jit(solution)/shard_map/ppermute | solution.py:35
  66.5 10.9 %collective-permute-done.12.refs_5_ = bf16[128,2048]{1,0:T(8,128)(2,1)S(1)} collective-permute-done((bf16[128,2048]{1,0:T(8,128)(2,1)S(1)}, bf16[128,2048]{1,0:T(8,128)(2,1)S(1)}, u32[]{:S(2)}, u32[]{:S(2)}) %collective-permute-start.12) | collective-permute-done | bytes 524320 | tf_op jit(solution)/shard_map/ppermute | solution.py:35
  80.8 3.1 collective-permute-start.20
  85.4 12.1 %shard_map.288 = (bf16[1024,2048]{1,0:T(8,128)(2,1)S(1)}, f32[1024,384]{1,0:T(8,128)S(1)}, f32[16,128]{1,0:T(8,128)S(1)}, f32[2,2048]{1,0:T(2,128)S(1)}, f32[2,128]{1,0:T(2,128)S(1)}) custom-call(s32[64]{0:T(128)S(1)} %copy-done.73, bf16[128,2048]{1,0:T(8,128)(2,1)S(1)} %get-tuple-element.248.refs_1_, bf16[128,2048]{1,0:T(8,128)(2,1)S(1)} %get-tuple-element.249.refs_2_, ...), custom_call_target="tpu_custom_call" | custom-call | flops 1610612736 | bytes 4194304 | tf_op jit(solution)/shard_map/pallas_call | solution.py:70
  99.6 8.9 %collective-permute-done.22.refs_14_ = bf16[128,2176]{1,0:T(8,128)(2,1)S(1)} collective-permute-done((bf16[128,2176]{1,0:T(8,128)(2,1)S(1)}, bf16[128,2176]{1,0:T(8,128)(2,1)S(1)}, u32[]{:S(2)}, u32[]{:S(2)}) %collective-permute-start.22) | collective-permute-done | bytes 557088 | tf_op jit(solution)/shard_map/ppermute | solution.py:35
  120.9 3.1 collective-permute-done.29.refs_6_
  127.6 5.7 %shard_map.289 = (f32[1024,2]{1,0:T(8,128)S(1)}, bf16[1024,128]{1,0:T(8,128)(2,1)S(1)}, bf16[1024,128]{1,0:T(8,128)(2,1)S(1)}, bf16[1024,128]{1,0:T(8,128)(2,1)S...) custom-call(s32[64]{0:T(128)S(1)} %copy-done.73, ...), custom_call_target="tpu_custom_call" | custom-call | flops 536870912 | bytes 4194304 | tf_op jit(solution)/shard_map/pallas_call | solution.py:70
  139.5 15.3 %collective-permute-done.66.refs_2_ = bf16[256,2048]{1,0:T(8,128)(2,1)S(1)} collective-permute-done((bf16[256,2048]{1,0:T(8,128)(2,1)S(1)}, bf16[256,2048]{1,0:T(8,128)(2,1)S(1)}, u32[]{:S(2)}, u32[]{:S(2)}) %collective-permute-start.66) | collective-permute-done | bytes 1048608 | tf_op jit(solution)/shard_map/ppermute | solution.py:35
  161.3 4.1 collective-permute-done.34.refs_4_
  208.8 5.6 %collective-permute-done.54.refs_4_ = bf16[64,2048]{1,0:T(8,128)(2,1)S(1)} collective-permute-done((bf16[64,2048]{1,0:T(8,128)(2,1)S(1)}, bf16[64,2048]{1,0:T(8,128)(2,1)S(1)}, u32[]{:S(2)}, u32[]{:S(2)}) %collective-permute-start.54) | collective-permute-done | bytes 262176 | tf_op jit(solution)/shard_map/ppermute | solution.py:35
  222.0 9.4 %collective-permute-done.58.refs_4_ = bf16[128,2048]{1,0:T(8,128)(2,1)S(1)} collective-permute-done((bf16[128,2048]{1,0:T(8,128)(2,1)S(1)}, bf16[128,2048]{1,0:T(8,128)(2,1)S(1)}, u32[]{:S(2)}, u32[]{:S(2)}) %collective-permute-start.58) | collective-permute-done | bytes 524320 | tf_op jit(solution)/shard_map/ppermute | solution.py:35
  234.7 37.4 %shard_map.302 = (bf16[1024,2048]{1,0:T(8,128)(2,1)}, bf16[1024,2048]{1,0:T(8,128)(2,1)}, bf16[1024,640]{1,0:T(8,128)(2,1)}, bf16[1024,1408]{1,0:T(8,128)(2,1)},...) custom-call(s32[64]{0:T(128)} %copy-done.72, ...), custom_call_target="tpu_custom_call" | custom-call | flops 17179869184 | bytes 37748736 | tf_op jit(solution)/shard_map/pallas_call | solution.py:767
  279.9 13.6 %shard_map.313 = (bf16[1024,2048]{1,0:T(8,128)(2,1)S(1)}, bf16[1024,2048]{1,0:T(8,128)(2,1)S(1)}) custom-call(bf16[1024,2048]{1,0:T(8,128)(2,1)} %get-tuple-element.387.refs_0_, bf16[1024,1408]{1,0:T(8,128)(2,1)S(1)} %copy-done.96, bf16[1024,2048]{1,0:T(8,128)(2,1)} %get-tuple-element.389.refs_2_, bf16[1024,640]{1,0:T(8,128)(2,1)S(1)} %copy-done.97), custom_call_target="tpu_custom_call" | custom-call | flops 8589934592 | bytes 4194304 | tf_op jit(solution)/shard_map/pallas_call | solution.py:70
  305.2 11.1 %collective-permute-done.73.refs_4_ = bf16[64,4096]{1,0:T(8,128)(2,1)S(1)} collective-permute-done((bf16[64,4096]{1,0:T(8,128)(2,1)S(1)}, bf16[64,4096]{1,0:T(8,128)(2,1)S(1)}, u32[]{:S(2)}, u32[]{:S(2)}) %collective-permute-start.73) | collective-permute-done | bytes 524320 | tf_op jit(solution)/shard_map/ppermute | solution.py:35
  357.1 3.0 collective-permute-done.90.refs_5_
  365.6 4.1 collective-permute-done.93.refs_4_
  369.7 5.6 %collective-permute-done.94.refs_5_ = bf16[64,2048]{1,0:T(8,128)(2,1)S(1)} collective-permute-done((bf16[64,2048]{1,0:T(8,128)(2,1)S(1)}, bf16[64,2048]{1,0:T(8,128)(2,1)S(1)}, u32[]{:S(2)}, u32[]{:S(2)}) %collective-permute-start.94) | collective-permute-done | bytes 262176 | tf_op jit(solution)/shard_map/ppermute | solution.py:35
  384.1 4.8 collective-permute-done.98.refs_6_
  391.0 7.0 %shard_map.311 = (bf16[1024,2048]{1,0:T(8,128)(2,1)}, f32[1024,128]{1,0:T(8,128)S(1)}, f32[1024,128]{1,0:T(8,128)S(1)}, bf16[1024,128]{1,0:T(8,128)(2,1)S(1)}, f...) custom-call(s32[64]{0:T(128)S(1)} %copy-done.74, s32[1]{0:T(128)} %dynamic_slice.3.length.refs_1_, ...), custom_call_target="tpu_custom_call" | custom-call | flops 1342177280 | bytes 4194304 | tf_op jit(solution)/shard_map/pallas_call | solution.py:70
  411.0 3.8 shard_map.316
  421.0 4.2 shard_map.317
  425.2 3.5 collective-permute-done.112.refs_4_
  436.5 4.5 all-to-all-start.1
  455.9 8.9 %collective-permute-done.118.refs_4_ = bf16[64,2048]{1,0:T(8,128)(2,1)S(1)} collective-permute-done((bf16[64,2048]{1,0:T(8,128)(2,1)S(1)}, bf16[64,2048]{1,0:T(8,128)(2,1)S(1)}, u32[]{:S(2)}, u32[]{:S(2)}) %collective-permute-start.118) | collective-permute-done | bytes 262176 | tf_op jit(solution)/shard_map/ppermute | solution.py:35
  474.3 3.5 collective-permute-start.123
  481.8 3.7 collective-permute-done.124.refs_6_
  495.7 3.4 collective-permute-done.129.refs_9_
  504.2 3.2 collective-permute-start.135
  508.4 4.0 collective-permute-done.133.refs_2_
  512.3 4.1 collective-permute-done.134.refs_3_
  521.3 4.4 collective-permute-done.137
  (524 shorter events, 291.5 us)
Async XLA Ops:
  44.6 15.1 %collective-permute-start.18 = (bf16[512,640]{1,0:T(8,128)(2,1)S(1)}, bf16[512,640]{1,0:T(8,128)(2,1)S(1)}, u32[]{:S(2)}, u32[]{:S(2)}) collective-permute-start(bf16[512,640]{1,0:T(8,128)(2,1)S(1)} %shard_map.286.refs_1_), channel_id=1, source_target_pairs={{0,96},{32,64},{64,32},{96,0},{1,97},{33,65},{65,33},{97,1},{2,98}... | collective-permute-start | bytes 1966088 | tf_op jit(solution)/shard_map/ppermute | solution.py:35
  61.4 22.6 %collective-permute-start.19 = (bf16[1024,640]{1,0:T(8,128)(2,1)S(1)}, bf16[1024,640]{1,0:T(8,128)(2,1)S(1)}, u32[]{:S(2)}, u32[]{:S(2)}) collective-permute-start(bf16[1024,640]{1,0:T(8,128)(2,1)S(1)} %shard_map.287.refs_10_.refs_12_), channel_id=1, source_target_pairs={{0,1},{1,0},{2,3},{3,2},{4,5},{5,4},{6,7},{7,6},{8,9},{9,8},{10,11... | collective-permute-start | bytes 3932168 | tf_op jit(solution)/shard_map/ppermute | solution.py:35
  61.8 15.6 %collective-permute-start.12 = (bf16[128,2048]{1,0:T(8,128)(2,1)S(1)}, bf16[128,2048]{1,0:T(8,128)(2,1)S(1)}, u32[]{:S(2)}, u32[]{:S(2)}) collective-permute-start(bf16[128,2048]{1,0:T(8,128)(2,1)S(1)} %get-tuple-element.248.refs_1_), channel_id=1, source_target_pairs={{0,6},{2,4},{4,2},{6,0},{1,7},{3,5},{5,3},{7,1},{8,14},{10,12},{12... | collective-permute-start | bytes 1572872 | tf_op jit(solution)/shard_map/ppermute | solution.py:35
  65.1 15.0 %collective-permute-start.15 = (bf16[128,2048]{1,0:T(8,128)(2,1)S(1)}, bf16[128,2048]{1,0:T(8,128)(2,1)S(1)}, u32[]{:S(2)}, u32[]{:S(2)}) collective-permute-start(bf16[128,2048]{1,0:T(8,128)(2,1)S(1)} %get-tuple-element.251.refs_4_), channel_id=1, source_target_pairs={{0,24},{8,16},{16,8},{24,0},{1,25},{9,17},{17,9},{25,1},{2,26},{10... | collective-permute-start | bytes 1572872 | tf_op jit(solution)/shard_map/ppermute | solution.py:35
  80.1 33.8 %collective-permute-start.62 = (bf16[4,64,2048]{2,1,0:T(8,128)(2,1)S(1)}, bf16[4,64,2048]{2,1,0:T(8,128)(2,1)S(1)}, u32[]{:S(2)}, u32[]{:S(2)}) collective-permute-start(bf16[4,64,2048]{2,1,0:T(8,128)(2,1)S(1)} %shard_map.297), channel_id=1, source_target_pairs={{0,0},{1,4},{4,1},{5,5},{2,2},{3,6},{6,3},{7,7},{8,8},{9,12},{12,9... | collective-permute-start | bytes 3145736 | tf_op jit(solution)/shard_map/ppermute | solution.py:42
  80.8 18.7 %collective-permute-start.20 = (bf16[128,2176]{1,0:T(8,128)(2,1)S(1)}, bf16[128,2176]{1,0:T(8,128)(2,1)S(1)}, u32[]{:S(2)}, u32[]{:S(2)}) collective-permute-start(bf16[128,2176]{1,0:T(8,128)(2,1)S(1)} %get-tuple-element.263.refs_8_), channel_id=1, source_target_pairs={{0,6},{2,4},{4,2},{6,0},{1,7},{3,5},{5,3},{7,1},{8,14},{10,12},{12... | collective-permute-start | bytes 1671176 | tf_op jit(solution)/shard_map/ppermute | solution.py:35
  83.9 15.6 %collective-permute-start.21 = (bf16[128,2176]{1,0:T(8,128)(2,1)S(1)}, bf16[128,2176]{1,0:T(8,128)(2,1)S(1)}, u32[]{:S(2)}, u32[]{:S(2)}) collective-permute-start(bf16[128,2176]{1,0:T(8,128)(2,1)S(1)} %get-tuple-element.264.refs_9_), channel_id=1, source_target_pairs={{0,8},{8,0},{16,24},{24,16},{1,9},{9,1},{17,25},{25,17},{2,10},{10... | collective-permute-start | bytes 1671176 | tf_op jit(solution)/shard_map/ppermute | solution.py:35
  83.9 24.5 %collective-permute-start.22 = (bf16[128,2176]{1,0:T(8,128)(2,1)S(1)}, bf16[128,2176]{1,0:T(8,128)(2,1)S(1)}, u32[]{:S(2)}, u32[]{:S(2)}) collective-permute-start(bf16[128,2176]{1,0:T(8,128)(2,1)S(1)} %get-tuple-element.265.refs_10_), channel_id=1, source_target_pairs={{0,4},{2,6},{4,0},{6,2},{1,5},{3,7},{5,1},{7,3},{8,12},{10,14},{12... | collective-permute-start | bytes 1671176 | tf_op jit(solution)/shard_map/ppermute | solution.py:35
  84.0 24.4 %collective-permute-start.23 = (bf16[128,2176]{1,0:T(8,128)(2,1)S(1)}, bf16[128,2176]{1,0:T(8,128)(2,1)S(1)}, u32[]{:S(2)}, u32[]{:S(2)}) collective-permute-start(bf16[128,2176]{1,0:T(8,128)(2,1)S(1)} %get-tuple-element.266.refs_11_), channel_id=1, source_target_pairs={{0,24},{8,16},{16,8},{24,0},{1,25},{9,17},{17,9},{25,1},{2,26},{10... | collective-permute-start | bytes 1671176 | tf_op jit(solution)/shard_map/ppermute | solution.py:35
  114.5 18.9 %collective-permute-start.63 = (bf16[1,64,2048]{2,1,0:T(8,128)(2,1)S(1)}, bf16[1,64,2048]{2,1,0:T(8,128)(2,1)S(1)}, u32[]{:S(2)}, u32[]{:S(2)}) collective-permute-start(bf16[1,64,2048]{2,1,0:T(8,128)(2,1)S(1)} %get-tuple-element.321), channel_id=1, source_target_pairs={{0,8},{8,0},{16,24},{24,16},{1,9},{9,1},{17,25},{25,17},{2,10},{10... | collective-permute-start | bytes 786440 | tf_op jit(solution)/shard_map/ppermute | solution.py:35
  116.4 17.1 %collective-permute-start.64 = (bf16[1,64,2048]{2,1,0:T(8,128)(2,1)S(1)}, bf16[1,64,2048]{2,1,0:T(8,128)(2,1)S(1)}, u32[]{:S(2)}, u32[]{:S(2)}) collective-permute-start(bf16[1,64,2048]{2,1,0:T(8,128)(2,1)S(1)} %get-tuple-element.322), channel_id=1, source_target_pairs={{0,24},{8,16},{16,8},{24,0},{1,25},{9,17},{17,9},{25,1},{2,26},{10... | collective-permute-start | bytes 786440 | tf_op jit(solution)/shard_map/ppermute | solution.py:35
  117.5 15.9 %collective-permute-start.65 = (bf16[1,64,2048]{2,1,0:T(8,128)(2,1)S(1)}, bf16[1,64,2048]{2,1,0:T(8,128)(2,1)S(1)}, u32[]{:S(2)}, u32[]{:S(2)}) collective-permute-start(bf16[1,64,2048]{2,1,0:T(8,128)(2,1)S(1)} %get-tuple-element.323), channel_id=1, source_target_pairs={{0,16},{8,24},{16,0},{24,8},{1,17},{9,25},{17,1},{25,9},{2,18},{10... | collective-permute-start | bytes 786440 | tf_op jit(solution)/shard_map/ppermute | solution.py:35
  134.1 20.7 %collective-permute-start.66 = (bf16[256,2048]{1,0:T(8,128)(2,1)S(1)}, bf16[256,2048]{1,0:T(8,128)(2,1)S(1)}, u32[]{:S(2)}, u32[]{:S(2)}) collective-permute-start(bf16[256,2048]{1,0:T(8,128)(2,1)S(1)} %bitcast.30), channel_id=1, source_target_pairs={{0,32},{32,0},{64,96},{96,64},{1,33},{33,1},{65,97},{97,65},{2,34}... | collective-permute-start | bytes 3145736 | tf_op jit(solution)/shard_map/ppermute | solution.py:35
  134.8 20.7 %collective-permute-start.30 = (bf16[128,2048]{1,0:T(8,128)(2,1)S(1)}, bf16[128,2048]{1,0:T(8,128)(2,1)S(1)}, u32[]{:S(2)}, u32[]{:S(2)}) collective-permute-start(bf16[128,2048]{1,0:T(8,128)(2,1)S(1)} %get-tuple-element.273), channel_id=1, source_target_pairs={{0,6},{2,4},{4,2},{6,0},{1,7},{3,5},{5,3},{7,1},{8,14},{10,12},{12... | collective-permute-start | bytes 1572872 | tf_op jit(solution)/shard_map/ppermute | solution.py:35
  134.8 20.7 %collective-permute-start.31 = (bf16[128,2048]{1,0:T(8,128)(2,1)S(1)}, bf16[128,2048]{1,0:T(8,128)(2,1)S(1)}, u32[]{:S(2)}, u32[]{:S(2)}) collective-permute-start(bf16[128,2048]{1,0:T(8,128)(2,1)S(1)} %get-tuple-element.274), channel_id=1, source_target_pairs={{0,8},{8,0},{16,24},{24,16},{1,9},{9,1},{17,25},{25,17},{2,10},{10... | collective-permute-start | bytes 1572872 | tf_op jit(solution)/shard_map/ppermute | solution.py:35
  136.5 19.0 %collective-permute-start.32 = (bf16[128,2048]{1,0:T(8,128)(2,1)S(1)}, bf16[128,2048]{1,0:T(8,128)(2,1)S(1)}, u32[]{:S(2)}, u32[]{:S(2)}) collective-permute-start(bf16[128,2048]{1,0:T(8,128)(2,1)S(1)} %get-tuple-element.275), channel_id=1, source_target_pairs={{0,4},{2,6},{4,0},{6,2},{1,5},{3,7},{5,1},{7,3},{8,12},{10,14},{12... | collective-permute-start | bytes 1572872 | tf_op jit(solution)/shard_map/ppermute | solution.py:35
  137.9 17.6 %collective-permute-start.33 = (bf16[128,2048]{1,0:T(8,128)(2,1)S(1)}, bf16[128,2048]{1,0:T(8,128)(2,1)S(1)}, u32[]{:S(2)}, u32[]{:S(2)}) collective-permute-start(bf16[128,2048]{1,0:T(8,128)(2,1)S(1)} %get-tuple-element.276), channel_id=1, source_target_pairs={{0,24},{8,16},{16,8},{24,0},{1,25},{9,17},{17,9},{25,1},{2,26},{10... | collective-permute-start | bytes 1572872 | tf_op jit(solution)/shard_map/ppermute | solution.py:35
  155.6 44.4 %collective-permute-start.67 = (bf16[512,2048]{1,0:T(8,128)(2,1)S(1)}, bf16[512,2048]{1,0:T(8,128)(2,1)S(1)}, u32[]{:S(2)}, u32[]{:S(2)}) collective-permute-start(bf16[512,2048]{1,0:T(8,128)(2,1)S(1)} %shard_map.300.refs_1_), channel_id=1, source_target_pairs={{0,96},{32,64},{64,32},{96,0},{1,97},{33,65},{65,33},{97,1},{2,98}... | collective-permute-start | bytes 6291464 | tf_op jit(solution)/shard_map/ppermute | solution.py:35
  204.4 30.3 %collective-permute-start.68 = (bf16[1024,2048]{1,0:T(8,128)(2,1)S(1)}, bf16[1024,2048]{1,0:T(8,128)(2,1)}, u32[]{:S(2)}, u32[]{:S(2)}) collective-permute-start(bf16[1024,2048]{1,0:T(8,128)(2,1)S(1)} %shard_map.301.refs_16_), channel_id=1, source_target_pairs={{0,1},{1,0},{2,3},{3,2},{4,5},{5,4},{6,7},{7,6},{8,9},{9,8},{10,11... | collective-permute-start | bytes 12582920 | tf_op jit(solution)/shard_map/ppermute | solution.py:35
  272.1 23.9 %collective-permute-start.69 = (bf16[128,4096]{1,0:T(8,128)(2,1)}, bf16[128,4096]{1,0:T(8,128)(2,1)S(1)}, u32[]{:S(2)}, u32[]{:S(2)}) collective-permute-start(bf16[128,4096]{1,0:T(8,128)(2,1)} %get-tuple-element.331), channel_id=1, source_target_pairs={{0,6},{2,4},{4,2},{6,0},{1,7},{3,5},{5,3},{7,1},{8,14},{10,12},{12... | collective-permute-start | bytes 3145736 | tf_op jit(solution)/shard_map/ppermute | solution.py:35
  273.8 22.2 %collective-permute-start.70 = (bf16[128,4096]{1,0:T(8,128)(2,1)}, bf16[128,4096]{1,0:T(8,128)(2,1)S(1)}, u32[]{:S(2)}, u32[]{:S(2)}) collective-permute-start(bf16[128,4096]{1,0:T(8,128)(2,1)} %get-tuple-element.332), channel_id=1, source_target_pairs={{0,8},{8,0},{16,24},{24,16},{1,9},{9,1},{17,25},{25,17},{2,10},{10... | collective-permute-start | bytes 3145736 | tf_op jit(solution)/shard_map/ppermute | solution.py:35
  274.0 22.6 %collective-permute-start.71 = (bf16[128,4096]{1,0:T(8,128)(2,1)}, bf16[128,4096]{1,0:T(8,128)(2,1)}, u32[]{:S(2)}, u32[]{:S(2)}) collective-permute-start(bf16[128,4096]{1,0:T(8,128)(2,1)} %get-tuple-element.333), channel_id=1, source_target_pairs={{0,4},{2,6},{4,0},{6,2},{1,5},{3,7},{5,1},{7,3},{8,12},{10,14},{12... | collective-permute-start | bytes 3145736 | tf_op jit(solution)/shard_map/ppermute | solution.py:35
  275.0 23.2 %collective-permute-start.72 = (bf16[128,4096]{1,0:T(8,128)(2,1)}, bf16[128,4096]{1,0:T(8,128)(2,1)}, u32[]{:S(2)}, u32[]{:S(2)}) collective-permute-start(bf16[128,4096]{1,0:T(8,128)(2,1)} %get-tuple-element.334), channel_id=1, source_target_pairs={{0,24},{8,16},{16,8},{24,0},{1,25},{9,17},{17,9},{25,1},{2,26},{10... | collective-permute-start | bytes 3145736 | tf_op jit(solution)/shard_map/ppermute | solution.py:35
  298.2 25.5 %collective-permute-start.103 = (bf16[1024,2048]{1,0:T(8,128)(2,1)}, bf16[1024,2048]{1,0:T(8,128)(2,1)S(1)}, u32[]{:S(2)}, u32[]{:S(2)}) collective-permute-start(bf16[1024,2048]{1,0:T(8,128)(2,1)} %copy-done.84), channel_id=1, source_target_pairs={{0,1},{1,0},{2,3},{3,2},{4,5},{5,4},{6,7},{7,6},{8,9},{9,8},{10,11... | collective-permute-start | bytes 12582920 | tf_op jit(solution)/shard_map/ppermute | solution.py:35
  300.7 15.6 %collective-permute-start.73 = (bf16[64,4096]{1,0:T(8,128)(2,1)S(1)}, bf16[64,4096]{1,0:T(8,128)(2,1)S(1)}, u32[]{:S(2)}, u32[]{:S(2)}) collective-permute-start(bf16[64,4096]{1,0:T(8,128)(2,1)S(1)} %get-tuple-element.339), channel_id=1, source_target_pairs={{0,24},{8,16},{16,8},{24,0},{1,25},{9,17},{17,9},{25,1},{2,26},{10... | collective-permute-start | bytes 1572872 | tf_op jit(solution)/shard_map/ppermute | solution.py:35
  302.4 15.3 %collective-permute-start.74 = (bf16[64,4096]{1,0:T(8,128)(2,1)S(1)}, bf16[64,4096]{1,0:T(8,128)(2,1)S(1)}, u32[]{:S(2)}, u32[]{:S(2)}) collective-permute-start(bf16[64,4096]{1,0:T(8,128)(2,1)S(1)} %get-tuple-element.340), channel_id=1, source_target_pairs={{0,6},{2,4},{4,2},{6,0},{1,7},{3,5},{5,3},{7,1},{8,14},{10,12},{12... | collective-permute-start | bytes 1572872 | tf_op jit(solution)/shard_map/ppermute | solution.py:35
  329.0 51.5 %collective-permute-start.104 = (bf16[512,2048]{1,0:T(8,128)(2,1)S(1)}, bf16[512,2048]{1,0:T(8,128)(2,1)S(1)}, u32[]{:S(2)}, u32[]{:S(2)}) collective-permute-start(bf16[512,2048]{1,0:T(8,128)(2,1)S(1)} %get-tuple-element.396), channel_id=1, source_target_pairs={{0,96},{32,64},{64,32},{96,0},{1,97},{33,65},{65,33},{97,1},{2,98}... | collective-permute-start | bytes 6291464 | tf_op jit(solution)/shard_map/ppermute | solution.py:35
  383.3 25.6 %collective-permute-start.105 = (bf16[256,2048]{1,0:T(8,128)(2,1)S(1)}, bf16[256,2048]{1,0:T(8,128)(2,1)S(1)}, u32[]{:S(2)}, u32[]{:S(2)}) collective-permute-start(bf16[256,2048]{1,0:T(8,128)(2,1)S(1)} %get-tuple-element.399), channel_id=1, source_target_pairs={{0,32},{32,0},{64,96},{96,64},{1,33},{33,1},{65,97},{97,65},{2,34}... | collective-permute-start | bytes 3145736 | tf_op jit(solution)/shard_map/ppermute | solution.py:35
  436.5 33.7 %all-to-all-start.1 = ((bf16[16,64,640]{2,1,0:T(8,128)(2,1)}), bf16[16,64,640]{2,1,0:T(8,128)(2,1)}, u32[]{:S(2)}, u32[]{:S(2)}) async-start(bf16[16,64,640]{2,1,0:T(8,128)(2,1)} %bitcast.15), calls=%async_computation.1 | async-start | bytes 2621440 | tf_op jit(solution)/shard_map/all_to_all | solution.py:54
  441.0 60.8 %collective-permute-start.132 = (bf16[4,64,2048]{2,1,0:T(8,128)(2,1)S(1)}, bf16[4,64,2048]{2,1,0:T(8,128)(2,1)S(1)}, u32[]{:S(2)}, u32[]{:S(2)}) collective-permute-start(bf16[4,64,2048]{2,1,0:T(8,128)(2,1)S(1)} %bitcast.33), channel_id=1, source_target_pairs={{0,0},{1,4},{4,1},{5,5},{2,2},{3,6},{6,3},{7,7},{8,8},{9,12},{12,9... | collective-permute-start | bytes 3145736 | tf_op jit(solution)/shard_map/ppermute | solution.py:42
  449.6 15.2 %collective-permute-start.118 = (bf16[64,2048]{1,0:T(8,128)(2,1)S(1)}, bf16[64,2048]{1,0:T(8,128)(2,1)S(1)}, u32[]{:S(2)}, u32[]{:S(2)}) collective-permute-start(bf16[64,2048]{1,0:T(8,128)(2,1)S(1)} %get-tuple-element.422), channel_id=1, source_target_pairs={{0,24},{8,16},{16,8},{24,0},{1,25},{9,17},{17,9},{25,1},{2,26},{10... | collective-permute-start | bytes 786440 | tf_op jit(solution)/shard_map/ppermute | solution.py:35
  472.5 26.6 %collective-permute-start.117 = (bf16[4,64,640]{2,1,0:T(8,128)(2,1)}, bf16[4,64,640]{2,1,0:T(8,128)(2,1)S(1)}, u32[]{:S(2)}, u32[]{:S(2)}) collective-permute-start(bf16[4,64,640]{2,1,0:T(8,128)(2,1)} %reduce_sum.12), channel_id=1, source_target_pairs={{0,0},{1,4},{4,1},{5,5},{2,2},{3,6},{6,3},{7,7},{8,8},{9,12},{12,9... | collective-permute-start | bytes 983048 | tf_op jit(solution)/shard_map/ppermute | solution.py:42
  (214 other events, 2308.6 us)

commit v4 on v3

--- a/solution.py
+++ b/solution.py
@@ -23,7 +23,6 @@
 WEIGHT = ("x", "z", "yl")
 GROUP = ("z", "yl", "yh")
 Y = ("yl", "yh")
-SWAP = ("yl", "c")
 VMEM = pl.BlockSpec(memory_space=pltpu.VMEM)
 SMEM = pl.BlockSpec(memory_space=pltpu.SMEM)
 ANY = pl.BlockSpec(memory_space=pl.ANY)
@@ -39,15 +38,34 @@
 ALONG_Z = (exchange("z", 4, 1), exchange("z", 4, 3), exchange("z", 4, 2))
 ALONG_Y = (exchange(Y, 4, 2), exchange(Y, 4, 3), exchange(Y, 4, 1))
 X_PAIR, X_ACROSS = exchange("x", 4, 1), exchange("x", 4, 3)
-swap_cores = lambda v: lax.ppermute(v, SWAP, [(0, 0), (1, 2), (2, 1), (3, 3)])
+LINE = ("z", "yl", "c")
+
+
+def swapped_along_z(mask):
+    pairs = [
+        (4 * z + 2 * yl + core, 4 * (z ^ mask) + 2 * core + yl)
+        for z in range(4)
+        for yl in range(2)
+        for core in range(2)
+    ]
+    return lambda v: lax.ppermute(v, LINE, pairs)
+
+
+SWAPPED = tuple(swapped_along_z(mask) for mask in (0, 1, 3, 2))
 other_core = exchange("c", 2, 1)
 other_half = exchange("yh", 2, 1)
+other_both = exchange(TENSOR, 4, 3)
 
 
 def dot(a, b, left=1, right=0, precision=None):
     return lax.dot_general(
         a, b, (((left,), (right,)), ((), ())), preferred_element_type=F32, precision=precision
     )
+
+
+def dot_in_two(a, b, left, right):
+    upper = a.astype(BF)
+    return dot(upper, b, left, right) + dot((a - upper.astype(F32)).astype(BF), b, left, right)
 
 
 def all_to_all(v, axes):
@@ -100,11 +118,11 @@
     return [CUBE[(i + step) % 4](parts[i]) for i in range(4)]
 
 
-def cube_gather(parts, seen=None):
+def cube_gather(parts, seen=None, earlier=None):
     parts = list(parts)
     for step in range(3):
         arrived = cube_step(parts, step)
-        parts = join(parts, arrived, [parts[0].shape[1]])
+        parts = join(parts, arrived, [parts[0].shape[1]], (earlier or {}).get(step, ()))
         if seen is not None:
             seen.append(arrived)
     return list(parts) + cube_step(parts, 3)
@@ -160,10 +178,10 @@
     sent = kernel_call(pick_kernel, [((1,) + blocks.shape[1:], BF)] * 4, [SMEM, VMEM], 8)(
         ids, blocks
     )
-    arrived = [move(held) for move, held in zip(ALONG_Z, sent[1:])]
+    arrived = [move(held) for move, held in zip(SWAPPED, sent)]
     return kernel_call(
         place_kernel, [(blocks.shape, BF)], [SMEM] + [VMEM] * 4, 8
-    )(ids, sent[0], *arrived)[0]
+    )(ids, *arrived)[0]
 
 
 def token_terms(stats):
@@ -179,7 +197,7 @@
         send[...] = (kept[half:, :].astype(F32) + arrived[half:, :].astype(F32)).astype(BF)
 
 
-def cube_scatter(pieces, seen=None):
+def cube_scatter(pieces, seen=None, earlier=None):
     kept, sent = pieces[:4], pieces[4:]
     for step in (3, 2, 1, 0):
         arrived = cube_step(sent, step)
@@ -187,7 +205,9 @@
             seen.append(arrived)
         if step:
             half = ((kept[0].shape[0] // 2, kept[0].shape[1]), BF)
-            folded = kernel_call(fold_kernel, [half] * 8, [VMEM] * 8, 16)(*kept, *arrived)
+            folded = kernel_call(
+                fold_kernel, [half] * 8, [VMEM] * 8, 16, earlier=(earlier or {}).get(step, ())
+            )(*kept, *arrived)
             kept, sent = folded[:4], folded[4:]
     return list(kept) + arrived
 
@@ -380,20 +400,26 @@
     return jnp.where(jnp.logical_and(here, (row & 63) < 4), 1.0, 0.0).astype(BF)
 
 
-def enter_kernel(places, *refs):
-    pieces, (ids, near, far, normed, qkv, stats, lines, gains) = refs[:8], refs[8:]
+def gain_line(near, far, column, out):
     eye = identity(128, F32)
     for at, weight in enumerate((near, far)):
         for b in range(8):
             held = weight[128 * b : 128 * b + 128, 384:512].astype(F32)
-            for n in range(2):
-                line = jnp.sum(held[:, n : n + 1] * eye, axis=0, keepdims=True)
-                lines[n : n + 1, 1024 * at + 128 * b : 1024 * at + 128 * b + 128] = line
+            line = jnp.sum(held[:, column : column + 1] * eye, axis=0, keepdims=True)
+            out[0:1, 1024 * at + 128 * b : 1024 * at + 128 * b + 128] = line
+
+
+def gains_kernel(ids, near, far, line, gains):
+    gain_line(near, far, 1, line)
     total = jnp.zeros((128, 128), F32)
     for at, weight in enumerate((near, far)):
         total += dot(weight[:, 384:512], gain_places(ids[0], at), 0, 0)
     gains[...] = total[2:4, :]
-    gain = lines.at[0:1, :]
+
+
+def enter_kernel(places, *refs):
+    pieces, (near, far, normed, gain) = refs[:8], refs[8:]
+    gain_line(near, far, 0, gain)
     for k in range(8):
 
         def norm_rows(j, _):
@@ -403,6 +429,9 @@
             return 0
 
         lax.fori_loop(0, 8, norm_rows, 0)
+
+
+def project_kernel(normed, near, far, qkv, stats):
     for b in range(4):
         rows = slice(256 * b, 256 * b + 256)
         held = dot(normed[rows, :1024], near[:, :384]) + dot(normed[rows, 1024:], far[:, :384])
@@ -460,8 +489,12 @@
 def mixture_kernel(places, length, ids, *refs):
     arrays, scratch = refs[:30], refs[30:]
     sources, outs = arrays[:18], arrays[18:]
-    held, (mixed, grad_out, gated, hidden_grad), made = scratch[:18], scratch[18:22], scratch[22:30]
-    chosen_rows, ordered, gated_ordered, spread, in_sems, out_sems = scratch[30:]
+    buffers, (near, far, mixed, grad_out, gated, hidden_grad) = scratch[:8], scratch[8:14]
+    chosen_rows, ordered, gated_ordered, spread, in_sems, out_sems = scratch[14:]
+    pieces = [held.at[:, :2048] for held in buffers]
+    routed = [held.at[:, 2048:] for held in buffers]
+    made = [held.at[:, :4096] for held in buffers]
+    held = pieces + routed + [near, far]
     loads = [
         pltpu.make_async_copy(source, target, in_sems.at[n])
         for n, (source, target) in enumerate(zip(sources, held))
@@ -469,15 +502,14 @@
     stores = [
         pltpu.make_async_copy(source, target, out_sems.at[n])
         for n, (source, target) in enumerate(
-            zip((mixed, grad_out, gated, hidden_grad) + tuple(made), outs)
+            zip([mixed, grad_out, gated, hidden_grad] + made, outs)
         )
     ]
     for load in loads:
         load.start()
-    pieces, routed, (near, far) = held[:8], held[8:16], held[16:]
     expert = lax.broadcasted_iota(jnp.int32, (128, 640), 0)
     tile = 5 * ids[3] + (lax.broadcasted_iota(jnp.int32, (128, 640), 1) >> 7)
-    spread[...] = ((tile >> 1) == expert).astype(F32)
+    spread[...] = ((tile >> 1) == expert).astype(F32).astype(BF)
     for load in loads[:8]:
         load.wait()
     put_pieces(places, pieces, mixed)
@@ -495,10 +527,10 @@
     stores[1].start()
     for load in loads[16:]:
         load.wait()
-    lane = lax.broadcasted_iota(jnp.int32, (256, 128), 1)
+    lane = lax.broadcasted_iota(jnp.int32, (512, 128), 1)
 
     def block(b, _):
-        rows = pl.ds(pl.multiple_of(b * 256, 256), 256)
+        rows = pl.ds(pl.multiple_of(b * 512, 512), 512)
         chosen = chosen_rows[rows, :].astype(F32)
         hidden = dot(mixed[rows, :1024], near[:, :1408]) + dot(mixed[rows, 1024:], far[:, :1408])
         out_grad = dot(grad_out[rows, :1024], near[:, 1408:]) + dot(
@@ -508,7 +540,7 @@
         logits = jnp.where(lane < 10, hidden[:, 1280:], -1e30)
         raised = jnp.exp(logits - jnp.max(logits, axis=1, keepdims=True))
         route_probs = raised / jnp.sum(raised, axis=1, keepdims=True)
-        gates = dot(route_probs * chosen, spread[...], 1, 0, HIGHEST)
+        gates = dot_in_two(route_probs * chosen, spread[...], 1, 0)
         sig = 1.0 / (1.0 + jnp.exp(-gate_h))
         silu = gate_h * sig
         activated = (silu * up_h).astype(BF).astype(F32)
@@ -516,12 +548,12 @@
         act_grad = out_grad * gates
         hidden_grad[rows, :640] = (act_grad * up_h * sig * (1.0 + gate_h * (1.0 - sig))).astype(BF)
         hidden_grad[rows, 640:1280] = (act_grad * silu).astype(BF)
-        chosen_grad = dot(activated * out_grad, spread[...], 1, 1, HIGHEST) * chosen
+        chosen_grad = dot_in_two(activated * out_grad, spread[...], 1, 1) * chosen
         inner = jnp.sum(chosen_grad * route_probs, axis=1, keepdims=True)
         hidden_grad[rows, 1280:] = (route_probs * (chosen_grad - inner)).astype(BF)
         return 0
 
-    lax.fori_loop(0, 4, block, 0)
+    lax.fori_loop(0, 2, block, 0)
     stores[2].start()
     stores[3].start()
     for first in (4, 0):
@@ -648,9 +680,16 @@
     out[pl.ds(64 - here, 64), :] = far[...]
 
 
-def slots_kernel(ids, own, far, out):
-    out[pl.ds(ids[0], 1), :, :] = own[...].astype(out.dtype)[None]
-    out[pl.ds(1 - ids[0], 1), :, :] = far[...].astype(out.dtype)[None]
+def two_slots_kernel(ids, own, far, out):
+    out[pl.ds(ids[0], 1), :, :] = own[...][None]
+    out[pl.ds(1 - ids[0], 1), :, :] = far[...][None]
+
+
+def slots_kernel(ids, own, half, core, both, out):
+    here = pl.multiple_of(ids[1] * 64, 64)
+    for slot, near, far in ((ids[0], own, half), (1 - ids[0], core, both)):
+        out[slot, pl.ds(here, 64), :] = near[...].astype(out.dtype)
+        out[slot, pl.ds(64 - here, 64), :] = far[...].astype(out.dtype)
 
 
 def angles(head_size):
@@ -702,10 +741,9 @@
         w_query, w_key, w_value, w_out.T, attn_gain[None], mlp_gain[None], q_gain, k_gain
     )
 
-    swapped = swap_cores(after(first_pack, own_tokens))
+    held = line_exchange(after(first_pack, own_tokens), ids).reshape(256, 640)
     arrived = cube_step(parts, 0)
     parts = join(parts, arrived, [4224])
-    held = all_to_all(after(swapped, arrived), "z").reshape(256, 640)
     arrived = cube_step(parts, 1)
     parts = join(parts, arrived, [4224])
     held = after(pair(4, ids, held, X_PAIR(held)), arrived)
@@ -714,29 +752,32 @@
     )(w_gate, w_up, w_down.swapaxes(1, 2), router.T)
     arrived = cube_step(parts, 2)
     joined = join(parts, arrived, [2048, 2176])
-    first = after(pair(5, ids, held, X_ACROSS(held)), arrived)
+    first = after(pair(5, ids, held, X_ACROSS(held)), joined)
     first_far = other_core(first)
     token_pieces, routed_pieces = list(joined[0::2]), list(joined[1::2])
     token_pieces += cube_step(token_pieces, 3)
     routed_pieces += cube_step(after(routed_pieces, token_pieces), 3)
-    swapped = swap_cores(after(second_pack, token_pieces[4:]))
-
-    normed, qkv, stats, lines, gain_rows = kernel_call(
+
+    normed, attn_row = kernel_call(
         enter_kernel,
-        [
-            ((1024, 2048), BF),
-            ((1024, 384), F32),
-            ((16, 128), F32),
-            ((2, 2048), F32),
-            ((2, 128), F32),
-        ],
-        [SMEM] + [VMEM] * 8 + [SMEM] + [VMEM] * 2,
-        24,
+        [((1024, 2048), BF), ((1, 2048), F32)],
+        [SMEM] + [VMEM] * 10,
+        20,
         2 * 1024 * 2048 * 384,
-    )(places, *token_pieces, ids, first, first_far)
-    attn_row, mlp_row = lines[0:1], lines[1:2]
-    terms = token_terms(after(stats, routed_pieces[4:]))
-    held = line_exchange(after(swapped, terms[0]), ids).reshape(256, 2048)
+    )(places, *token_pieces, first, first_far)
+    qkv, stats = kernel_call(
+        project_kernel,
+        [((1024, 384), F32), ((16, 128), F32)],
+        [VMEM] * 3,
+        20,
+        2 * 1024 * 2048 * 384,
+        earlier=routed_pieces[4:],
+    )(normed, first, first_far)
+    mlp_row, gain_rows = kernel_call(
+        gains_kernel, [((1, 2048), F32), ((2, 128), F32)], [SMEM] + [VMEM] * 2, 12, earlier=[stats]
+    )(ids, first, first_far)
+    terms = token_terms(stats)
+    held = line_exchange(after(second_pack, terms[1:]), ids).reshape(256, 2048)
     cosine, sine = angles(128)
     rates, queries, keys, values, attended, log_total, *pieces = kernel_call(
         forward_kernel,
@@ -753,14 +794,14 @@
     held = pair(4, ids, held, X_PAIR(after(held, pieces)))
     seen = []
     terms = cube_scatter(pieces, seen)
-    second = pair(5, ids, held, X_ACROSS(after(held, seen[0])))
+    second = pair(5, ids, held, X_ACROSS(after(held, seen[1])))
     middle, *parts = kernel_call(
         middle_kernel, [own_row] + [own_part] * 4, [VMEM] * 10, 8
     )(*terms, own_tokens, mlp_row)
 
     seen = []
     mixed_pieces = cube_gather(parts, seen)
-    second_far = other_core(after(second, seen[1]))
+    second_far = other_core(after(second, seen[2]))
     sums = [((1024, 2048), BF), ((1024, 2048), BF), ((1024, 640), BF), ((1024, 1408), BF)]
     sums += [((128, 4096), BF)] * 8
     taken = [*mixed_pieces, *routed_pieces, second, second_far]
@@ -769,13 +810,14 @@
         out_shape=[jax.ShapeDtypeStruct(shape, kind) for shape, kind in sums],
         in_specs=[SMEM] * 3 + [ANY] * 18,
         out_specs=[ANY] * 12,
-        scratch_shapes=[pltpu.VMEM(held.shape, BF) for held in taken]
-        + [pltpu.VMEM(shape, BF) for shape, _ in sums]
+        scratch_shapes=[pltpu.VMEM((128, 4224), BF)] * 8
+        + [pltpu.VMEM((1024, 2048), BF)] * 2
+        + [pltpu.VMEM(shape, BF) for shape, _ in sums[:4]]
         + [
             pltpu.VMEM((1024, 128), BF),
             pltpu.VMEM((512, 1408), BF),
             pltpu.VMEM((512, 640), BF),
-            pltpu.VMEM((128, 640), F32),
+            pltpu.VMEM((128, 640), BF),
             pltpu.SemaphoreType.DMA((18,)),
             pltpu.SemaphoreType.DMA((12,)),
         ],
@@ -794,17 +836,18 @@
         2 * 1024 * 2048 * 2048,
     )(mixed, hidden_grad, grad_out, gated)
     keep, send = split(5, ids, near, other_core(after(far, seen[0])))
-    far_seen = seen
+    first_send = X_ACROSS(after(send, seen[2]))
     middle_grad, own_output, *parts = kernel_call(
         middle_grad_kernel,
         [own_row, ((64, 2048), BF)] + [own_part] * 4,
         [SMEM, SMEM] + [VMEM] * 11,
         8,
     )(ids, slot_length, *terms, middle, own_cot, mlp_row)
+    keep, send = split(4, ids, keep, first_send)
     seen = []
     branch_pieces = cube_gather(parts, seen)
-    keep, send = split(4, ids, keep, X_ACROSS(after(send, far_seen[2])))
-    send = after(send, seen[0])
+    expert_grads = (keep + X_PAIR(after(send, seen[0]))).reshape(4, 64, 2048)
+    output_far = other_half(after(own_output, seen[2]))
 
     branch, q_scaled, k_scaled, v_grad, inner, gain_grads = kernel_call(
         backward_kernel,
@@ -817,18 +860,19 @@
         places, slot_length, *branch_pieces, first, first_far,
         qkv, rates, gain_rows, cosine, sine, queries, keys, values, log_total,
     )
-    def whole(own, kind, earlier=None):
-        (both,) = kernel_call(both_kernel, [((128, 2048), BF)], [SMEM] + [VMEM] * 2, 4)(
-            ids, own, other_half(own)
-        )
-        if earlier is not None:
-            both = after(both, earlier)
-        return kernel_call(slots_kernel, [((2, 128, 2048), kind)], [SMEM] + [VMEM] * 2, 8)(
-            ids, both, other_core(both)
+    def whole(quarters, kind):
+        return kernel_call(slots_kernel, [((2, 128, 2048), kind)], [SMEM] + [VMEM] * 4, 8)(
+            ids, *quarters
         )[0]
 
-    expert_grads = (keep + X_PAIR(send)).reshape(4, 64, 2048)
-    output = whole(after(own_output, seen[2]), BF, inner)
+    (both,) = kernel_call(both_kernel, [((128, 2048), BF)], [SMEM] + [VMEM] * 2, 4)(
+        ids, own_output, output_far
+    )
+    both = after(both, inner)
+    (output,) = kernel_call(
+        two_slots_kernel, [((2, 128, 2048), BF)], [SMEM] + [VMEM] * 2, 8
+    )(ids, both, other_core(both))
+    inner_terms = token_terms(inner)
     qkv_grad, *pieces = kernel_call(
         exit_kernel,
         [((1024, 384), BF)] + [PIECE] * 8,
@@ -837,7 +881,7 @@
         2 * 1024 * 2048 * 384,
         [pltpu.VMEM((1024, 384), BF)],
         [output, expert_grads],
-    )(places, q_scaled, k_scaled, v_grad, qkv, rates, *token_terms(inner), first, first_far)
+    )(places, q_scaled, k_scaled, v_grad, qkv, rates, *inner_terms, first, first_far)
     seen = []
     terms = cube_scatter(pieces, seen)
     near, far = kernel_call(
@@ -847,16 +891,18 @@
         24,
         2 * 1024 * 2048 * 512,
     )(ids, normed, qkv_grad, branch, attended, gain_grads)
-    attn_grads = near + other_core(after(far, seen[0]))
-    attn_grads = all_to_all(attn_grads.reshape(16, 64, 640), ("x", "z"))
-    attn_grads = jnp.sum(attn_grads.reshape(4, 4, 64, 640).astype(F32), axis=0).astype(BF)
-    attn_grads = swap_cores(attn_grads)
+    keep, send = split(5, ids, near, other_core(after(far, seen[0])))
+    keep, send = split(4, ids, keep, X_ACROSS(send))
+    attn_grads = (keep + X_PAIR(after(send, seen[2]))).reshape(4, 64, 640)
+    attn_grads = line_exchange(attn_grads, ids)
     (own_input_grad,) = kernel_call(
-        input_grad_kernel, [((64, 2048), BF)], [SMEM] + [VMEM] * 11, 8, earlier=[attn_grads]
+        input_grad_kernel, [((64, 2048), BF)], [SMEM] + [VMEM] * 11, 8
     )(ids, *terms, middle_grad, own_tokens, attn_row)
-    expert_grads = swap_cores(after(expert_grads, seen[0]))
+
     expert_grads = line_exchange(after(expert_grads, own_input_grad), ids)
-
+    input_quarters = [own_input_grad] + [
+        move(own_input_grad) for move in (other_half, other_core, other_both)
+    ]
     q_grads, k_grads, v_grads, o_grads, attn_part = kernel_call(
         first_unpack_kernel,
         [((64, 512), F32)] * 4 + [((64, 128), F32)],
@@ -875,7 +921,7 @@
     summed = summed + other_half(summed)
     return (
         output,
-        whole(own_input_grad, F32),
+        whole(input_quarters, F32),
         summed[:, 11] / attn_gain.astype(F32),
         attn_grads[:, :4, 512].astype(F32),
         attn_grads[:, :4, 513].astype(F32),

time: 536 us -> 508 us (0.948)
  local copies, waits for them, and re-layouts: 31.8 us -> 14.3 us
  blocking collectives: 9.47 us -> 0 us
  starting transfers between devices: 161 us -> 169 us
    ppermute x134 -> x131, waiting for transfers between devices: 205 us -> 185 us  [exchange(): return lambda v: lax.ppermute(v, axes, pairs)]
    ppermute x4 -> x16, waiting for transfers between devices: 0.01 us -> 17.5 us  [swapped_along_z(): return lambda v: lax.ppermute(v, LINE, pairs)]
    unnamed x214 -> x138, local copies, waits for them, and re-layouts: 29.8 us -> 12.8 us
    ppermute x4 -> x16, starting transfers between devices: 3.88 us -> 18.8 us  [swapped_along_z(): return lambda v: lax.ppermute(v, LINE, pairs)]
    all_to_all x1 -> x0, blocking collectives: 9.47 us -> none  [all_to_all(): return lax.all_to_all(v, axes, split_axis=0, concat_axis=0, tiled=True)]
    ppermute x134 -> x131, starting transfers between devices: 153 us -> 151 us  [exchange(): return lambda v: lax.ppermute(v, axes, pairs)]
    pallas_call x45 -> x52, Pallas kernels: 73.8 us -> 74.1 us  [kernel_call(): return lambda *args: call(*earlier, *args)]
  transfers between devices with their start and end apart: 139 -> 147, of which waited for: 89 -> 93; matrix products, arithmetic and copies ran while one was open for 1% -> 0% of each run, Pallas kernels for 12% -> 13%
where the time goes in v4:
time: 508 us; the launch traced here: 502 us
  waiting for transfers between devices  203 us (40%)
  starting transfers between devices  169 us (33%)
  Pallas kernels  111 us (22%)
  local copies, waits for them, and re-layouts  14.3 us (3%)
    ppermute x131, waiting for transfers between devices, exchange(): return lambda v: lax.ppermute(v, axes, pairs)  185 us
    ppermute x131, starting transfers between devices, exchange(): return lambda v: lax.ppermute(v, axes, pairs)  151 us
    pallas_call x52, Pallas kernels, kernel_call(): return lambda *args: call(*earlier, *args)  74.1 us
    pallas_call x1, Pallas kernels, per_device(): pl.pallas_call(mixture_kernel, out_shape=[jax.ShapeDtypeStruct(shape, kin...  34.8 us
    ppermute x16, starting transfers between devices, swapped_along_z(): return lambda v: lax.ppermute(v, LINE, pairs)  18.8 us
    ppermute x16, waiting for transfers between devices, swapped_along_z(): return lambda v: lax.ppermute(v, LINE, pairs)  17.5 us
    unnamed x138, local copies, waits for them, and re-layouts  12.8 us
  transfers between devices with their start and end apart: 147, of which 93 were waited for; matrix products, arithmetic and copies ran while one was open for 0% of the time, Pallas kernels for 13%

profile of v4, /device:TPU:0, one launch (start us, length us, event | category | flops | bytes accessed | tf_op | source)
XLA Modules:
  0.0 501.5 jit_solution(11853333567709815385)
XLA Ops:
  15.1 4.6 collective-permute-start.1
  45.4 7.7 %collective-permute-done.8.refs_4_ = bf16[64,4224]{1,0:T(8,128)(2,1)S(1)} collective-permute-done((bf16[64,4224]{1,0:T(8,128)(2,1)S(1)}, bf16[64,4224]{1,0:T(8,128)(2,1)S(1)}, u32[]{:S(2)}, u32[]{:S(2)}) %collective-permute-start.8) | collective-permute-done | bytes 540704 | tf_op jit(solution)/shard_map/ppermute | solution.py:34
  60.7 11.3 %collective-permute-done.12.refs_5_ = bf16[128,2048]{1,0:T(8,128)(2,1)S(1)} collective-permute-done((bf16[128,2048]{1,0:T(8,128)(2,1)S(1)}, bf16[128,2048]{1,0:T(8,128)(2,1)S(1)}, u32[]{:S(2)}, u32[]{:S(2)}) %collective-permute-start.12) | collective-permute-done | bytes 524320 | tf_op jit(solution)/shard_map/ppermute | solution.py:34
  78.4 8.1 %shard_map.290 = (bf16[1024,2048]{1,0:T(8,128)(2,1)S(1)}, f32[1,2048]{1,0:T(1,128)S(1)}) custom-call(s32[64]{0:T(128)S(1)} %multiply_add_fusion.places.refs_0_.refs_2_, bf16[128,2048]{1,0:T(8,128)(2,1)S(1)} %get-tuple-element.262.refs_1_, bf16[128,2048]{1,0:T(8,128)(2,1)S(1)} %get-tuple-element.263.refs_2_, ...), custom_call_target="tpu_custom_call" | custom-call | flops 1610612736 | bytes 4194304 | tf_op jit(solution)/shard_map/pallas_call | solution.py:88
  86.5 3.2 collective-permute-done.16.refs_0_.refs_12_
  91.6 3.7 shard_map.291
  116.3 5.7 %shard_map.293 = (f32[1024,2]{1,0:T(8,128)S(1)}, bf16[1024,128]{1,0:T(8,128)(2,1)S(1)}, bf16[1024,128]{1,0:T(8,128)(2,1)S(1)}, bf16[1024,128]{1,0:T(8,128)(2,1)S...) custom-call(s32[64]{0:T(128)S(1)} %multiply_add_fusion.places.refs_0, ...), custom_call_target="tpu_custom_call" | custom-call | flops 536870912 | bytes 4194304 | tf_op jit(solution)/shard_map/pallas_call | solution.py:88
  122.1 6.6 %collective-permute-done.68.refs_4_ = bf16[1,64,2048]{2,1,0:T(8,128)(2,1)S(1)} collective-permute-done((bf16[1,64,2048]{2,1,0:T(8,128)(2,1)S(1)}, bf16[1,64,2048]{2,1,0:T(8,128)(2,1)S(1)}, u32[]{:S(2)}, u32[]{:S(2)}) %collective-permute-start.68) | collective-permute-done | bytes 262176 | tf_op jit(solution)/shard_map/ppermute | solution.py:51
  133.0 10.5 %collective-permute-done.33.refs_4_ = bf16[128,2048]{1,0:T(8,128)(2,1)S(1)} collective-permute-done((bf16[128,2048]{1,0:T(8,128)(2,1)S(1)}, bf16[128,2048]{1,0:T(8,128)(2,1)S(1)}, u32[]{:S(2)}, u32[]{:S(2)}) %collective-permute-start.33) | collective-permute-done | bytes 524320 | tf_op jit(solution)/shard_map/ppermute | solution.py:34
  143.7 2.9 collective-permute-done.36.refs_7_
  150.6 2.8 collective-permute-done.69.refs_2_
  199.2 6.0 %collective-permute-done.70.refs_2_ = bf16[512,2048]{1,0:T(8,128)(2,1)S(1)} collective-permute-done((bf16[512,2048]{1,0:T(8,128)(2,1)S(1)}, bf16[512,2048]{1,0:T(8,128)(2,1)S(1)}, u32[]{:S(2)}, u32[]{:S(2)}) %collective-permute-start.70) | collective-permute-done | bytes 2097184 | tf_op jit(solution)/shard_map/ppermute | solution.py:34
  213.6 10.9 %collective-permute-done.61.refs_4_ = bf16[128,2048]{1,0:T(8,128)(2,1)S(1)} collective-permute-done((bf16[128,2048]{1,0:T(8,128)(2,1)S(1)}, bf16[128,2048]{1,0:T(8,128)(2,1)S(1)}, u32[]{:S(2)}, u32[]{:S(2)}) %collective-permute-start.61) | collective-permute-done | bytes 524320 | tf_op jit(solution)/shard_map/ppermute | solution.py:34
  228.0 34.8 %shard_map.306 = (bf16[1024,2048]{1,0:T(8,128)(2,1)}, bf16[1024,2048]{1,0:T(8,128)(2,1)}, bf16[1024,640]{1,0:T(8,128)(2,1)}, bf16[1024,1408]{1,0:T(8,128)(2,1)},...) custom-call(s32[64]{0:T(128)} %copy-done.46, ...), custom_call_target="tpu_custom_call" | custom-call | flops 17179869184 | bytes 37748736 | tf_op jit(solution)/shard_map/pallas_call | solution.py:808
  269.8 13.6 %shard_map.317 = (bf16[1024,2048]{1,0:T(8,128)(2,1)S(1)}, bf16[1024,2048]{1,0:T(8,128)(2,1)S(1)}) custom-call(bf16[1024,2048]{1,0:T(8,128)(2,1)} %get-tuple-element.398.refs_0_, bf16[1024,1408]{1,0:T(8,128)(2,1)S(1)} %copy-done.62, bf16[1024,2048]{1,0:T(8,128)(2,1)} %get-tuple-element.400.refs_2_, bf16[1024,640]{1,0:T(8,128)(2,1)S(1)} %copy-done.63), custom_call_target="tpu_custom_call" | custom-call | flops 8589934592 | bytes 4194304 | tf_op jit(solution)/shard_map/pallas_call | solution.py:88
  285.4 3.1 collective-permute-done.72.refs_4_
  296.8 11.5 %collective-permute-done.76.refs_4_ = bf16[64,4096]{1,0:T(8,128)(2,1)S(1)} collective-permute-done((bf16[64,4096]{1,0:T(8,128)(2,1)S(1)}, bf16[64,4096]{1,0:T(8,128)(2,1)S(1)}, u32[]{:S(2)}, u32[]{:S(2)}) %collective-permute-start.76) | collective-permute-done | bytes 524320 | tf_op jit(solution)/shard_map/ppermute | solution.py:34
  347.6 3.7 collective-permute-done.93.refs_5_
  356.7 3.8 collective-permute-done.96.refs_4_
  360.4 5.4 %collective-permute-done.97.refs_5_ = bf16[64,2048]{1,0:T(8,128)(2,1)S(1)} collective-permute-done((bf16[64,2048]{1,0:T(8,128)(2,1)S(1)}, bf16[64,2048]{1,0:T(8,128)(2,1)S(1)}, u32[]{:S(2)}, u32[]{:S(2)}) %collective-permute-start.97) | collective-permute-done | bytes 262176 | tf_op jit(solution)/shard_map/ppermute | solution.py:34
  374.9 4.5 collective-permute-done.101.refs_6_
  382.1 7.0 %shard_map.315 = (bf16[1024,2048]{1,0:T(8,128)(2,1)}, f32[1024,128]{1,0:T(8,128)S(1)}, f32[1024,128]{1,0:T(8,128)S(1)}, bf16[1024,128]{1,0:T(8,128)(2,1)S(1)}, f...) custom-call(s32[64]{0:T(128)S(1)} %copy-done.47, s32[1]{0:T(128)} %dynamic_slice.3.length.refs_1_, ...), custom_call_target="tpu_custom_call" | custom-call | flops 1342177280 | bytes 4194304 | tf_op jit(solution)/shard_map/pallas_call | solution.py:88
  401.9 3.8 shard_map.320
  411.2 4.2 shard_map.329
  415.4 3.4 collective-permute-done.115.refs_4_
  422.1 3.0 collective-permute-done.138.refs_2_
  432.0 6.0 %collective-permute-done.119.refs_4_ = bf16[64,2048]{1,0:T(8,128)(2,1)S(1)} collective-permute-done((bf16[64,2048]{1,0:T(8,128)(2,1)S(1)}, bf16[64,2048]{1,0:T(8,128)(2,1)S(1)}, u32[]{:S(2)}, u32[]{:S(2)}) %collective-permute-start.119) | collective-permute-done | bytes 262176 | tf_op jit(solution)/shard_map/ppermute | solution.py:34
  466.3 3.5 collective-permute-done.135.refs_2_
  469.8 3.6 collective-permute-start.133
  474.2 4.2 collective-permute-done.137.refs_4_
  487.2 6.2 %collective-permute-start.145 = (f32[64,12]{0,1:T(8,128)S(1)}, f32[64,12]{0,1:T(8,128)S(1)}, u32[]{:S(2)}, u32[]{:S(2)}) collective-permute-start(f32[64,12]{0,1:T(8,128)S(1)} %pad_maximum_fusion), channel_id=1, source_target_pairs={{0,1},{1,0},{2,3},{3,2},{4,5},{5,4},{6,7},{7,6},{8,9},{9,8},{10,11... | collective-permute-start | bytes 9224 | tf_op jit(solution)/shard_map/ppermute | solution.py:34
  495.5 3.2 collective-permute-start.146
  (468 shorter events, 286.9 us)
Async XLA Ops:
  38.5 17.2 %collective-permute-start.25 = (bf16[512,640]{1,0:T(8,128)(2,1)S(1)}, bf16[512,640]{1,0:T(8,128)(2,1)S(1)}, u32[]{:S(2)}, u32[]{:S(2)}) collective-permute-start(bf16[512,640]{1,0:T(8,128)(2,1)S(1)} %shard_map.288.refs_1_), channel_id=1, source_target_pairs={{0,96},{32,64},{64,32},{96,0},{1,97},{33,65},{65,33},{97,1},{2,98}... | collective-permute-start | bytes 1966088 | tf_op jit(solution)/shard_map/ppermute | solution.py:34
  56.4 22.0 %collective-permute-start.26 = (bf16[1024,640]{1,0:T(8,128)(2,1)S(1)}, bf16[1024,640]{1,0:T(8,128)(2,1)S(1)}, u32[]{:S(2)}, u32[]{:S(2)}) collective-permute-start(bf16[1024,640]{1,0:T(8,128)(2,1)S(1)} %shard_map.289.refs_9_.refs_5_.refs_2_.refs_10_.refs_12_), channel_id=1, source_target_pairs={{0,1},{1,0},{2,3},{3,2},{4,5},{5,4},{6,7},{7,6},{8,9},{9,8},{10,11... | collective-permute-start | bytes 3932168 | tf_op jit(solution)/shard_map/ppermute | solution.py:34
  56.5 15.6 %collective-permute-start.12 = (bf16[128,2048]{1,0:T(8,128)(2,1)S(1)}, bf16[128,2048]{1,0:T(8,128)(2,1)S(1)}, u32[]{:S(2)}, u32[]{:S(2)}) collective-permute-start(bf16[128,2048]{1,0:T(8,128)(2,1)S(1)} %get-tuple-element.262.refs_1_), channel_id=1, source_target_pairs={{0,6},{2,4},{4,2},{6,0},{1,7},{3,5},{5,3},{7,1},{8,14},{10,12},{12... | collective-permute-start | bytes 1572872 | tf_op jit(solution)/shard_map/ppermute | solution.py:34
  58.3 14.0 %collective-permute-start.13 = (bf16[128,2048]{1,0:T(8,128)(2,1)S(1)}, bf16[128,2048]{1,0:T(8,128)(2,1)S(1)}, u32[]{:S(2)}, u32[]{:S(2)}) collective-permute-start(bf16[128,2048]{1,0:T(8,128)(2,1)S(1)} %get-tuple-element.263.refs_2_), channel_id=1, source_target_pairs={{0,8},{8,0},{16,24},{24,16},{1,9},{9,1},{17,25},{25,17},{2,10},{10... | collective-permute-start | bytes 1572872 | tf_op jit(solution)/shard_map/ppermute | solution.py:34
  60.0 14.9 %collective-permute-start.15 = (bf16[128,2048]{1,0:T(8,128)(2,1)S(1)}, bf16[128,2048]{1,0:T(8,128)(2,1)S(1)}, u32[]{:S(2)}, u32[]{:S(2)}) collective-permute-start(bf16[128,2048]{1,0:T(8,128)(2,1)S(1)} %get-tuple-element.265.refs_4_), channel_id=1, source_target_pairs={{0,24},{8,16},{16,8},{24,0},{1,25},{9,17},{17,9},{25,1},{2,26},{10... | collective-permute-start | bytes 1572872 | tf_op jit(solution)/shard_map/ppermute | solution.py:34
  75.0 14.7 %collective-permute-start.16 = (bf16[128,2176]{1,0:T(8,128)(2,1)S(1)}, bf16[128,2176]{1,0:T(8,128)(2,1)S(1)}, u32[]{:S(2)}, u32[]{:S(2)}) collective-permute-start(bf16[128,2176]{1,0:T(8,128)(2,1)S(1)} %get-tuple-element.266.refs_8_), channel_id=1, source_target_pairs={{0,6},{2,4},{4,2},{6,0},{1,7},{3,5},{5,3},{7,1},{8,14},{10,12},{12... | collective-permute-start | bytes 1671176 | tf_op jit(solution)/shard_map/ppermute | solution.py:34
  77.6 14.0 %collective-permute-start.19 = (bf16[128,2176]{1,0:T(8,128)(2,1)S(1)}, bf16[128,2176]{1,0:T(8,128)(2,1)S(1)}, u32[]{:S(2)}, u32[]{:S(2)}) collective-permute-start(bf16[128,2176]{1,0:T(8,128)(2,1)S(1)} %get-tuple-element.269.refs_11_), channel_id=1, source_target_pairs={{0,24},{8,16},{16,8},{24,0},{1,25},{9,17},{17,9},{25,1},{2,26},{10... | collective-permute-start | bytes 1671176 | tf_op jit(solution)/shard_map/ppermute | solution.py:34
  112.6 16.1 %collective-permute-start.68 = (bf16[1,64,2048]{2,1,0:T(8,128)(2,1)S(1)}, bf16[1,64,2048]{2,1,0:T(8,128)(2,1)S(1)}, u32[]{:S(2)}, u32[]{:S(2)}) collective-permute-start(bf16[1,64,2048]{2,1,0:T(8,128)(2,1)S(1)} %get-tuple-element.335), channel_id=1, source_target_pairs={{0,16},{1,20},{4,17},{5,21},{8,24},{9,28},{12,25},{13,29},{16,0},{... | collective-permute-start | bytes 786440 | tf_op jit(solution)/shard_map/ppermute | solution.py:51
  129.3 24.1 %collective-permute-start.69 = (bf16[256,2048]{1,0:T(8,128)(2,1)S(1)}, bf16[256,2048]{1,0:T(8,128)(2,1)S(1)}, u32[]{:S(2)}, u32[]{:S(2)}) collective-permute-start(bf16[256,2048]{1,0:T(8,128)(2,1)S(1)} %bitcast.31), channel_id=1, source_target_pairs={{0,32},{32,0},{64,96},{96,64},{1,33},{33,1},{65,97},{97,65},{2,34}... | collective-permute-start | bytes 3145736 | tf_op jit(solution)/shard_map/ppermute | solution.py:34
  129.7 13.9 %collective-permute-start.33 = (bf16[128,2048]{1,0:T(8,128)(2,1)S(1)}, bf16[128,2048]{1,0:T(8,128)(2,1)S(1)}, u32[]{:S(2)}, u32[]{:S(2)}) collective-permute-start(bf16[128,2048]{1,0:T(8,128)(2,1)S(1)} %get-tuple-element.286), channel_id=1, source_target_pairs={{0,6},{2,4},{4,2},{6,0},{1,7},{3,5},{5,3},{7,1},{8,14},{10,12},{12... | collective-permute-start | bytes 1572872 | tf_op jit(solution)/shard_map/ppermute | solution.py:34
  130.8 15.7 %collective-permute-start.36 = (bf16[128,2048]{1,0:T(8,128)(2,1)S(1)}, bf16[128,2048]{1,0:T(8,128)(2,1)S(1)}, u32[]{:S(2)}, u32[]{:S(2)}) collective-permute-start(bf16[128,2048]{1,0:T(8,128)(2,1)S(1)} %get-tuple-element.289), channel_id=1, source_target_pairs={{0,24},{8,16},{16,8},{24,0},{1,25},{9,17},{17,9},{25,1},{2,26},{10... | collective-permute-start | bytes 1572872 | tf_op jit(solution)/shard_map/ppermute | solution.py:34
  158.0 47.2 %collective-permute-start.70 = (bf16[512,2048]{1,0:T(8,128)(2,1)S(1)}, bf16[512,2048]{1,0:T(8,128)(2,1)S(1)}, u32[]{:S(2)}, u32[]{:S(2)}) collective-permute-start(bf16[512,2048]{1,0:T(8,128)(2,1)S(1)} %shard_map.304.refs_1_), channel_id=1, source_target_pairs={{0,96},{32,64},{64,32},{96,0},{1,97},{33,65},{65,33},{97,1},{2,98}... | collective-permute-start | bytes 6291464 | tf_op jit(solution)/shard_map/ppermute | solution.py:34
  208.0 20.0 %collective-permute-start.71 = (bf16[1024,2048]{1,0:T(8,128)(2,1)S(1)}, bf16[1024,2048]{1,0:T(8,128)(2,1)}, u32[]{:S(2)}, u32[]{:S(2)}) collective-permute-start(bf16[1024,2048]{1,0:T(8,128)(2,1)S(1)} %shard_map.305.refs_16_), channel_id=1, source_target_pairs={{0,1},{1,0},{2,3},{3,2},{4,5},{5,4},{6,7},{7,6},{8,9},{9,8},{10,11... | collective-permute-start | bytes 12582920 | tf_op jit(solution)/shard_map/ppermute | solution.py:34
  208.9 15.5 %collective-permute-start.61 = (bf16[128,2048]{1,0:T(8,128)(2,1)S(1)}, bf16[128,2048]{1,0:T(8,128)(2,1)S(1)}, u32[]{:S(2)}, u32[]{:S(2)}) collective-permute-start(bf16[128,2048]{1,0:T(8,128)(2,1)S(1)} %get-tuple-element.327.refs_0_), channel_id=1, source_target_pairs={{0,6},{2,4},{4,2},{6,0},{1,7},{3,5},{5,3},{7,1},{8,14},{10,12},{12... | collective-permute-start | bytes 1572872 | tf_op jit(solution)/shard_map/ppermute | solution.py:34
  210.4 14.1 %collective-permute-start.62 = (bf16[128,2048]{1,0:T(8,128)(2,1)S(1)}, bf16[128,2048]{1,0:T(8,128)(2,1)S(1)}, u32[]{:S(2)}, u32[]{:S(2)}) collective-permute-start(bf16[128,2048]{1,0:T(8,128)(2,1)S(1)} %get-tuple-element.328.refs_1_), channel_id=1, source_target_pairs={{0,8},{8,0},{16,24},{24,16},{1,9},{9,1},{17,25},{25,17},{2,10},{10... | collective-permute-start | bytes 1572872 | tf_op jit(solution)/shard_map/ppermute | solution.py:34
  211.8 13.8 %collective-permute-start.63 = (bf16[128,2048]{1,0:T(8,128)(2,1)S(1)}, bf16[128,2048]{1,0:T(8,128)(2,1)S(1)}, u32[]{:S(2)}, u32[]{:S(2)}) collective-permute-start(bf16[128,2048]{1,0:T(8,128)(2,1)S(1)} %get-tuple-element.329.refs_2_), channel_id=1, source_target_pairs={{0,4},{2,6},{4,0},{6,2},{1,5},{3,7},{5,1},{7,3},{8,12},{10,14},{12... | collective-permute-start | bytes 1572872 | tf_op jit(solution)/shard_map/ppermute | solution.py:34
  211.8 15.4 %collective-permute-start.64 = (bf16[128,2048]{1,0:T(8,128)(2,1)S(1)}, bf16[128,2048]{1,0:T(8,128)(2,1)S(1)}, u32[]{:S(2)}, u32[]{:S(2)}) collective-permute-start(bf16[128,2048]{1,0:T(8,128)(2,1)S(1)} %get-tuple-element.330.refs_3_), channel_id=1, source_target_pairs={{0,24},{8,16},{16,8},{24,0},{1,25},{9,17},{17,9},{25,1},{2,26},{10... | collective-permute-start | bytes 1572872 | tf_op jit(solution)/shard_map/ppermute | solution.py:34
  262.8 25.7 %collective-permute-start.72 = (bf16[128,4096]{1,0:T(8,128)(2,1)}, bf16[128,4096]{1,0:T(8,128)(2,1)S(1)}, u32[]{:S(2)}, u32[]{:S(2)}) collective-permute-start(bf16[128,4096]{1,0:T(8,128)(2,1)} %get-tuple-element.343), channel_id=1, source_target_pairs={{0,6},{2,4},{4,2},{6,0},{1,7},{3,5},{5,3},{7,1},{8,14},{10,12},{12... | collective-permute-start | bytes 3145736 | tf_op jit(solution)/shard_map/ppermute | solution.py:34
  263.5 25.0 %collective-permute-start.73 = (bf16[128,4096]{1,0:T(8,128)(2,1)}, bf16[128,4096]{1,0:T(8,128)(2,1)S(1)}, u32[]{:S(2)}, u32[]{:S(2)}) collective-permute-start(bf16[128,4096]{1,0:T(8,128)(2,1)} %get-tuple-element.344), channel_id=1, source_target_pairs={{0,8},{8,0},{16,24},{24,16},{1,9},{9,1},{17,25},{25,17},{2,10},{10... | collective-permute-start | bytes 3145736 | tf_op jit(solution)/shard_map/ppermute | solution.py:34
  264.4 24.4 %collective-permute-start.74 = (bf16[128,4096]{1,0:T(8,128)(2,1)}, bf16[128,4096]{1,0:T(8,128)(2,1)}, u32[]{:S(2)}, u32[]{:S(2)}) collective-permute-start(bf16[128,4096]{1,0:T(8,128)(2,1)} %get-tuple-element.345), channel_id=1, source_target_pairs={{0,4},{2,6},{4,0},{6,2},{1,5},{3,7},{5,1},{7,3},{8,12},{10,14},{12... | collective-permute-start | bytes 3145736 | tf_op jit(solution)/shard_map/ppermute | solution.py:34
  265.1 25.1 %collective-permute-start.75 = (bf16[128,4096]{1,0:T(8,128)(2,1)}, bf16[128,4096]{1,0:T(8,128)(2,1)}, u32[]{:S(2)}, u32[]{:S(2)}) collective-permute-start(bf16[128,4096]{1,0:T(8,128)(2,1)} %get-tuple-element.346), channel_id=1, source_target_pairs={{0,24},{8,16},{16,8},{24,0},{1,25},{9,17},{17,9},{25,1},{2,26},{10... | collective-permute-start | bytes 3145736 | tf_op jit(solution)/shard_map/ppermute | solution.py:34
  290.2 25.7 %collective-permute-start.106 = (bf16[1024,2048]{1,0:T(8,128)(2,1)}, bf16[1024,2048]{1,0:T(8,128)(2,1)S(1)}, u32[]{:S(2)}, u32[]{:S(2)}) collective-permute-start(bf16[1024,2048]{1,0:T(8,128)(2,1)} %copy-done.53), channel_id=1, source_target_pairs={{0,1},{1,0},{2,3},{3,2},{4,5},{5,4},{6,7},{7,6},{8,9},{9,8},{10,11... | collective-permute-start | bytes 12582920 | tf_op jit(solution)/shard_map/ppermute | solution.py:34
  292.7 15.6 %collective-permute-start.76 = (bf16[64,4096]{1,0:T(8,128)(2,1)S(1)}, bf16[64,4096]{1,0:T(8,128)(2,1)S(1)}, u32[]{:S(2)}, u32[]{:S(2)}) collective-permute-start(bf16[64,4096]{1,0:T(8,128)(2,1)S(1)} %get-tuple-element.351), channel_id=1, source_target_pairs={{0,24},{8,16},{16,8},{24,0},{1,25},{9,17},{17,9},{25,1},{2,26},{10... | collective-permute-start | bytes 1572872 | tf_op jit(solution)/shard_map/ppermute | solution.py:34
  294.2 15.3 %collective-permute-start.77 = (bf16[64,4096]{1,0:T(8,128)(2,1)S(1)}, bf16[64,4096]{1,0:T(8,128)(2,1)S(1)}, u32[]{:S(2)}, u32[]{:S(2)}) collective-permute-start(bf16[64,4096]{1,0:T(8,128)(2,1)S(1)} %get-tuple-element.352), channel_id=1, source_target_pairs={{0,6},{2,4},{4,2},{6,0},{1,7},{3,5},{5,3},{7,1},{8,14},{10,12},{12... | collective-permute-start | bytes 1572872 | tf_op jit(solution)/shard_map/ppermute | solution.py:34
  296.2 13.8 %collective-permute-start.78 = (bf16[64,4096]{1,0:T(8,128)(2,1)S(1)}, bf16[64,4096]{1,0:T(8,128)(2,1)S(1)}, u32[]{:S(2)}, u32[]{:S(2)}) collective-permute-start(bf16[64,4096]{1,0:T(8,128)(2,1)S(1)} %get-tuple-element.353), channel_id=1, source_target_pairs={{0,8},{8,0},{16,24},{24,16},{1,9},{9,1},{17,25},{25,17},{2,10},{10... | collective-permute-start | bytes 1572872 | tf_op jit(solution)/shard_map/ppermute | solution.py:34
  321.2 50.4 %collective-permute-start.107 = (bf16[512,2048]{1,0:T(8,128)(2,1)S(1)}, bf16[512,2048]{1,0:T(8,128)(2,1)S(1)}, u32[]{:S(2)}, u32[]{:S(2)}) collective-permute-start(bf16[512,2048]{1,0:T(8,128)(2,1)S(1)} %get-tuple-element.407), channel_id=1, source_target_pairs={{0,96},{32,64},{64,32},{96,0},{1,97},{33,65},{65,33},{97,1},{2,98}... | collective-permute-start | bytes 6291464 | tf_op jit(solution)/shard_map/ppermute | solution.py:34
  374.0 25.8 %collective-permute-start.108 = (bf16[256,2048]{1,0:T(8,128)(2,1)S(1)}, bf16[256,2048]{1,0:T(8,128)(2,1)S(1)}, u32[]{:S(2)}, u32[]{:S(2)}) collective-permute-start(bf16[256,2048]{1,0:T(8,128)(2,1)S(1)} %get-tuple-element.410), channel_id=1, source_target_pairs={{0,32},{32,0},{64,96},{96,64},{1,33},{33,1},{65,97},{97,65},{2,34}... | collective-permute-start | bytes 3145736 | tf_op jit(solution)/shard_map/ppermute | solution.py:34
  426.0 28.5 %collective-permute-start.139 = (bf16[512,640]{1,0:T(8,128)(2,1)S(1)}, bf16[512,640]{1,0:T(8,128)(2,1)S(1)}, u32[]{:S(2)}, u32[]{:S(2)}) collective-permute-start(bf16[512,640]{1,0:T(8,128)(2,1)S(1)} %get-tuple-element.462), channel_id=1, source_target_pairs={{0,96},{32,64},{64,32},{96,0},{1,97},{33,65},{65,33},{97,1},{2,98}... | collective-permute-start | bytes 1966088 | tf_op jit(solution)/shard_map/ppermute | solution.py:34
  462.7 15.7 %collective-permute-start.137 = (bf16[1,64,2048]{2,1,0:T(8,128)(2,1)S(1)}, bf16[1,64,2048]{2,1,0:T(8,128)(2,1)S(1)}, u32[]{:S(2)}, u32[]{:S(2)}) collective-permute-start(bf16[1,64,2048]{2,1,0:T(8,128)(2,1)S(1)} %get-tuple-element.452), channel_id=1, source_target_pairs={{0,16},{1,20},{4,17},{5,21},{8,24},{9,28},{12,25},{13,29},{16,0},{... | collective-permute-start | bytes 786440 | tf_op jit(solution)/shard_map/ppermute | solution.py:51
  469.8 23.7 %collective-permute-start.133 = (bf16[64,2048]{1,0:T(8,128)(2,1)S(1)}, bf16[64,2048]{1,0:T(8,128)(2,1)S(1)}, u32[]{:S(2)}, u32[]{:S(2)}) collective-permute-start(bf16[64,2048]{1,0:T(8,128)(2,1)S(1)} %shard_map.324.refs_1_), channel_id=1, source_target_pairs={{0,3},{1,2},{2,1},{3,0},{4,7},{5,6},{6,5},{7,4},{8,11},{9,10},{10,... | collective-permute-start | bytes 786440 | tf_op jit(solution)/shard_map/ppermute | solution.py:34
  473.4 20.1 %collective-permute-start.132 = (bf16[64,2048]{1,0:T(8,128)(2,1)S(1)}, bf16[64,2048]{1,0:T(8,128)(2,1)S(1)}, u32[]{:S(2)}, u32[]{:S(2)}) collective-permute-start(bf16[64,2048]{1,0:T(8,128)(2,1)S(1)} %shard_map.324.refs_1_), channel_id=1, source_target_pairs={{0,1},{1,0},{2,3},{3,2},{4,5},{5,4},{6,7},{7,6},{8,9},{9,8},{10,11... | collective-permute-start | bytes 786440 | tf_op jit(solution)/shard_map/ppermute | solution.py:34
  478.4 15.1 %collective-permute-start.131 = (bf16[64,2048]{1,0:T(8,128)(2,1)S(1)}, bf16[64,2048]{1,0:T(8,128)(2,1)S(1)}, u32[]{:S(2)}, u32[]{:S(2)}) collective-permute-start(bf16[64,2048]{1,0:T(8,128)(2,1)S(1)} %shard_map.324.refs_1_), channel_id=1, source_target_pairs={{0,2},{2,0},{1,3},{3,1},{4,6},{6,4},{5,7},{7,5},{8,10},{10,8},{9,1... | collective-permute-start | bytes 786440 | tf_op jit(solution)/shard_map/ppermute | solution.py:34
  (184 other events, 2115.8 us)

commit v5 on v4

--- a/solution.py
+++ b/solution.py
@@ -128,14 +128,23 @@
     return list(parts) + cube_step(parts, 3)
 
 
-def pick_kernel(ids, blocks, *outs):
+def pick_kernel(ids, *refs):
+    arrays, outs = refs[:-4], refs[-4:]
     for mask, out in zip((0, 1, 3, 2), outs):
-        out[...] = blocks[pl.ds(ids[3] ^ mask, 1)]
-
-
-def place_kernel(ids, own, a, b, c, out):
-    for mask, held in zip((0, 1, 3, 2), (own, a, b, c)):
-        out[pl.ds(ids[3] ^ mask, 1)] = held[...]
+        at = 0
+        for blocks in arrays:
+            columns = slice(at, at + blocks.shape[2])
+            out[:, :, columns] = blocks[pl.ds(ids[3] ^ mask, 1)]
+            at += blocks.shape[2]
+
+
+def place_kernel(ids, *refs):
+    arrived, outs = refs[:4], refs[4:]
+    for mask, held in zip((0, 1, 3, 2), arrived):
+        at = 0
+        for out in outs:
+            out[pl.ds(ids[3] ^ mask, 1)] = held[:, :, at : at + out.shape[2]]
+            at += out.shape[2]
 
 
 def pair_kernel(bit, ids, own, far, out):
@@ -174,14 +183,13 @@
     )(ids, a, b)
 
 
-def line_exchange(blocks, ids):
-    sent = kernel_call(pick_kernel, [((1,) + blocks.shape[1:], BF)] * 4, [SMEM, VMEM], 8)(
-        ids, blocks
-    )
+def line_exchange(ids, *arrays):
+    wide = ((1, arrays[0].shape[1], sum(v.shape[2] for v in arrays)), BF)
+    sent = kernel_call(pick_kernel, [wide] * 4, [SMEM] + [VMEM] * len(arrays), 8)(ids, *arrays)
     arrived = [move(held) for move, held in zip(SWAPPED, sent)]
     return kernel_call(
-        place_kernel, [(blocks.shape, BF)], [SMEM] + [VMEM] * 4, 8
-    )(ids, *arrived)[0]
+        place_kernel, [(v.shape, BF) for v in arrays], [SMEM] + [VMEM] * 4, 8
+    )(ids, *arrived)
 
 
 def token_terms(stats):
@@ -428,7 +436,7 @@
             normed[rows_at(places, 8 * k + j), :] = (held * rate * gain[...]).astype(BF)
             return 0
 
-        lax.fori_loop(0, 8, norm_rows, 0)
+        lax.fori_loop(0, 8, norm_rows, 0, unroll=True)
 
 
 def project_kernel(normed, near, far, qkv, stats):
@@ -553,7 +561,7 @@
         hidden_grad[rows, 1280:] = (route_probs * (chosen_grad - inner)).astype(BF)
         return 0
 
-    lax.fori_loop(0, 2, block, 0)
+    lax.fori_loop(0, 2, block, 0, unroll=True)
     stores[2].start()
     stores[3].start()
     for first in (4, 0):
@@ -741,7 +749,7 @@
         w_query, w_key, w_value, w_out.T, attn_gain[None], mlp_gain[None], q_gain, k_gain
     )
 
-    held = line_exchange(after(first_pack, own_tokens), ids).reshape(256, 640)
+    held = line_exchange(ids, after(first_pack, own_tokens))[0].reshape(256, 640)
     arrived = cube_step(parts, 0)
     parts = join(parts, arrived, [4224])
     arrived = cube_step(parts, 1)
@@ -771,13 +779,12 @@
         [VMEM] * 3,
         20,
         2 * 1024 * 2048 * 384,
-        earlier=routed_pieces[4:],
     )(normed, first, first_far)
     mlp_row, gain_rows = kernel_call(
         gains_kernel, [((1, 2048), F32), ((2, 128), F32)], [SMEM] + [VMEM] * 2, 12, earlier=[stats]
     )(ids, first, first_far)
-    terms = token_terms(stats)
-    held = line_exchange(after(second_pack, terms[1:]), ids).reshape(256, 2048)
+    terms = token_terms(after(stats, routed_pieces[4:]))
+    held = line_exchange(ids, after(second_pack, terms[1:]))[0].reshape(256, 2048)
     cosine, sine = angles(128)
     rates, queries, keys, values, attended, log_total, *pieces = kernel_call(
         forward_kernel,
@@ -894,12 +901,13 @@
     keep, send = split(5, ids, near, other_core(after(far, seen[0])))
     keep, send = split(4, ids, keep, X_ACROSS(send))
     attn_grads = (keep + X_PAIR(after(send, seen[2]))).reshape(4, 64, 640)
-    attn_grads = line_exchange(attn_grads, ids)
     (own_input_grad,) = kernel_call(
         input_grad_kernel, [((64, 2048), BF)], [SMEM] + [VMEM] * 11, 8
     )(ids, *terms, middle_grad, own_tokens, attn_row)
 
-    expert_grads = line_exchange(after(expert_grads, own_input_grad), ids)
+    expert_grads, attn_grads = line_exchange(
+        ids, expert_grads, after(attn_grads, own_input_grad)
+    )
     input_quarters = [own_input_grad] + [
         move(own_input_grad) for move in (other_half, other_core, other_both)
     ]

time: 508 us -> 503 us (level)
  starting transfers between devices: 169 us -> 161 us
  Pallas kernels: 111 us -> 104 us
  waiting for transfers between devices: 203 us -> 210 us
    ppermute x131, starting transfers between devices: 151 us -> 144 us  [exchange(): return lambda v: lax.ppermute(v, axes, pairs)]
    pallas_call x52 -> x50, Pallas kernels: 74.1 us -> 67.7 us  [kernel_call(): return lambda *args: call(*earlier, *args)]
    ppermute x131, waiting for transfers between devices: 185 us -> 191 us  [exchange(): return lambda v: lax.ppermute(v, axes, pairs)]
    ppermute x16 -> x12, starting transfers between devices: 18.8 us -> 16.4 us  [swapped_along_z(): return lambda v: lax.ppermute(v, LINE, pairs)]
    ppermute x16 -> x12, waiting for transfers between devices: 17.5 us -> 19 us  [swapped_along_z(): return lambda v: lax.ppermute(v, LINE, pairs)]
  transfers between devices with their start and end apart: 147 -> 143, of which waited for: 93 -> 93; matrix products, arithmetic and copies ran while one was open for 0% -> 0% of each run, Pallas kernels for 13% -> 12%
where the time goes in v5:
time: 503 us; the launch traced here: 493 us
  waiting for transfers between devices  210 us (42%)
  starting transfers between devices  161 us (32%)
  Pallas kernels  104 us (21%)
  local copies, waits for them, and re-layouts  14.3 us (3%)
    ppermute x131, waiting for transfers between devices, exchange(): return lambda v: lax.ppermute(v, axes, pairs)  191 us
    ppermute x131, starting transfers between devices, exchange(): return lambda v: lax.ppermute(v, axes, pairs)  144 us
    pallas_call x50, Pallas kernels, kernel_call(): return lambda *args: call(*earlier, *args)  67.7 us
    pallas_call x1, Pallas kernels, per_device(): pl.pallas_call(mixture_kernel, out_shape=[jax.ShapeDtypeStruct(shape, kin...  34.1 us
    ppermute x12, waiting for transfers between devices, swapped_along_z(): return lambda v: lax.ppermute(v, LINE, pairs)  19 us
    ppermute x12, starting transfers between devices, swapped_along_z(): return lambda v: lax.ppermute(v, LINE, pairs)  16.4 us
    unnamed x138, local copies, waits for them, and re-layouts  12.9 us
  transfers between devices with their start and end apart: 143, of which 93 were waited for; matrix products, arithmetic and copies ran while one was open for 0% of the time, Pallas kernels for 12%

profile of v5, /device:TPU:0, one launch (start us, length us, event | category | flops | bytes accessed | tf_op | source)
XLA Modules:
  0.0 493.1 jit_solution(12422784446403560340)
XLA Ops:
  15.1 4.6 collective-permute-start.1
  29.4 2.7 collective-permute-start.6
  38.5 2.8 collective-permute-start.21
  45.4 7.7 %collective-permute-done.8.refs_4_ = bf16[64,4224]{1,0:T(8,128)(2,1)S(1)} collective-permute-done((bf16[64,4224]{1,0:T(8,128)(2,1)S(1)}, bf16[64,4224]{1,0:T(8,128)(2,1)S(1)}, u32[]{:S(2)}, u32[]{:S(2)}) %collective-permute-start.8) | collective-permute-done | bytes 540704 | tf_op jit(solution)/shard_map/ppermute | solution.py:34
  60.7 11.3 %collective-permute-done.12.refs_5_ = bf16[128,2048]{1,0:T(8,128)(2,1)S(1)} collective-permute-done((bf16[128,2048]{1,0:T(8,128)(2,1)S(1)}, bf16[128,2048]{1,0:T(8,128)(2,1)S(1)}, u32[]{:S(2)}, u32[]{:S(2)}) %collective-permute-start.12) | collective-permute-done | bytes 524320 | tf_op jit(solution)/shard_map/ppermute | solution.py:34
  80.8 3.7 shard_map.291
  84.5 5.2 %collective-permute-done.23.refs_12_ = bf16[128,2176]{1,0:T(8,128)(2,1)S(1)} collective-permute-done((bf16[128,2176]{1,0:T(8,128)(2,1)S(1)}, bf16[128,2176]{1,0:T(8,128)(2,1)S(1)}, u32[]{:S(2)}, u32[]{:S(2)}) %collective-permute-start.23) | collective-permute-done | bytes 557088 | tf_op jit(solution)/shard_map/ppermute | solution.py:34
  108.8 3.1 collective-permute-start.68
  112.9 5.7 %shard_map.293 = (f32[1024,2]{1,0:T(8,128)S(1)}, bf16[1024,128]{1,0:T(8,128)(2,1)S(1)}, bf16[1024,128]{1,0:T(8,128)(2,1)S(1)}, bf16[1024,128]{1,0:T(8,128)(2,1)S...) custom-call(s32[64]{0:T(128)S(1)} %multiply_add_fusion.places.refs_0, ...), custom_call_target="tpu_custom_call" | custom-call | flops 536870912 | bytes 4194304 | tf_op jit(solution)/shard_map/pallas_call | solution.py:88
  118.7 6.2 %collective-permute-done.68.refs_4_ = bf16[1,64,2048]{2,1,0:T(8,128)(2,1)S(1)} collective-permute-done((bf16[1,64,2048]{2,1,0:T(8,128)(2,1)S(1)}, bf16[1,64,2048]{2,1,0:T(8,128)(2,1)S(1)}, u32[]{:S(2)}, u32[]{:S(2)}) %collective-permute-start.68) | collective-permute-done | bytes 262176 | tf_op jit(solution)/shard_map/ppermute | solution.py:51
  129.0 10.7 %collective-permute-done.33.refs_4_ = bf16[128,2048]{1,0:T(8,128)(2,1)S(1)} collective-permute-done((bf16[128,2048]{1,0:T(8,128)(2,1)S(1)}, bf16[128,2048]{1,0:T(8,128)(2,1)S(1)}, u32[]{:S(2)}, u32[]{:S(2)}) %collective-permute-start.33) | collective-permute-done | bytes 524320 | tf_op jit(solution)/shard_map/ppermute | solution.py:34
  139.9 2.7 collective-permute-done.36.refs_7_
  146.6 3.1 collective-permute-done.69.refs_2_
  187.5 2.6 collective-permute-done.54.refs_5_
  195.1 6.1 %collective-permute-done.70.refs_2_ = bf16[512,2048]{1,0:T(8,128)(2,1)S(1)} collective-permute-done((bf16[512,2048]{1,0:T(8,128)(2,1)S(1)}, bf16[512,2048]{1,0:T(8,128)(2,1)S(1)}, u32[]{:S(2)}, u32[]{:S(2)}) %collective-permute-start.70) | collective-permute-done | bytes 2097184 | tf_op jit(solution)/shard_map/ppermute | solution.py:34
  209.4 11.0 %collective-permute-done.61.refs_4_ = bf16[128,2048]{1,0:T(8,128)(2,1)S(1)} collective-permute-done((bf16[128,2048]{1,0:T(8,128)(2,1)S(1)}, bf16[128,2048]{1,0:T(8,128)(2,1)S(1)}, u32[]{:S(2)}, u32[]{:S(2)}) %collective-permute-start.61) | collective-permute-done | bytes 524320 | tf_op jit(solution)/shard_map/ppermute | solution.py:34
  223.8 34.1 %shard_map.306 = (bf16[1024,2048]{1,0:T(8,128)(2,1)}, bf16[1024,2048]{1,0:T(8,128)(2,1)}, bf16[1024,640]{1,0:T(8,128)(2,1)}, bf16[1024,1408]{1,0:T(8,128)(2,1)},...) custom-call(s32[64]{0:T(128)} %copy-done.42, ...), custom_call_target="tpu_custom_call" | custom-call | flops 17179869184 | bytes 37748736 | tf_op jit(solution)/shard_map/pallas_call | solution.py:815
  265.2 13.6 %shard_map.317 = (bf16[1024,2048]{1,0:T(8,128)(2,1)S(1)}, bf16[1024,2048]{1,0:T(8,128)(2,1)S(1)}) custom-call(bf16[1024,2048]{1,0:T(8,128)(2,1)} %get-tuple-element.398.refs_0_, bf16[1024,1408]{1,0:T(8,128)(2,1)S(1)} %copy-done.58, bf16[1024,2048]{1,0:T(8,128)(2,1)} %get-tuple-element.400.refs_2_, bf16[1024,640]{1,0:T(8,128)(2,1)S(1)} %copy-done.59), custom_call_target="tpu_custom_call" | custom-call | flops 8589934592 | bytes 4194304 | tf_op jit(solution)/shard_map/pallas_call | solution.py:88
  280.7 2.8 collective-permute-done.72.refs_4_
  292.2 11.7 %collective-permute-done.76.refs_4_ = bf16[64,4096]{1,0:T(8,128)(2,1)S(1)} collective-permute-done((bf16[64,4096]{1,0:T(8,128)(2,1)S(1)}, bf16[64,4096]{1,0:T(8,128)(2,1)S(1)}, u32[]{:S(2)}, u32[]{:S(2)}) %collective-permute-start.76) | collective-permute-done | bytes 524320 | tf_op jit(solution)/shard_map/ppermute | solution.py:34
  342.8 3.5 collective-permute-done.93.refs_5_
  351.8 3.7 collective-permute-done.96.refs_4_
  355.5 5.5 %collective-permute-done.97.refs_5_ = bf16[64,2048]{1,0:T(8,128)(2,1)S(1)} collective-permute-done((bf16[64,2048]{1,0:T(8,128)(2,1)S(1)}, bf16[64,2048]{1,0:T(8,128)(2,1)S(1)}, u32[]{:S(2)}, u32[]{:S(2)}) %collective-permute-start.97) | collective-permute-done | bytes 262176 | tf_op jit(solution)/shard_map/ppermute | solution.py:34
  369.8 4.7 collective-permute-done.101.refs_6_
  377.2 7.0 %shard_map.315 = (bf16[1024,2048]{1,0:T(8,128)(2,1)}, f32[1024,128]{1,0:T(8,128)S(1)}, f32[1024,128]{1,0:T(8,128)S(1)}, bf16[1024,128]{1,0:T(8,128)(2,1)S(1)}, f...) custom-call(s32[64]{0:T(128)S(1)} %copy-done.43, s32[1]{0:T(128)} %dynamic_slice.3.length.refs_1_, ...), custom_call_target="tpu_custom_call" | custom-call | flops 1342177280 | bytes 4194304 | tf_op jit(solution)/shard_map/pallas_call | solution.py:88
  397.0 3.8 shard_map.320
  406.2 4.2 shard_map.326
  410.4 3.5 collective-permute-done.115.refs_4_
  417.3 3.0 collective-permute-done.134.refs_2_
  427.3 5.9 %collective-permute-done.119.refs_4_ = bf16[64,2048]{1,0:T(8,128)(2,1)S(1)} collective-permute-done((bf16[64,2048]{1,0:T(8,128)(2,1)S(1)}, bf16[64,2048]{1,0:T(8,128)(2,1)S(1)}, u32[]{:S(2)}, u32[]{:S(2)}) %collective-permute-start.119) | collective-permute-done | bytes 262176 | tf_op jit(solution)/shard_map/ppermute | solution.py:34
  460.0 4.3 collective-permute-start.133
  466.8 10.2 %collective-permute-done.140.refs_4_ = bf16[1,64,2688]{2,1,0:T(8,128)(2,1)S(1)} collective-permute-done((bf16[1,64,2688]{2,1,0:T(8,128)(2,1)S(1)}, bf16[1,64,2688]{2,1,0:T(8,128)(2,1)S(1)}, u32[]{:S(2)}, u32[]{:S(2)}) %collective-permute-start.140) | collective-permute-done | bytes 344096 | tf_op jit(solution)/shard_map/ppermute | solution.py:51
  (458 shorter events, 280.2 us)
Async XLA Ops:
  38.5 17.2 %collective-permute-start.21 = (bf16[512,640]{1,0:T(8,128)(2,1)S(1)}, bf16[512,640]{1,0:T(8,128)(2,1)S(1)}, u32[]{:S(2)}, u32[]{:S(2)}) collective-permute-start(bf16[512,640]{1,0:T(8,128)(2,1)S(1)} %shard_map.288.refs_1_), channel_id=1, source_target_pairs={{0,96},{32,64},{64,32},{96,0},{1,97},{33,65},{65,33},{97,1},{2,98}... | collective-permute-start | bytes 1966088 | tf_op jit(solution)/shard_map/ppermute | solution.py:34
  56.4 22.0 %collective-permute-start.22 = (bf16[1024,640]{1,0:T(8,128)(2,1)S(1)}, bf16[1024,640]{1,0:T(8,128)(2,1)S(1)}, u32[]{:S(2)}, u32[]{:S(2)}) collective-permute-start(bf16[1024,640]{1,0:T(8,128)(2,1)S(1)} %shard_map.289.refs_9_.refs_1_.refs_2_.refs_10_.refs_12_), channel_id=1, source_target_pairs={{0,1},{1,0},{2,3},{3,2},{4,5},{5,4},{6,7},{7,6},{8,9},{9,8},{10,11... | collective-permute-start | bytes 3932168 | tf_op jit(solution)/shard_map/ppermute | solution.py:34
  56.5 15.6 %collective-permute-start.12 = (bf16[128,2048]{1,0:T(8,128)(2,1)S(1)}, bf16[128,2048]{1,0:T(8,128)(2,1)S(1)}, u32[]{:S(2)}, u32[]{:S(2)}) collective-permute-start(bf16[128,2048]{1,0:T(8,128)(2,1)S(1)} %get-tuple-element.257.refs_1_), channel_id=1, source_target_pairs={{0,6},{2,4},{4,2},{6,0},{1,7},{3,5},{5,3},{7,1},{8,14},{10,12},{12... | collective-permute-start | bytes 1572872 | tf_op jit(solution)/shard_map/ppermute | solution.py:34
  58.3 14.0 %collective-permute-start.13 = (bf16[128,2048]{1,0:T(8,128)(2,1)S(1)}, bf16[128,2048]{1,0:T(8,128)(2,1)S(1)}, u32[]{:S(2)}, u32[]{:S(2)}) collective-permute-start(bf16[128,2048]{1,0:T(8,128)(2,1)S(1)} %get-tuple-element.258.refs_2_), channel_id=1, source_target_pairs={{0,8},{8,0},{16,24},{24,16},{1,9},{9,1},{17,25},{25,17},{2,10},{10... | collective-permute-start | bytes 1572872 | tf_op jit(solution)/shard_map/ppermute | solution.py:34
  60.0 14.9 %collective-permute-start.15 = (bf16[128,2048]{1,0:T(8,128)(2,1)S(1)}, bf16[128,2048]{1,0:T(8,128)(2,1)S(1)}, u32[]{:S(2)}, u32[]{:S(2)}) collective-permute-start(bf16[128,2048]{1,0:T(8,128)(2,1)S(1)} %get-tuple-element.260.refs_4_), channel_id=1, source_target_pairs={{0,24},{8,16},{16,8},{24,0},{1,25},{9,17},{17,9},{25,1},{2,26},{10... | collective-permute-start | bytes 1572872 | tf_op jit(solution)/shard_map/ppermute | solution.py:34
  75.0 14.7 %collective-permute-start.23 = (bf16[128,2176]{1,0:T(8,128)(2,1)S(1)}, bf16[128,2176]{1,0:T(8,128)(2,1)S(1)}, u32[]{:S(2)}, u32[]{:S(2)}) collective-permute-start(bf16[128,2176]{1,0:T(8,128)(2,1)S(1)} %get-tuple-element.276.refs_8_), channel_id=1, source_target_pairs={{0,6},{2,4},{4,2},{6,0},{1,7},{3,5},{5,3},{7,1},{8,14},{10,12},{12... | collective-permute-start | bytes 1671176 | tf_op jit(solution)/shard_map/ppermute | solution.py:34
  77.6 14.1 %collective-permute-start.26 = (bf16[128,2176]{1,0:T(8,128)(2,1)S(1)}, bf16[128,2176]{1,0:T(8,128)(2,1)S(1)}, u32[]{:S(2)}, u32[]{:S(2)}) collective-permute-start(bf16[128,2176]{1,0:T(8,128)(2,1)S(1)} %get-tuple-element.279.refs_11_), channel_id=1, source_target_pairs={{0,24},{8,16},{16,8},{24,0},{1,25},{9,17},{17,9},{25,1},{2,26},{10... | collective-permute-start | bytes 1671176 | tf_op jit(solution)/shard_map/ppermute | solution.py:34
  108.8 16.1 %collective-permute-start.68 = (bf16[1,64,2048]{2,1,0:T(8,128)(2,1)S(1)}, bf16[1,64,2048]{2,1,0:T(8,128)(2,1)S(1)}, u32[]{:S(2)}, u32[]{:S(2)}) collective-permute-start(bf16[1,64,2048]{2,1,0:T(8,128)(2,1)S(1)} %get-tuple-element.335), channel_id=1, source_target_pairs={{0,16},{1,20},{4,17},{5,21},{8,24},{9,28},{12,25},{13,29},{16,0},{... | collective-permute-start | bytes 786440 | tf_op jit(solution)/shard_map/ppermute | solution.py:51
  125.6 24.1 %collective-permute-start.69 = (bf16[256,2048]{1,0:T(8,128)(2,1)S(1)}, bf16[256,2048]{1,0:T(8,128)(2,1)S(1)}, u32[]{:S(2)}, u32[]{:S(2)}) collective-permute-start(bf16[256,2048]{1,0:T(8,128)(2,1)S(1)} %bitcast.31), channel_id=1, source_target_pairs={{0,32},{32,0},{64,96},{96,64},{1,33},{33,1},{65,97},{97,65},{2,34}... | collective-permute-start | bytes 3145736 | tf_op jit(solution)/shard_map/ppermute | solution.py:34
  125.9 13.9 %collective-permute-start.33 = (bf16[128,2048]{1,0:T(8,128)(2,1)S(1)}, bf16[128,2048]{1,0:T(8,128)(2,1)S(1)}, u32[]{:S(2)}, u32[]{:S(2)}) collective-permute-start(bf16[128,2048]{1,0:T(8,128)(2,1)S(1)} %get-tuple-element.286), channel_id=1, source_target_pairs={{0,6},{2,4},{4,2},{6,0},{1,7},{3,5},{5,3},{7,1},{8,14},{10,12},{12... | collective-permute-start | bytes 1572872 | tf_op jit(solution)/shard_map/ppermute | solution.py:34
  127.1 15.5 %collective-permute-start.36 = (bf16[128,2048]{1,0:T(8,128)(2,1)S(1)}, bf16[128,2048]{1,0:T(8,128)(2,1)S(1)}, u32[]{:S(2)}, u32[]{:S(2)}) collective-permute-start(bf16[128,2048]{1,0:T(8,128)(2,1)S(1)} %get-tuple-element.289), channel_id=1, source_target_pairs={{0,24},{8,16},{16,8},{24,0},{1,25},{9,17},{17,9},{25,1},{2,26},{10... | collective-permute-start | bytes 1572872 | tf_op jit(solution)/shard_map/ppermute | solution.py:34
  154.0 47.2 %collective-permute-start.70 = (bf16[512,2048]{1,0:T(8,128)(2,1)S(1)}, bf16[512,2048]{1,0:T(8,128)(2,1)S(1)}, u32[]{:S(2)}, u32[]{:S(2)}) collective-permute-start(bf16[512,2048]{1,0:T(8,128)(2,1)S(1)} %shard_map.304.refs_1_), channel_id=1, source_target_pairs={{0,96},{32,64},{64,32},{96,0},{1,97},{33,65},{65,33},{97,1},{2,98}... | collective-permute-start | bytes 6291464 | tf_op jit(solution)/shard_map/ppermute | solution.py:34
  203.9 19.8 %collective-permute-start.71 = (bf16[1024,2048]{1,0:T(8,128)(2,1)S(1)}, bf16[1024,2048]{1,0:T(8,128)(2,1)}, u32[]{:S(2)}, u32[]{:S(2)}) collective-permute-start(bf16[1024,2048]{1,0:T(8,128)(2,1)S(1)} %shard_map.305.refs_16_), channel_id=1, source_target_pairs={{0,1},{1,0},{2,3},{3,2},{4,5},{5,4},{6,7},{7,6},{8,9},{9,8},{10,11... | collective-permute-start | bytes 12582920 | tf_op jit(solution)/shard_map/ppermute | solution.py:34
  204.9 15.5 %collective-permute-start.61 = (bf16[128,2048]{1,0:T(8,128)(2,1)S(1)}, bf16[128,2048]{1,0:T(8,128)(2,1)S(1)}, u32[]{:S(2)}, u32[]{:S(2)}) collective-permute-start(bf16[128,2048]{1,0:T(8,128)(2,1)S(1)} %get-tuple-element.327.refs_0_), channel_id=1, source_target_pairs={{0,6},{2,4},{4,2},{6,0},{1,7},{3,5},{5,3},{7,1},{8,14},{10,12},{12... | collective-permute-start | bytes 1572872 | tf_op jit(solution)/shard_map/ppermute | solution.py:34
  206.3 14.1 %collective-permute-start.62 = (bf16[128,2048]{1,0:T(8,128)(2,1)S(1)}, bf16[128,2048]{1,0:T(8,128)(2,1)S(1)}, u32[]{:S(2)}, u32[]{:S(2)}) collective-permute-start(bf16[128,2048]{1,0:T(8,128)(2,1)S(1)} %get-tuple-element.328.refs_1_), channel_id=1, source_target_pairs={{0,8},{8,0},{16,24},{24,16},{1,9},{9,1},{17,25},{25,17},{2,10},{10... | collective-permute-start | bytes 1572872 | tf_op jit(solution)/shard_map/ppermute | solution.py:34
  207.8 13.8 %collective-permute-start.63 = (bf16[128,2048]{1,0:T(8,128)(2,1)S(1)}, bf16[128,2048]{1,0:T(8,128)(2,1)S(1)}, u32[]{:S(2)}, u32[]{:S(2)}) collective-permute-start(bf16[128,2048]{1,0:T(8,128)(2,1)S(1)} %get-tuple-element.329.refs_2_), channel_id=1, source_target_pairs={{0,4},{2,6},{4,0},{6,2},{1,5},{3,7},{5,1},{7,3},{8,12},{10,14},{12... | collective-permute-start | bytes 1572872 | tf_op jit(solution)/shard_map/ppermute | solution.py:34
  207.8 15.1 %collective-permute-start.64 = (bf16[128,2048]{1,0:T(8,128)(2,1)S(1)}, bf16[128,2048]{1,0:T(8,128)(2,1)S(1)}, u32[]{:S(2)}, u32[]{:S(2)}) collective-permute-start(bf16[128,2048]{1,0:T(8,128)(2,1)S(1)} %get-tuple-element.330.refs_3_), channel_id=1, source_target_pairs={{0,24},{8,16},{16,8},{24,0},{1,25},{9,17},{17,9},{25,1},{2,26},{10... | collective-permute-start | bytes 1572872 | tf_op jit(solution)/shard_map/ppermute | solution.py:34
  257.9 25.7 %collective-permute-start.72 = (bf16[128,4096]{1,0:T(8,128)(2,1)}, bf16[128,4096]{1,0:T(8,128)(2,1)S(1)}, u32[]{:S(2)}, u32[]{:S(2)}) collective-permute-start(bf16[128,4096]{1,0:T(8,128)(2,1)} %get-tuple-element.343), channel_id=1, source_target_pairs={{0,6},{2,4},{4,2},{6,0},{1,7},{3,5},{5,3},{7,1},{8,14},{10,12},{12... | collective-permute-start | bytes 3145736 | tf_op jit(solution)/shard_map/ppermute | solution.py:34
  258.6 25.0 %collective-permute-start.73 = (bf16[128,4096]{1,0:T(8,128)(2,1)}, bf16[128,4096]{1,0:T(8,128)(2,1)S(1)}, u32[]{:S(2)}, u32[]{:S(2)}) collective-permute-start(bf16[128,4096]{1,0:T(8,128)(2,1)} %get-tuple-element.344), channel_id=1, source_target_pairs={{0,8},{8,0},{16,24},{24,16},{1,9},{9,1},{17,25},{25,17},{2,10},{10... | collective-permute-start | bytes 3145736 | tf_op jit(solution)/shard_map/ppermute | solution.py:34
  259.7 24.4 %collective-permute-start.74 = (bf16[128,4096]{1,0:T(8,128)(2,1)}, bf16[128,4096]{1,0:T(8,128)(2,1)}, u32[]{:S(2)}, u32[]{:S(2)}) collective-permute-start(bf16[128,4096]{1,0:T(8,128)(2,1)} %get-tuple-element.345), channel_id=1, source_target_pairs={{0,4},{2,6},{4,0},{6,2},{1,5},{3,7},{5,1},{7,3},{8,12},{10,14},{12... | collective-permute-start | bytes 3145736 | tf_op jit(solution)/shard_map/ppermute | solution.py:34
  260.2 25.5 %collective-permute-start.75 = (bf16[128,4096]{1,0:T(8,128)(2,1)}, bf16[128,4096]{1,0:T(8,128)(2,1)}, u32[]{:S(2)}, u32[]{:S(2)}) collective-permute-start(bf16[128,4096]{1,0:T(8,128)(2,1)} %get-tuple-element.346), channel_id=1, source_target_pairs={{0,24},{8,16},{16,8},{24,0},{1,25},{9,17},{17,9},{25,1},{2,26},{10... | collective-permute-start | bytes 3145736 | tf_op jit(solution)/shard_map/ppermute | solution.py:34
  285.7 25.7 %collective-permute-start.106 = (bf16[1024,2048]{1,0:T(8,128)(2,1)}, bf16[1024,2048]{1,0:T(8,128)(2,1)S(1)}, u32[]{:S(2)}, u32[]{:S(2)}) collective-permute-start(bf16[1024,2048]{1,0:T(8,128)(2,1)} %copy-done.49), channel_id=1, source_target_pairs={{0,1},{1,0},{2,3},{3,2},{4,5},{5,4},{6,7},{7,6},{8,9},{9,8},{10,11... | collective-permute-start | bytes 12582920 | tf_op jit(solution)/shard_map/ppermute | solution.py:34
  288.2 15.6 %collective-permute-start.76 = (bf16[64,4096]{1,0:T(8,128)(2,1)S(1)}, bf16[64,4096]{1,0:T(8,128)(2,1)S(1)}, u32[]{:S(2)}, u32[]{:S(2)}) collective-permute-start(bf16[64,4096]{1,0:T(8,128)(2,1)S(1)} %get-tuple-element.351), channel_id=1, source_target_pairs={{0,24},{8,16},{16,8},{24,0},{1,25},{9,17},{17,9},{25,1},{2,26},{10... | collective-permute-start | bytes 1572872 | tf_op jit(solution)/shard_map/ppermute | solution.py:34
  289.8 15.3 %collective-permute-start.77 = (bf16[64,4096]{1,0:T(8,128)(2,1)S(1)}, bf16[64,4096]{1,0:T(8,128)(2,1)S(1)}, u32[]{:S(2)}, u32[]{:S(2)}) collective-permute-start(bf16[64,4096]{1,0:T(8,128)(2,1)S(1)} %get-tuple-element.352), channel_id=1, source_target_pairs={{0,6},{2,4},{4,2},{6,0},{1,7},{3,5},{5,3},{7,1},{8,14},{10,12},{12... | collective-permute-start | bytes 1572872 | tf_op jit(solution)/shard_map/ppermute | solution.py:34
  291.6 13.8 %collective-permute-start.78 = (bf16[64,4096]{1,0:T(8,128)(2,1)S(1)}, bf16[64,4096]{1,0:T(8,128)(2,1)S(1)}, u32[]{:S(2)}, u32[]{:S(2)}) collective-permute-start(bf16[64,4096]{1,0:T(8,128)(2,1)S(1)} %get-tuple-element.353), channel_id=1, source_target_pairs={{0,8},{8,0},{16,24},{24,16},{1,9},{9,1},{17,25},{25,17},{2,10},{10... | collective-permute-start | bytes 1572872 | tf_op jit(solution)/shard_map/ppermute | solution.py:34
  316.7 50.1 %collective-permute-start.107 = (bf16[512,2048]{1,0:T(8,128)(2,1)S(1)}, bf16[512,2048]{1,0:T(8,128)(2,1)S(1)}, u32[]{:S(2)}, u32[]{:S(2)}) collective-permute-start(bf16[512,2048]{1,0:T(8,128)(2,1)S(1)} %get-tuple-element.407), channel_id=1, source_target_pairs={{0,96},{32,64},{64,32},{96,0},{1,97},{33,65},{65,33},{97,1},{2,98}... | collective-permute-start | bytes 6291464 | tf_op jit(solution)/shard_map/ppermute | solution.py:34
  369.0 26.0 %collective-permute-start.108 = (bf16[256,2048]{1,0:T(8,128)(2,1)S(1)}, bf16[256,2048]{1,0:T(8,128)(2,1)S(1)}, u32[]{:S(2)}, u32[]{:S(2)}) collective-permute-start(bf16[256,2048]{1,0:T(8,128)(2,1)S(1)} %get-tuple-element.410), channel_id=1, source_target_pairs={{0,32},{32,0},{64,96},{96,64},{1,33},{33,1},{65,97},{97,65},{2,34}... | collective-permute-start | bytes 3145736 | tf_op jit(solution)/shard_map/ppermute | solution.py:34
  421.2 18.5 %collective-permute-start.135 = (bf16[512,640]{1,0:T(8,128)(2,1)S(1)}, bf16[512,640]{1,0:T(8,128)(2,1)S(1)}, u32[]{:S(2)}, u32[]{:S(2)}) collective-permute-start(bf16[512,640]{1,0:T(8,128)(2,1)S(1)} %get-tuple-element.456), channel_id=1, source_target_pairs={{0,96},{32,64},{64,32},{96,0},{1,97},{33,65},{65,33},{97,1},{2,98}... | collective-permute-start | bytes 1966088 | tf_op jit(solution)/shard_map/ppermute | solution.py:34
  458.0 19.0 %collective-permute-start.140 = (bf16[1,64,2688]{2,1,0:T(8,128)(2,1)S(1)}, bf16[1,64,2688]{2,1,0:T(8,128)(2,1)S(1)}, u32[]{:S(2)}, u32[]{:S(2)}) collective-permute-start(bf16[1,64,2688]{2,1,0:T(8,128)(2,1)S(1)} %get-tuple-element.464), channel_id=1, source_target_pairs={{0,16},{1,20},{4,17},{5,21},{8,24},{9,28},{12,25},{13,29},{16,0},{... | collective-permute-start | bytes 1032200 | tf_op jit(solution)/shard_map/ppermute | solution.py:51
  460.0 24.4 %collective-permute-start.133 = (bf16[64,2048]{1,0:T(8,128)(2,1)S(1)}, bf16[64,2048]{1,0:T(8,128)(2,1)S(1)}, u32[]{:S(2)}, u32[]{:S(2)}) collective-permute-start(bf16[64,2048]{1,0:T(8,128)(2,1)S(1)} %shard_map.324.refs_1_), channel_id=1, source_target_pairs={{0,3},{1,2},{2,1},{3,0},{4,7},{5,6},{6,5},{7,4},{8,11},{9,10},{10,... | collective-permute-start | bytes 786440 | tf_op jit(solution)/shard_map/ppermute | solution.py:34
  464.3 20.2 %collective-permute-start.132 = (bf16[64,2048]{1,0:T(8,128)(2,1)S(1)}, bf16[64,2048]{1,0:T(8,128)(2,1)S(1)}, u32[]{:S(2)}, u32[]{:S(2)}) collective-permute-start(bf16[64,2048]{1,0:T(8,128)(2,1)S(1)} %shard_map.324.refs_1_), channel_id=1, source_target_pairs={{0,1},{1,0},{2,3},{3,2},{4,5},{5,4},{6,7},{7,6},{8,9},{9,8},{10,11... | collective-permute-start | bytes 786440 | tf_op jit(solution)/shard_map/ppermute | solution.py:34
  466.8 17.6 %collective-permute-start.131 = (bf16[64,2048]{1,0:T(8,128)(2,1)S(1)}, bf16[64,2048]{1,0:T(8,128)(2,1)}, u32[]{:S(2)}, u32[]{:S(2)}) collective-permute-start(bf16[64,2048]{1,0:T(8,128)(2,1)S(1)} %shard_map.324.refs_1_), channel_id=1, source_target_pairs={{0,2},{2,0},{1,3},{3,1},{4,6},{6,4},{5,7},{7,5},{8,10},{10,8},{9,1... | collective-permute-start | bytes 786440 | tf_op jit(solution)/shard_map/ppermute | solution.py:34
  (180 other events, 2147.7 us)
